TPU v7x, 32 devices: a whole 2x2x4 slice. The times are simulated.
32 devices in a mesh: row: 8 (over z, x), col: 4 (over y, core).
Axes of the slice: x: 2, y: 2, z: 4, core: 2. Of those that a mesh axis runs over, the one named last changes fastest.
Arguments:
- embeddings: bfloat16 [8192, 4096], P(('row', 'col')), as said below
- cluster_sizes: int32 [8], replicated, may hold values from 2 to 2048, as said below
Outputs:
- highest: float32 [8192], P(('row', 'col'))
Inputs may be any that keep to these rules, and one draw needn't show every extreme that they name: `cluster_sizes`: 8 sizes summing to 8192; the largest is exactly 2048. `embeddings`: no row is zero.
All inputs are finite; a program needn't handle non-finite values.
Results may differ from a plain program's by a relative error of at most 0.00044.
Values may be sent and summed in bfloat16 or wider, within the bound.
No kernel may reach another device: no remote copies, remote signals or barrier semaphores. Data moves between devices by JAX's collectives and lax.ppermute only.
A program may use at most 128 MiB of HBM per device.

v0:
```python
import jax
import jax.numpy as jnp
from jax import lax
from jax.sharding import PartitionSpec as P

SPAN = 8


def passed_along(x, axis, by):
    length = lax.axis_size(axis)
    pairs = [(i, i + by) for i in range(length) if 0 <= i + by < length]
    return lax.ppermute(x, axis, pairs)


def cluster_of(leading, length, cluster_sizes):
    positions = leading + lax.iota(jnp.int32, length)
    bounds = jnp.cumsum(cluster_sizes)
    labels = jnp.sum((bounds[None, :] <= positions[:, None]).astype(jnp.int32), axis=1)
    return jnp.where(positions < 0, -1, labels)


def pair_block(own_rows, partner, own_labels, partner_labels):
    length = own_rows.shape[0]

    def work(unused):
        scores = lax.dot_general(
            own_rows, partner, (((1,), (1,)), ((), ())), preferred_element_type=jnp.float32
        )
        shared = own_labels[:, None] == partner_labels[None, :]
        masked = jnp.where(shared, scores, jnp.float32(-2.0))
        return (jnp.max(masked, axis=1), jnp.max(masked, axis=0))

    def nothing(unused):
        filler = jnp.full((length,), -2.0, jnp.float32)
        return (filler, filler)

    touches = (own_labels[-1] >= partner_labels[0]) & (partner_labels[-1] >= own_labels[0])
    return lax.cond(touches, work, nothing, 0)


def local(embeddings, cluster_sizes):
    length = embeddings.shape[0]
    position = lax.axis_index(("row", "col"))
    widened = embeddings.astype(jnp.float32)
    squares = jnp.sum(widened * widened, axis=1, keepdims=True) + 1e-06
    normed = (widened * lax.rsqrt(squares)).astype(jnp.bfloat16)
    own_labels = cluster_of(position * length, length, cluster_sizes)
    scores = lax.dot_general(
        normed, normed, (((1,), (1,)), ((), ())), preferred_element_type=jnp.float32
    )
    diagonal = lax.iota(jnp.int32, length)
    shared = (own_labels[:, None] == own_labels[None, :]) & (diagonal[:, None] != diagonal[None, :])
    highest = jnp.max(jnp.where(shared, scores, jnp.float32(-2.0)), axis=1)
    for distance in range(1, SPAN + 1):
        ahead = passed_along(normed, ("row", "col"), -distance)
        ahead_labels = cluster_of((position + distance) * length, length, cluster_sizes)
        found, unused_cols = pair_block(normed, ahead, own_labels, ahead_labels)
        highest = jnp.maximum(highest, found)
        behind = passed_along(normed, ("row", "col"), distance)
        behind_labels = cluster_of((position - distance) * length, length, cluster_sizes)
        found, unused_cols = pair_block(normed, behind, own_labels, behind_labels)
        highest = jnp.maximum(highest, found)
    return highest


def solution(mesh):
    in_specs = (P(("row", "col"), None), P())
    out_specs = P(("row", "col"))
    return jax.shard_map(local, mesh=mesh, in_specs=in_specs, out_specs=out_specs, check_vma=False)
```

profile of v0, /device:TPU:28, one launch (start us, length us, event | category | flops | bytes accessed | tf_op | source)
XLA Modules:
  0.0 482.0 jit_solution(9887677616889642859)
XLA Ops:
  0.0 2.2 fusion.16
  2.9 1.9 collective-permute-start
  4.8 2.4 collective-permute-start.1
  7.2 3.7 collective-permute-start.2
  10.9 3.1 collective-permute-start.3
  14.0 6.1 %collective-permute-start.4 = (bf16[256,4096]{1,0:T(8,128)(2,1)S(1)}, bf16[256,4096]{1,0:T(8,128)(2,1)}, u32[]{:S(2)}, u32[]{:S(2)}) collective-permute-start(bf16[256,4096]{1,0:T(8,128)(2,1)S(1)} %fusion.17), channel_id=1, source_target_pairs={{3,0},{4,1},{5,2},{6,3},{7,4},{8,5},{9,6},{10,7},{11,8},{12,9},{13... | collective-permute-start | bytes 6291464 | tf_op jit(solution)/shard_map/ppermute | solution.py:12
  20.4 92.3 %collective-permute-done = bf16[256,4096]{1,0:T(8,128)(2,1)} collective-permute-done((bf16[256,4096]{1,0:T(8,128)(2,1)S(1)}, bf16[256,4096]{1,0:T(8,128)(2,1)}, u32[]{:S(2)}, u32[]{:S(2)}) %collective-permute-start) | collective-permute-done | bytes 2097184 | tf_op jit(solution)/shard_map/ppermute | solution.py:12
  112.6 6.6 %collective-permute-start.5 = (bf16[256,4096]{1,0:T(8,128)(2,1)S(1)}, bf16[256,4096]{1,0:T(8,128)(2,1)S(1)}, u32[]{:S(2)}, u32[]{:S(2)}) collective-permute-start(bf16[256,4096]{1,0:T(8,128)(2,1)S(1)} %fusion.17), channel_id=1, source_target_pairs={{0,3},{1,4},{2,5},{3,6},{4,7},{5,8},{6,9},{7,10},{8,11},{9,12},{10... | collective-permute-start | bytes 6291464 | tf_op jit(solution)/shard_map/ppermute | solution.py:12
  119.4 0.6 fusion.20
  120.0 0.6 fusion.35
  123.3 0.6 fusion.21
  126.5 0.6 fusion.22
  129.7 13.8 %collective-permute-done.1 = bf16[256,4096]{1,0:T(8,128)(2,1)} collective-permute-done((bf16[256,4096]{1,0:T(8,128)(2,1)S(1)}, bf16[256,4096]{1,0:T(8,128)(2,1)}, u32[]{:S(2)}, u32[]{:S(2)}) %collective-permute-start.1) | collective-permute-done | bytes 2097184 | tf_op jit(solution)/shard_map/ppermute | solution.py:12
  143.5 4.2 collective-permute-start.6
  147.7 32.4 %collective-permute-done.2 = bf16[256,4096]{1,0:T(8,128)(2,1)} collective-permute-done((bf16[256,4096]{1,0:T(8,128)(2,1)S(1)}, bf16[256,4096]{1,0:T(8,128)(2,1)}, u32[]{:S(2)}, u32[]{:S(2)}) %collective-permute-start.2) | collective-permute-done | bytes 2097184 | tf_op jit(solution)/shard_map/ppermute | solution.py:12
  180.0 5.1 %collective-permute-start.7 = (bf16[256,4096]{1,0:T(8,128)(2,1)S(1)}, bf16[256,4096]{1,0:T(8,128)(2,1)S(1)}, u32[]{:S(2)}, u32[]{:S(2)}) collective-permute-start(bf16[256,4096]{1,0:T(8,128)(2,1)S(1)} %fusion.17), channel_id=1, source_target_pairs={{0,4},{1,5},{2,6},{3,7},{4,8},{5,9},{6,10},{7,11},{8,12},{9,13},{1... | collective-permute-start | bytes 6291464 | tf_op jit(solution)/shard_map/ppermute | solution.py:12
  185.2 6.0 %collective-permute-start.8 = (bf16[256,4096]{1,0:T(8,128)(2,1)S(1)}, bf16[256,4096]{1,0:T(8,128)(2,1)S(1)}, u32[]{:S(2)}, u32[]{:S(2)}) collective-permute-start(bf16[256,4096]{1,0:T(8,128)(2,1)S(1)} %fusion.17), channel_id=1, source_target_pairs={{5,0},{6,1},{7,2},{8,3},{9,4},{10,5},{11,6},{12,7},{13,8},{14,9},{... | collective-permute-start | bytes 6291464 | tf_op jit(solution)/shard_map/ppermute | solution.py:12
  191.2 1.9 collective-permute-start.9
  193.2 6.4 %collective-permute-start.10 = (bf16[256,4096]{1,0:T(8,128)(2,1)S(1)}, bf16[256,4096]{1,0:T(8,128)(2,1)S(1)}, u32[]{:S(2)}, u32[]{:S(2)}) collective-permute-start(bf16[256,4096]{1,0:T(8,128)(2,1)S(1)} %fusion.17), channel_id=1, source_target_pairs={{6,0},{7,1},{8,2},{9,3},{10,4},{11,5},{12,6},{13,7},{14,8},{15,9},... | collective-permute-start | bytes 6291464 | tf_op jit(solution)/shard_map/ppermute | solution.py:12
  199.6 0.6 fusion.23
  202.8 0.6 fusion.24
  212.5 0.6 fusion.27
  215.7 0.6 fusion.28
  219.0 0.6 fusion.29
  222.2 53.6 %collective-permute-done.6 = bf16[256,4096]{1,0:T(8,128)(2,1)S(1)} collective-permute-done((bf16[256,4096]{1,0:T(8,128)(2,1)S(1)}, bf16[256,4096]{1,0:T(8,128)(2,1)S(1)}, u32[]{:S(2)}, u32[]{:S(2)}) %collective-permute-start.6) | collective-permute-done | bytes 2097184 | tf_op jit(solution)/shard_map/ppermute | solution.py:12
  275.8 1.3 collective-permute-start.11
  277.1 91.3 %collective-permute-start.12 = (bf16[256,4096]{1,0:T(8,128)(2,1)S(1)}, bf16[256,4096]{1,0:T(8,128)(2,1)}, u32[]{:S(2)}, u32[]{:S(2)}) collective-permute-start(bf16[256,4096]{1,0:T(8,128)(2,1)S(1)} %fusion.17), channel_id=1, source_target_pairs={{7,0},{8,1},{9,2},{10,3},{11,4},{12,5},{13,6},{14,7},{15,8},{16,9}... | collective-permute-start | bytes 6291464 | tf_op jit(solution)/shard_map/ppermute | solution.py:12
  368.4 1.3 collective-permute-start.13
  369.7 25.4 %collective-permute-start.14 = (bf16[256,4096]{1,0:T(8,128)(2,1)S(1)}, bf16[256,4096]{1,0:T(8,128)(2,1)}, u32[]{:S(2)}, u32[]{:S(2)}) collective-permute-start(bf16[256,4096]{1,0:T(8,128)(2,1)S(1)} %fusion.17), channel_id=1, source_target_pairs={{8,0},{9,1},{10,2},{11,3},{12,4},{13,5},{14,6},{15,7},{16,8},{17,9... | collective-permute-start | bytes 6291464 | tf_op jit(solution)/shard_map/ppermute | solution.py:12
  395.1 1.3 collective-permute-start.15
  402.7 0.6 fusion.32
  412.1 0.7 fusion.36
  415.5 0.8 fusion.18
  416.3 2.4 conditional.16
  416.3 2.3 fusion
  418.6 2.4 conditional.17
  418.7 2.3 fusion.1
  421.0 2.4 conditional.18
  421.0 2.3 fusion.2
  423.4 2.4 conditional.20
  423.4 2.3 fusion.4
  425.8 2.4 conditional.22
  425.8 2.3 fusion.6
  428.2 2.4 conditional.24
  428.2 2.3 fusion.8
  430.9 1.9 collective-permute-done.13
  432.8 2.8 collective-permute-done.14
  435.6 45.8 %collective-permute-done.15 = bf16[256,4096]{1,0:T(8,128)(2,1)} collective-permute-done((bf16[256,4096]{1,0:T(8,128)(2,1)S(1)}, bf16[256,4096]{1,0:T(8,128)(2,1)}, u32[]{:S(2)}, u32[]{:S(2)}) %collective-permute-start.15) | collective-permute-done | bytes 2097184 | tf_op jit(solution)/shard_map/ppermute | solution.py:12
  (82 shorter events, 5.7 us)
Async XLA Ops:
  0.0 2.2 copy-start
  2.3 17.8 %copy-start.7 = (s32[8]{0:T(128)S(1)}, s32[8]{0:T(128)}, u32[]{:S(2)}) copy-start(s32[8]{0:T(128)} %param.35) | copy-start | bytes 100
  2.9 109.8 %collective-permute-start = (bf16[256,4096]{1,0:T(8,128)(2,1)S(1)}, bf16[256,4096]{1,0:T(8,128)(2,1)}, u32[]{:S(2)}, u32[]{:S(2)}) collective-permute-start(bf16[256,4096]{1,0:T(8,128)(2,1)S(1)} %fusion.17), channel_id=1, source_target_pairs={{1,0},{2,1},{3,2},{4,3},{5,4},{6,5},{7,6},{8,7},{9,8},{10,9},{11,1... | collective-permute-start | bytes 6291464 | tf_op jit(solution)/shard_map/ppermute | solution.py:12
  4.8 138.7 %collective-permute-start.1 = (bf16[256,4096]{1,0:T(8,128)(2,1)S(1)}, bf16[256,4096]{1,0:T(8,128)(2,1)}, u32[]{:S(2)}, u32[]{:S(2)}) collective-permute-start(bf16[256,4096]{1,0:T(8,128)(2,1)S(1)} %fusion.17), channel_id=1, source_target_pairs={{0,1},{1,2},{2,3},{3,4},{4,5},{5,6},{6,7},{7,8},{8,9},{9,10},{10,1... | collective-permute-start | bytes 6291464 | tf_op jit(solution)/shard_map/ppermute | solution.py:12
  7.2 172.8 %collective-permute-start.2 = (bf16[256,4096]{1,0:T(8,128)(2,1)S(1)}, bf16[256,4096]{1,0:T(8,128)(2,1)}, u32[]{:S(2)}, u32[]{:S(2)}) collective-permute-start(bf16[256,4096]{1,0:T(8,128)(2,1)S(1)} %fusion.17), channel_id=1, source_target_pairs={{2,0},{3,1},{4,2},{5,3},{6,4},{7,5},{8,6},{9,7},{10,8},{11,9},{12,... | collective-permute-start | bytes 6291464 | tf_op jit(solution)/shard_map/ppermute | solution.py:12
  10.9 174.3 %collective-permute-start.3 = (bf16[256,4096]{1,0:T(8,128)(2,1)S(1)}, bf16[256,4096]{1,0:T(8,128)(2,1)}, u32[]{:S(2)}, u32[]{:S(2)}) collective-permute-start(bf16[256,4096]{1,0:T(8,128)(2,1)S(1)} %fusion.17), channel_id=1, source_target_pairs={{0,2},{1,3},{2,4},{3,5},{4,6},{5,7},{6,8},{7,9},{8,10},{9,11},{10,... | collective-permute-start | bytes 6291464 | tf_op jit(solution)/shard_map/ppermute | solution.py:12
  14.0 177.2 %collective-permute-start.4 = (bf16[256,4096]{1,0:T(8,128)(2,1)S(1)}, bf16[256,4096]{1,0:T(8,128)(2,1)}, u32[]{:S(2)}, u32[]{:S(2)}) collective-permute-start(bf16[256,4096]{1,0:T(8,128)(2,1)S(1)} %fusion.17), channel_id=1, source_target_pairs={{3,0},{4,1},{5,2},{6,3},{7,4},{8,5},{9,6},{10,7},{11,8},{12,9},{13... | collective-permute-start | bytes 6291464 | tf_op jit(solution)/shard_map/ppermute | solution.py:12
  112.6 80.5 %collective-permute-start.5 = (bf16[256,4096]{1,0:T(8,128)(2,1)S(1)}, bf16[256,4096]{1,0:T(8,128)(2,1)S(1)}, u32[]{:S(2)}, u32[]{:S(2)}) collective-permute-start(bf16[256,4096]{1,0:T(8,128)(2,1)S(1)} %fusion.17), channel_id=1, source_target_pairs={{0,3},{1,4},{2,5},{3,6},{4,7},{5,8},{6,9},{7,10},{8,11},{9,12},{10... | collective-permute-start | bytes 6291464 | tf_op jit(solution)/shard_map/ppermute | solution.py:12
  143.5 132.3 %collective-permute-start.6 = (bf16[256,4096]{1,0:T(8,128)(2,1)S(1)}, bf16[256,4096]{1,0:T(8,128)(2,1)S(1)}, u32[]{:S(2)}, u32[]{:S(2)}) collective-permute-start(bf16[256,4096]{1,0:T(8,128)(2,1)S(1)} %fusion.17), channel_id=1, source_target_pairs={{4,0},{5,1},{6,2},{7,3},{8,4},{9,5},{10,6},{11,7},{12,8},{13,9},{1... | collective-permute-start | bytes 6291464 | tf_op jit(solution)/shard_map/ppermute | solution.py:12
  180.0 97.0 %collective-permute-start.7 = (bf16[256,4096]{1,0:T(8,128)(2,1)S(1)}, bf16[256,4096]{1,0:T(8,128)(2,1)S(1)}, u32[]{:S(2)}, u32[]{:S(2)}) collective-permute-start(bf16[256,4096]{1,0:T(8,128)(2,1)S(1)} %fusion.17), channel_id=1, source_target_pairs={{0,4},{1,5},{2,6},{3,7},{4,8},{5,9},{6,10},{7,11},{8,12},{9,13},{1... | collective-permute-start | bytes 6291464 | tf_op jit(solution)/shard_map/ppermute | solution.py:12
  185.2 183.2 %collective-permute-start.8 = (bf16[256,4096]{1,0:T(8,128)(2,1)S(1)}, bf16[256,4096]{1,0:T(8,128)(2,1)S(1)}, u32[]{:S(2)}, u32[]{:S(2)}) collective-permute-start(bf16[256,4096]{1,0:T(8,128)(2,1)S(1)} %fusion.17), channel_id=1, source_target_pairs={{5,0},{6,1},{7,2},{8,3},{9,4},{10,5},{11,6},{12,7},{13,8},{14,9},{... | collective-permute-start | bytes 6291464 | tf_op jit(solution)/shard_map/ppermute | solution.py:12
  191.2 178.5 %collective-permute-start.9 = (bf16[256,4096]{1,0:T(8,128)(2,1)S(1)}, bf16[256,4096]{1,0:T(8,128)(2,1)S(1)}, u32[]{:S(2)}, u32[]{:S(2)}) collective-permute-start(bf16[256,4096]{1,0:T(8,128)(2,1)S(1)} %fusion.17), channel_id=1, source_target_pairs={{0,5},{1,6},{2,7},{3,8},{4,9},{5,10},{6,11},{7,12},{8,13},{9,14},{... | collective-permute-start | bytes 6291464 | tf_op jit(solution)/shard_map/ppermute | solution.py:12
  193.2 222.3 %copy-start.1 = (bf16[256,4096]{1,0:T(8,128)(2,1)}, bf16[256,4096]{1,0:T(8,128)(2,1)S(1)}, u32[]{:S(2)}) copy-start(bf16[256,4096]{1,0:T(8,128)(2,1)S(1)} %collective-permute-done.5) | copy-start | bytes 6291460
  193.2 201.9 %collective-permute-start.10 = (bf16[256,4096]{1,0:T(8,128)(2,1)S(1)}, bf16[256,4096]{1,0:T(8,128)(2,1)S(1)}, u32[]{:S(2)}, u32[]{:S(2)}) collective-permute-start(bf16[256,4096]{1,0:T(8,128)(2,1)S(1)} %fusion.17), channel_id=1, source_target_pairs={{6,0},{7,1},{8,2},{9,3},{10,4},{11,5},{12,6},{13,7},{14,8},{15,9},... | collective-permute-start | bytes 6291464 | tf_op jit(solution)/shard_map/ppermute | solution.py:12
  275.8 140.4 %copy-start.6 = (bf16[256,4096]{1,0:T(8,128)(2,1)}, bf16[256,4096]{1,0:T(8,128)(2,1)S(1)}, u32[]{:S(2)}) copy-start(bf16[256,4096]{1,0:T(8,128)(2,1)S(1)} %collective-permute-done.6) | copy-start | bytes 6291460
  275.8 155.0 %collective-permute-start.11 = (bf16[256,4096]{1,0:T(8,128)(2,1)S(1)}, bf16[256,4096]{1,0:T(8,128)(2,1)}, u32[]{:S(2)}, u32[]{:S(2)}) collective-permute-start(bf16[256,4096]{1,0:T(8,128)(2,1)S(1)} %fusion.17), channel_id=1, source_target_pairs={{0,6},{1,7},{2,8},{3,9},{4,10},{5,11},{6,12},{7,13},{8,14},{9,15},... | collective-permute-start | bytes 6291464 | tf_op jit(solution)/shard_map/ppermute | solution.py:12
  277.1 139.2 %copy-start.5 = (bf16[256,4096]{1,0:T(8,128)(2,1)}, bf16[256,4096]{1,0:T(8,128)(2,1)S(1)}, u32[]{:S(2)}) copy-start(bf16[256,4096]{1,0:T(8,128)(2,1)S(1)} %collective-permute-done.7) | copy-start | bytes 6291460
  277.1 153.8 %collective-permute-start.12 = (bf16[256,4096]{1,0:T(8,128)(2,1)S(1)}, bf16[256,4096]{1,0:T(8,128)(2,1)}, u32[]{:S(2)}, u32[]{:S(2)}) collective-permute-start(bf16[256,4096]{1,0:T(8,128)(2,1)S(1)} %fusion.17), channel_id=1, source_target_pairs={{7,0},{8,1},{9,2},{10,3},{11,4},{12,5},{13,6},{14,7},{15,8},{16,9}... | collective-permute-start | bytes 6291464 | tf_op jit(solution)/shard_map/ppermute | solution.py:12
  368.4 47.9 %copy-start.4 = (bf16[256,4096]{1,0:T(8,128)(2,1)}, bf16[256,4096]{1,0:T(8,128)(2,1)S(1)}, u32[]{:S(2)}) copy-start(bf16[256,4096]{1,0:T(8,128)(2,1)S(1)} %collective-permute-done.8) | copy-start | bytes 6291460
  368.4 64.4 %collective-permute-start.13 = (bf16[256,4096]{1,0:T(8,128)(2,1)S(1)}, bf16[256,4096]{1,0:T(8,128)(2,1)}, u32[]{:S(2)}, u32[]{:S(2)}) collective-permute-start(bf16[256,4096]{1,0:T(8,128)(2,1)S(1)} %fusion.17), channel_id=1, source_target_pairs={{0,7},{1,8},{2,9},{3,10},{4,11},{5,12},{6,13},{7,14},{8,15},{9,16}... | collective-permute-start | bytes 6291464 | tf_op jit(solution)/shard_map/ppermute | solution.py:12
  369.7 45.8 %copy-start.3 = (bf16[256,4096]{1,0:T(8,128)(2,1)}, bf16[256,4096]{1,0:T(8,128)(2,1)S(1)}, u32[]{:S(2)}) copy-start(bf16[256,4096]{1,0:T(8,128)(2,1)S(1)} %collective-permute-done.9) | copy-start | bytes 6291460
  369.7 65.9 %collective-permute-start.14 = (bf16[256,4096]{1,0:T(8,128)(2,1)S(1)}, bf16[256,4096]{1,0:T(8,128)(2,1)}, u32[]{:S(2)}, u32[]{:S(2)}) collective-permute-start(bf16[256,4096]{1,0:T(8,128)(2,1)S(1)} %fusion.17), channel_id=1, source_target_pairs={{8,0},{9,1},{10,2},{11,3},{12,4},{13,5},{14,6},{15,7},{16,8},{17,9... | collective-permute-start | bytes 6291464 | tf_op jit(solution)/shard_map/ppermute | solution.py:12
  395.1 20.4 %copy-start.2 = (bf16[256,4096]{1,0:T(8,128)(2,1)}, bf16[256,4096]{1,0:T(8,128)(2,1)S(1)}, u32[]{:S(2)}) copy-start(bf16[256,4096]{1,0:T(8,128)(2,1)S(1)} %collective-permute-done.10) | copy-start | bytes 6291460
  395.1 86.3 %collective-permute-start.15 = (bf16[256,4096]{1,0:T(8,128)(2,1)S(1)}, bf16[256,4096]{1,0:T(8,128)(2,1)}, u32[]{:S(2)}, u32[]{:S(2)}) collective-permute-start(bf16[256,4096]{1,0:T(8,128)(2,1)S(1)} %fusion.17), channel_id=1, source_target_pairs={{0,8},{1,9},{2,10},{3,11},{4,12},{5,13},{6,14},{7,15},{8,16},{9,17... | collective-permute-start | bytes 6291464 | tf_op jit(solution)/shard_map/ppermute | solution.py:12
where the time goes:
time: 483 us; the launch traced here: 482 us
  waiting for transfers between devices  243 us (50%)
  starting transfers between devices  168 us (35%)
  between operations  41.8 us (9%)
  matrix products  14.8 us (3%)
  local copies, waits for them, and re-layouts  10.6 us (2%)
    ppermute x16, waiting for transfers between devices, passed_along(): return lax.ppermute(x, axis, pairs)  243 us
    ppermute x16, starting transfers between devices, passed_along(): return lax.ppermute(x, axis, pairs)  168 us
    dot_general x6, matrix products, work(): lax.dot_general(own_rows, partner, (((1,), (1,)), ((), ())), preferred_el...  14.1 us
    slice x16, local copies, waits for them, and re-layouts, pair_block(): partner_labels[-1] >= own_labels[0]  9.88 us
  transfers between devices with their start and end apart: 16, of which 7 were waited for; matrix products, arithmetic and copies ran while one was open for 5% of the time, Pallas kernels for 0%

commit v1 on v0

v1 whole, which is shorter than its diff:
```python
import functools

import jax
import jax.numpy as jnp
from jax import lax
from jax.experimental import pallas as pl
from jax.experimental.pallas import tpu as pltpu
from jax.sharding import PartitionSpec as P

AXES = ("row", "col")
QUAD = 4
STRIP = 16
FILLER = -2.0
NT = (((1,), (1,)), ((), ()))


def swapped(x, devices, bit):
    return lax.ppermute(x, AXES, [(i, i ^ bit) for i in range(devices)])


def shifted(x, devices, by):
    return lax.ppermute(x, AXES, [(i, i + by) for i in range(devices) if 0 <= i + by < devices])


def labels_of(bounds_ref, block, length, axis):
    shape = (length, 1) if axis == 0 else (1, length)
    positions = block * length + lax.broadcasted_iota(jnp.int32, shape, axis)
    labels = jnp.where(positions < 0, -1, 0)
    for c in range(bounds_ref.shape[0]):
        labels = labels + (bounds_ref[c] <= positions).astype(jnp.int32)
    return labels


def normalize(ref):
    def strip(i, unused):
        rows = pl.ds(pl.multiple_of(i * STRIP, STRIP), STRIP)
        widened = ref[rows, :].astype(jnp.float32)
        squares = jnp.sum(widened * widened, axis=1, keepdims=True) + 1e-06
        ref[rows, :] = (widened * lax.rsqrt(squares)).astype(jnp.bfloat16)
        return unused

    lax.fori_loop(0, ref.shape[0] // STRIP, strip, 0)


def masked_scores(left, right, left_labels, right_labels):
    scores = lax.dot_general(left[...], right[...], NT, preferred_element_type=jnp.float32)
    return jnp.where(left_labels == right_labels, scores, FILLER)


def over_lanes(masked):
    folded = masked[:, :128]
    for i in range(128, masked.shape[1], 128):
        folded = jnp.maximum(folded, masked[:, i:i + 128])
    return jnp.max(folded.T, axis=0, keepdims=True)


def chip_kernel(bounds_ref, place_ref, own_hbm, near_hbm, own_out, near_out, best_out, own, near, sems):
    length = own.shape[0]
    copies = [pltpu.make_async_copy(own_hbm, own, sems.at[0]), pltpu.make_async_copy(near_hbm, near, sems.at[1])]
    for copy in copies:
        copy.start()
    place = place_ref[0]
    own_labels = labels_of(bounds_ref, place, length, 1)
    copies[0].wait()
    normalize(own)
    back = [pltpu.make_async_copy(own, own_out, sems.at[2]), pltpu.make_async_copy(near, near_out, sems.at[3])]
    back[0].start()
    scores = masked_scores(own, own, labels_of(bounds_ref, place, length, 0), own_labels)
    same = lax.broadcasted_iota(jnp.int32, scores.shape, 0) == lax.broadcasted_iota(jnp.int32, scores.shape, 1)
    best = jnp.max(jnp.where(same, FILLER, scores), axis=0, keepdims=True)
    copies[1].wait()
    normalize(near)
    back[1].start()
    scores = masked_scores(near, own, labels_of(bounds_ref, place ^ 1, length, 0), own_labels)
    best_out[...] = jnp.maximum(best, jnp.max(scores, axis=0, keepdims=True))
    back[0].wait()
    back[1].wait()


def quad_kernel(bounds_ref, place_ref, *refs):
    sources, (best_in, best_out, quad_out, below_out, above_out), held, sems = refs[:6], refs[6:11], refs[11:17], refs[17]
    length = held[0].shape[0]
    copies = [pltpu.make_async_copy(sources[i], held[i], sems.at[i]) for i in range(6)]
    for i in (0, 1, 4, 5, 2, 3):
        copies[i].start()
    place = place_ref[0]
    quad_labels = [labels_of(bounds_ref, place ^ b, length, 1) for b in range(QUAD)]
    outside = (place - QUAD, place + 2 * QUAD)
    outside_labels = [labels_of(bounds_ref, block, length, 0) for block in outside]
    widest = [None, None]
    best = [None] * QUAD
    for b in range(QUAD):
        copies[b].wait()
        if b >= 2:
            normalize(held[b])
        for side in range(2):
            if b == 0:
                copies[4 + side].wait()
                normalize(held[4 + side])
            scores = masked_scores(held[4 + side], held[b], outside_labels[side], quad_labels[b])
            widest[side] = scores if b == 0 else jnp.maximum(widest[side], scores)
            found = jnp.max(scores, axis=0, keepdims=True)
            best[b] = found if side == 0 else jnp.maximum(best[b], found)
    for b in range(QUAD):
        quad_out[b:b + 1, :] = best[b]
    below_out[...] = over_lanes(widest[0])
    above_out[...] = over_lanes(widest[1])
    highest = best_in[...]
    for b in range(2, QUAD):
        scores = masked_scores(held[b], held[0], labels_of(bounds_ref, place ^ b, length, 0), quad_labels[0])
        highest = jnp.maximum(highest, jnp.max(scores, axis=0, keepdims=True))
    best_out[...] = highest


ANY = pl.BlockSpec(memory_space=pl.ANY)
VMEM = pl.BlockSpec(memory_space=pltpu.VMEM)
SMEM = pl.BlockSpec(memory_space=pltpu.SMEM)


def cost(products, blocks, length, width):
    return pl.CostEstimate(flops=2 * products * length * length * width, bytes_accessed=2 * blocks * length * width, transcendentals=0)


def local(devices, embeddings, cluster_sizes):
    length, width = embeddings.shape
    block = jax.ShapeDtypeStruct((length, width), jnp.bfloat16)
    line = jax.ShapeDtypeStruct((1, length), jnp.float32)
    place = lax.axis_index(AXES).astype(jnp.int32)
    bounds = jnp.cumsum(cluster_sizes).astype(jnp.int32)
    where = place.reshape(1)

    across = swapped(embeddings, devices, 2)
    below = shifted(embeddings, devices, QUAD)
    above = shifted(embeddings, devices, -2 * QUAD)
    near = swapped(embeddings, devices, 1)

    own_normed, near_normed, chip_best = pl.pallas_call(
        chip_kernel,
        out_shape=(block, block, line),
        in_specs=[SMEM, SMEM, ANY, ANY],
        out_specs=(ANY, ANY, VMEM),
        scratch_shapes=[pltpu.VMEM((length, width), jnp.bfloat16)] * 2 + [pltpu.SemaphoreType.DMA((4,))],
        compiler_params=pltpu.CompilerParams(vmem_limit_bytes=16 << 20),
        cost_estimate=cost(2, 4, length, width),
    )(bounds, where, embeddings, near)

    across_near = swapped(across, devices, 1)

    best, quad, to_below, to_above = pl.pallas_call(
        quad_kernel,
        out_shape=(line, jax.ShapeDtypeStruct((QUAD, length), jnp.float32), line, line),
        in_specs=[SMEM, SMEM] + [ANY] * 6 + [VMEM],
        out_specs=(VMEM,) * 4,
        scratch_shapes=[pltpu.VMEM((length, width), jnp.bfloat16)] * 6 + [pltpu.SemaphoreType.DMA((6,))],
        compiler_params=pltpu.CompilerParams(vmem_limit_bytes=24 << 20),
        cost_estimate=cost(10, 6, length, width),
    )(bounds, where, own_normed, near_normed, across, across_near, below, above, chip_best)

    filler = jnp.float32(FILLER)
    from_next = shifted(to_below, devices, -QUAD)
    from_previous = shifted(to_above, devices, 2 * QUAD)
    swapped_chip = swapped(quad[1::2], devices, 1)
    own_chip = jnp.maximum(quad[0::2], swapped_chip)
    swapped_quad = swapped(own_chip[1:2], devices, 2)
    best = jnp.maximum(jnp.maximum(best, own_chip[0:1]), swapped_quad)
    best = jnp.maximum(best, jnp.where(place + QUAD < devices, from_next, filler))
    best = jnp.maximum(best, jnp.where(place >= 2 * QUAD, from_previous, filler))
    return best.reshape(length)


def solution(mesh):
    devices = 1
    for axis in AXES:
        devices *= mesh.shape[axis]
    in_specs = (P(AXES, None), P())
    return jax.shard_map(functools.partial(local, devices), mesh=mesh, in_specs=in_specs, out_specs=P(AXES), check_vma=False)
```

time: 483 us -> 90.5 us (0.19)
  the two profiles are of different devices: /device:TPU:28 before, /device:TPU:0 now
where the time goes in v1:
time: 90.5 us; the launch traced here: 90.3 us
  waiting for transfers between devices  42 us (46%)
  Pallas kernels  27 us (30%)
  starting transfers between devices  18.1 us (20%)
  local copies, waits for them, and re-layouts  1.65 us (2%)
  other arithmetic  1.4 us (2%)
    ppermute x5, waiting for transfers between devices, swapped(): return lax.ppermute(x, AXES, [(i, i ^ bit) for i in range(devices)])  42 us
    pallas_call x1, Pallas kernels, local(): pl.pallas_call(quad_kernel, out_shape=(line, jax.ShapeDtypeStruct((QUAD,...  18.9 us
    ppermute x4, starting transfers between devices, shifted(): lax.ppermute(x, AXES, [(i, i + by) for i in range(devices) if 0 <= i + by...  13 us
    pallas_call x1, Pallas kernels, local(): pl.pallas_call(chip_kernel, out_shape=(block, block, line), in_specs=[SME...  8.13 us
    ppermute x5, starting transfers between devices, swapped(): return lax.ppermute(x, AXES, [(i, i ^ bit) for i in range(devices)])  5.11 us
  transfers between devices with their start and end apart: 9, of which 2 were waited for; matrix products, arithmetic and copies ran while one was open for 1% of the time, Pallas kernels for 9%

profile of v1, /device:TPU:0, one launch (start us, length us, event | category | flops | bytes accessed | tf_op | source)
XLA Modules:
  0.0 90.3 jit_solution(414833567235010900)
XLA Ops:
  0.0 3.0 %collective-permute-start.1 = (bf16[256,4096]{1,0:T(8,128)(2,1)}, bf16[256,4096]{1,0:T(8,128)(2,1)}, u32[]{:S(2)}, u32[]{:S(2)}) collective-permute-start(bf16[256,4096]{1,0:T(8,128)(2,1)} %own_hbm.1), channel_id=1, source_target_pairs={{0,2},{1,3},{2,0},{3,1},{4,6},{5,7},{6,4},{7,5},{8,10},{9,11},{10,... | collective-permute-start | bytes 6291464 | tf_op jit(solution)/shard_map/ppermute | solution.py:18
  3.0 0.0 collective-permute-start
  3.0 4.7 %collective-permute-start.3 = (bf16[256,4096]{1,0:T(8,128)(2,1)}, bf16[256,4096]{1,0:T(8,128)(2,1)}, u32[]{:S(2)}, u32[]{:S(2)}) collective-permute-start(bf16[256,4096]{1,0:T(8,128)(2,1)} %own_hbm.1), channel_id=1, source_target_pairs={{0,4},{1,5},{2,6},{3,7},{4,8},{5,9},{6,10},{7,11},{8,12},{9,13},{1... | collective-permute-start | bytes 6291464 | tf_op jit(solution)/shard_map/ppermute | solution.py:22
  7.7 1.3 %collective-permute-start.4 = (bf16[256,4096]{1,0:T(8,128)(2,1)}, bf16[256,4096]{1,0:T(8,128)(2,1)}, u32[]{:S(2)}, u32[]{:S(2)}) collective-permute-start(bf16[256,4096]{1,0:T(8,128)(2,1)} %own_hbm.1), channel_id=1, source_target_pairs={{8,0},{9,1},{10,2},{11,3},{12,4},{13,5},{14,6},{15,7},{16,8},{17,9... | collective-permute-start | bytes 6291464 | tf_op jit(solution)/shard_map/ppermute | solution.py:22
  9.0 39.9 %collective-permute-done.1.refs_2_ = bf16[256,4096]{1,0:T(8,128)(2,1)} collective-permute-done((bf16[256,4096]{1,0:T(8,128)(2,1)}, bf16[256,4096]{1,0:T(8,128)(2,1)}, u32[]{:S(2)}, u32[]{:S(2)}) %collective-permute-start.1) | collective-permute-done | bytes 2097184 | tf_op jit(solution)/shard_map/ppermute | solution.py:18
  48.9 0.0 collective-permute-start.2
  48.9 0.8 reduce-window.9
  49.7 0.0 collective-permute-done.near_hbm
  49.7 0.0 copy-start
  49.7 1.6 %copy-done = bf16[256,4096]{1,0:T(8,128)(2,1)S(1)} copy-done((bf16[256,4096]{1,0:T(8,128)(2,1)S(1)}, bf16[256,4096]{1,0:T(8,128)(2,1)}, u32[]{:S(2)}) %copy-start) | copy-done | bytes 2097176
  51.3 8.1 %shard_map.28 = (bf16[256,4096]{1,0:T(8,128)(2,1)S(1)}, bf16[256,4096]{1,0:T(8,128)(2,1)S(1)}, f32[1,256]{1,0:T(1,128)S(1)}) custom-call(s32[8]{0:T(128)S(1)} %bitcast.4, s32[1]{0:T(128)} %bitcast.2.place_ref, bf16[256,4096]{1,0:T(8,128)(2,1)S(1)} %copy-done, bf16[256,4096]{1,0:T(8,128)(2,1)S(1)} %collective-permute-done.near_hbm), custom_call_target="tpu_custom_call" | custom-call | flops 1073741824 | bytes 8388608 | tf_op jit(solution)/shard_map/pallas_call | solution.py:137
  59.5 0.0 collective-permute-done.3.refs_4_
  59.5 0.0 collective-permute-done.4.refs_5_
  59.5 0.0 collective-permute-done.2.refs_3_
  59.5 18.9 %shard_map.29 = (f32[1,256]{1,0:T(1,128)S(1)}, f32[4,256]{1,0:T(4,128)S(1)}, f32[1,256]{1,0:T(1,128)S(1)}, f32[1,256]{1,0:T(1,128)S(1)}) custom-call(s32[8]{0:T(128)S(1)} %bitcast.5, s32[1]{0:T(128)} %bitcast.2.place_ref, bf16[256,4096]{1,0:T(8,128)(2,1)S(1)} %get-tuple-element.12.refs_0_, bf16[256,4096]{1,0:T(8,128)(2,1)S(1)} %get-tuple-element.13.refs_1_, ...), custom_call_target="tpu_custom_call" | custom-call | flops 5368709120 | bytes 12582912 | tf_op jit(solution)/shard_map/pallas_call | solution.py:149
  78.5 0.5 collective-permute-start.5
  79.0 1.3 %collective-permute-start.7 = (f32[1,256]{1,0:T(1,128)S(1)}, f32[1,256]{1,0:T(1,128)S(1)}, u32[]{:S(2)}, u32[]{:S(2)}) collective-permute-start(f32[1,256]{1,0:T(1,128)S(1)} %get-tuple-element.17), channel_id=1, source_target_pairs={{4,0},{5,1},{6,2},{7,3},{8,4},{9,5},{10,6},{11,7},{12,8},{13,9},{1... | collective-permute-start | bytes 3080 | tf_op jit(solution)/shard_map/ppermute | solution.py:22
  80.3 5.7 %collective-permute-start.8 = (f32[1,256]{1,0:T(1,128)S(1)}, f32[1,256]{1,0:T(1,128)S(1)}, u32[]{:S(2)}, u32[]{:S(2)}) collective-permute-start(f32[1,256]{1,0:T(1,128)S(1)} %get-tuple-element.18), channel_id=1, source_target_pairs={{0,8},{1,9},{2,10},{3,11},{4,12},{5,13},{6,14},{7,15},{8,16},{9,17... | collective-permute-start | bytes 3080 | tf_op jit(solution)/shard_map/ppermute | solution.py:22
  86.0 0.0 collective-permute-done.5
  86.0 1.6 %collective-permute-start.6 = (f32[1,256]{1,0:T(1,128)S(1)}, f32[1,256]{1,0:T(1,128)S(1)}, u32[]{:S(2)}, u32[]{:S(2)}) collective-permute-start(f32[1,256]{1,0:T(1,128)S(1)} %slice.17), channel_id=1, source_target_pairs={{0,2},{1,3},{2,0},{3,1},{4,6},{5,7},{6,4},{7,5},{8,10},{9,11},{10,... | collective-permute-start | bytes 3080 | tf_op jit(solution)/shard_map/ppermute | solution.py:18
  87.6 0.0 collective-permute-done.7
  87.6 0.0 collective-permute-done.8
  87.6 2.0 %collective-permute-done.6 = f32[1,256]{1,0:T(1,128)S(1)} collective-permute-done((f32[1,256]{1,0:T(1,128)S(1)}, f32[1,256]{1,0:T(1,128)S(1)}, u32[]{:S(2)}, u32[]{:S(2)}) %collective-permute-start.6) | collective-permute-done | bytes 1056 | tf_op jit(solution)/shard_map/ppermute | solution.py:18
  89.7 0.6 fusion.1
  (4 shorter events, 0.1 us)
Async XLA Ops:
  0.0 48.9 %collective-permute-start.1 = (bf16[256,4096]{1,0:T(8,128)(2,1)}, bf16[256,4096]{1,0:T(8,128)(2,1)}, u32[]{:S(2)}, u32[]{:S(2)}) collective-permute-start(bf16[256,4096]{1,0:T(8,128)(2,1)} %own_hbm.1), channel_id=1, source_target_pairs={{0,2},{1,3},{2,0},{3,1},{4,6},{5,7},{6,4},{7,5},{8,10},{9,11},{10,... | collective-permute-start | bytes 6291464 | tf_op jit(solution)/shard_map/ppermute | solution.py:18
  3.0 46.8 %collective-permute-start = (bf16[256,4096]{1,0:T(8,128)(2,1)}, bf16[256,4096]{1,0:T(8,128)(2,1)S(1)}, u32[]{:S(2)}, u32[]{:S(2)}) collective-permute-start(bf16[256,4096]{1,0:T(8,128)(2,1)} %own_hbm.1), channel_id=1, source_target_pairs={{0,1},{1,0},{2,3},{3,2},{4,5},{5,4},{6,7},{7,6},{8,9},{9,8},{10,11... | collective-permute-start | bytes 6291464 | tf_op jit(solution)/shard_map/ppermute | solution.py:18
  3.0 56.5 %collective-permute-start.3 = (bf16[256,4096]{1,0:T(8,128)(2,1)}, bf16[256,4096]{1,0:T(8,128)(2,1)}, u32[]{:S(2)}, u32[]{:S(2)}) collective-permute-start(bf16[256,4096]{1,0:T(8,128)(2,1)} %own_hbm.1), channel_id=1, source_target_pairs={{0,4},{1,5},{2,6},{3,7},{4,8},{5,9},{6,10},{7,11},{8,12},{9,13},{1... | collective-permute-start | bytes 6291464 | tf_op jit(solution)/shard_map/ppermute | solution.py:22
  7.7 51.8 %collective-permute-start.4 = (bf16[256,4096]{1,0:T(8,128)(2,1)}, bf16[256,4096]{1,0:T(8,128)(2,1)}, u32[]{:S(2)}, u32[]{:S(2)}) collective-permute-start(bf16[256,4096]{1,0:T(8,128)(2,1)} %own_hbm.1), channel_id=1, source_target_pairs={{8,0},{9,1},{10,2},{11,3},{12,4},{13,5},{14,6},{15,7},{16,8},{17,9... | collective-permute-start | bytes 6291464 | tf_op jit(solution)/shard_map/ppermute | solution.py:22
  48.9 10.6 %collective-permute-start.2 = (bf16[256,4096]{1,0:T(8,128)(2,1)}, bf16[256,4096]{1,0:T(8,128)(2,1)}, u32[]{:S(2)}, u32[]{:S(2)}) collective-permute-start(bf16[256,4096]{1,0:T(8,128)(2,1)} %collective-permute-done.1.refs_2_), channel_id=1, source_target_pairs={{0,1},{1,0},{2,3},{3,2},{4,5},{5,4},{6,7},{7,6},{8,9},{9,8},{10,11... | collective-permute-start | bytes 6291464 | tf_op jit(solution)/shard_map/ppermute | solution.py:18
  49.7 1.6 %copy-start = (bf16[256,4096]{1,0:T(8,128)(2,1)S(1)}, bf16[256,4096]{1,0:T(8,128)(2,1)}, u32[]{:S(2)}) copy-start(bf16[256,4096]{1,0:T(8,128)(2,1)} %own_hbm.1) | copy-start | bytes 6291460
  78.5 7.6 %collective-permute-start.5 = (f32[2,256]{1,0:T(2,128)S(1)}, f32[2,256]{1,0:T(2,128)S(1)}, u32[]{:S(2)}, u32[]{:S(2)}) collective-permute-start(f32[2,256]{1,0:T(2,128)S(1)} %slice.13), channel_id=1, source_target_pairs={{0,1},{1,0},{2,3},{3,2},{4,5},{5,4},{6,7},{7,6},{8,9},{9,8},{10,11... | collective-permute-start | bytes 6152 | tf_op jit(solution)/shard_map/ppermute | solution.py:18
  79.0 8.6 %collective-permute-start.7 = (f32[1,256]{1,0:T(1,128)S(1)}, f32[1,256]{1,0:T(1,128)S(1)}, u32[]{:S(2)}, u32[]{:S(2)}) collective-permute-start(f32[1,256]{1,0:T(1,128)S(1)} %get-tuple-element.17), channel_id=1, source_target_pairs={{4,0},{5,1},{6,2},{7,3},{8,4},{9,5},{10,6},{11,7},{12,8},{13,9},{1... | collective-permute-start | bytes 3080 | tf_op jit(solution)/shard_map/ppermute | solution.py:22
  80.3 7.3 %collective-permute-start.8 = (f32[1,256]{1,0:T(1,128)S(1)}, f32[1,256]{1,0:T(1,128)S(1)}, u32[]{:S(2)}, u32[]{:S(2)}) collective-permute-start(f32[1,256]{1,0:T(1,128)S(1)} %get-tuple-element.18), channel_id=1, source_target_pairs={{0,8},{1,9},{2,10},{3,11},{4,12},{5,13},{6,14},{7,15},{8,16},{9,17... | collective-permute-start | bytes 3080 | tf_op jit(solution)/shard_map/ppermute | solution.py:22
  86.0 3.6 %collective-permute-start.6 = (f32[1,256]{1,0:T(1,128)S(1)}, f32[1,256]{1,0:T(1,128)S(1)}, u32[]{:S(2)}, u32[]{:S(2)}) collective-permute-start(f32[1,256]{1,0:T(1,128)S(1)} %slice.17), channel_id=1, source_target_pairs={{0,2},{1,3},{2,0},{3,1},{4,6},{5,7},{6,4},{7,5},{8,10},{9,11},{10,... | collective-permute-start | bytes 3080 | tf_op jit(solution)/shard_map/ppermute | solution.py:18

commit v2 on v1

v2 whole, which is shorter than its diff:
```python
import functools

import jax
import jax.numpy as jnp
from jax import lax
from jax.experimental import pallas as pl
from jax.experimental.pallas import tpu as pltpu
from jax.sharding import PartitionSpec as P

AXES = ("row", "col")
QUAD = 4
STRIP = 16
FILLER = -2.0
NT = (((1,), (1,)), ((), ()))


def swapped(x, devices, bit):
    return lax.ppermute(x, AXES, [(i, i ^ bit) for i in range(devices)])


def shifted(x, devices, by):
    return lax.ppermute(x, AXES, [(i, i + by) for i in range(devices) if 0 <= i + by < devices])


def labels_of(bounds_ref, block, length, axis):
    shape = (length, 1) if axis == 0 else (1, length)
    positions = block * length + lax.broadcasted_iota(jnp.int32, shape, axis)
    labels = jnp.where(positions < 0, -1, 0)
    for c in range(bounds_ref.shape[0]):
        labels = labels + (bounds_ref[c] <= positions).astype(jnp.int32)
    return labels


def label_at(bounds_ref, row):
    label = jnp.where(row < 0, -1, 0)
    for c in range(bounds_ref.shape[0]):
        label = label + jnp.where(bounds_ref[c] <= row, 1, 0)
    return label


def touch(bounds_ref, one, other, length):
    lower, upper = jnp.minimum(one, other), jnp.maximum(one, other)
    return label_at(bounds_ref, (lower + 1) * length - 1) == label_at(bounds_ref, upper * length)


def masked_scores(left, right, left_labels, right_labels):
    scores = lax.dot_general(left[...], right[...], NT, preferred_element_type=jnp.float32)
    return jnp.where(left_labels == right_labels, scores, FILLER)


def folded(masked):
    result = masked[:, :128]
    for i in range(128, masked.shape[1], 128):
        result = jnp.maximum(result, masked[:, i:i + 128])
    return result


def over_rows(masked):
    return jnp.max(masked, axis=0, keepdims=True)


def normalize_kernel(raw_hbm, normed_hbm, raw, normed, in_sems, out_sems):
    pieces = in_sems.shape[0]
    length = raw.shape[0] // pieces
    incoming, outgoing = [], []
    for i in range(pieces):
        rows = pl.ds(i * length, length)
        incoming.append(pltpu.make_async_copy(raw_hbm.at[rows], raw.at[rows], in_sems.at[i]))
        outgoing.append(pltpu.make_async_copy(normed.at[rows], normed_hbm.at[rows], out_sems.at[i]))
    for copy in incoming:
        copy.start()
    for i in range(pieces):
        incoming[i].wait()
        for j in range(0, length, STRIP):
            rows = pl.ds(i * length + j, STRIP)
            widened = raw[rows, :].astype(jnp.float32)
            squares = jnp.sum(widened * widened, axis=1, keepdims=True) + 1e-06
            normed[rows, :] = (widened * lax.rsqrt(squares)).astype(jnp.bfloat16)
        outgoing[i].start()
    for copy in outgoing:
        copy.wait()


def chip_kernel(bounds_ref, place_ref, own_hbm, near_hbm, best_out, own, near, sems):
    length = own.shape[0]
    copies = [pltpu.make_async_copy(own_hbm, own, sems.at[0]), pltpu.make_async_copy(near_hbm, near, sems.at[1])]
    for copy in copies:
        copy.start()
    place = place_ref[0]
    own_labels = labels_of(bounds_ref, place, length, 1)
    copies[0].wait()
    scores = masked_scores(own, own, labels_of(bounds_ref, place, length, 0), own_labels)
    same = lax.broadcasted_iota(jnp.int32, scores.shape, 0) == lax.broadcasted_iota(jnp.int32, scores.shape, 1)
    best = over_rows(jnp.where(same, FILLER, scores))
    copies[1].wait()
    scores = masked_scores(near, own, labels_of(bounds_ref, place ^ 1, length, 0), own_labels)
    best_out[...] = jnp.maximum(best, over_rows(scores))


def quad_kernel(bounds_ref, place_ref, *refs):
    sources, (best_in, best_out, quad_out, below_out, above_out), held, (widest, sems) = refs[:6], refs[6:11], refs[11:17], refs[17:]
    length = held[0].shape[0]
    copies = [pltpu.make_async_copy(sources[i], held[i], sems.at[i]) for i in range(6)]
    for i in (4, 0, 1, 5, 2, 3):
        copies[i].start()
    place = place_ref[0]
    outside = (place - QUAD, place + 2 * QUAD)
    outside_labels = [labels_of(bounds_ref, block, length, 0) for block in outside]
    widest[...] = jnp.full_like(widest, FILLER)
    quad_out[...] = jnp.full_like(quad_out, FILLER)
    best_out[...] = best_in[...]
    for b in range(QUAD):
        block = place ^ b
        block_labels = labels_of(bounds_ref, block, length, 1)
        for side in range(2):
            if b == 0:
                copies[4 + side].wait()
            if side == 0:
                copies[b].wait()

            @pl.when(touch(bounds_ref, block, outside[side], length))
            def _():
                scores = masked_scores(held[4 + side], held[b], outside_labels[side], block_labels)
                widest[side] = jnp.maximum(widest[side], folded(scores))
                quad_out[b:b + 1, :] = jnp.maximum(quad_out[b:b + 1, :], over_rows(scores))

        if b >= 2:

            @pl.when(touch(bounds_ref, block, place, length))
            def _():
                own_labels = labels_of(bounds_ref, place, length, 1)
                scores = masked_scores(held[b], held[0], labels_of(bounds_ref, block, length, 0), own_labels)
                best_out[...] = jnp.maximum(best_out[...], over_rows(scores))

    below_out[...] = over_rows(widest[0].T)
    above_out[...] = over_rows(widest[1].T)


ANY = pl.BlockSpec(memory_space=pl.ANY)
VMEM = pl.BlockSpec(memory_space=pltpu.VMEM)
SMEM = pl.BlockSpec(memory_space=pltpu.SMEM)


def cost(products, blocks, length, width):
    return pl.CostEstimate(flops=2 * products * length * length * width, bytes_accessed=2 * blocks * length * width, transcendentals=0)


def local(devices, embeddings, cluster_sizes):
    length, width = embeddings.shape
    block = jax.ShapeDtypeStruct((length, width), jnp.bfloat16)
    line = jax.ShapeDtypeStruct((1, length), jnp.float32)
    place = lax.axis_index(AXES).astype(jnp.int32)
    bounds = jnp.cumsum(cluster_sizes).astype(jnp.int32)
    where = place.reshape(1)

    normed = pl.pallas_call(
        normalize_kernel,
        out_shape=block,
        in_specs=[ANY],
        out_specs=ANY,
        scratch_shapes=[pltpu.VMEM((length, width), jnp.bfloat16)] * 2 + [pltpu.SemaphoreType.DMA((4,))] * 2,
        compiler_params=pltpu.CompilerParams(vmem_limit_bytes=60 << 20),
        cost_estimate=cost(0, 2, length, width),
    )(embeddings)

    across = swapped(normed, devices, 2)
    below = shifted(normed, devices, QUAD)
    above = shifted(normed, devices, -2 * QUAD)
    near = swapped(normed, devices, 1)

    chip_best = pl.pallas_call(
        chip_kernel,
        out_shape=line,
        in_specs=[SMEM, SMEM, ANY, ANY],
        out_specs=VMEM,
        scratch_shapes=[pltpu.VMEM((length, width), jnp.bfloat16)] * 2 + [pltpu.SemaphoreType.DMA((2,))],
        compiler_params=pltpu.CompilerParams(vmem_limit_bytes=24 << 20),
        cost_estimate=cost(2, 4, length, width),
    )(bounds, where, normed, near)

    across, chip_best = lax.optimization_barrier((across, chip_best))
    across_near = swapped(across, devices, 1)

    best, quad, to_below, to_above = pl.pallas_call(
        quad_kernel,
        out_shape=(line, jax.ShapeDtypeStruct((QUAD, length), jnp.float32), line, line),
        in_specs=[SMEM, SMEM] + [ANY] * 6 + [VMEM],
        out_specs=(VMEM,) * 4,
        scratch_shapes=[pltpu.VMEM((length, width), jnp.bfloat16)] * 6
        + [pltpu.VMEM((2, length, 128), jnp.float32), pltpu.SemaphoreType.DMA((6,))],
        compiler_params=pltpu.CompilerParams(vmem_limit_bytes=32 << 20),
        cost_estimate=cost(10, 6, length, width),
    )(bounds, where, normed, near, across, across_near, below, above, chip_best)

    filler = jnp.float32(FILLER)
    from_next = shifted(to_below, devices, -QUAD)
    from_previous = shifted(to_above, devices, 2 * QUAD)
    swapped_chip = swapped(quad[1::2], devices, 1)
    own_chip = jnp.maximum(quad[0::2], swapped_chip)
    swapped_quad = swapped(own_chip[1:2], devices, 2)
    best = jnp.maximum(jnp.maximum(best, own_chip[0:1]), swapped_quad)
    best = jnp.maximum(best, jnp.where(place + QUAD < devices, from_next, filler))
    best = jnp.maximum(best, jnp.where(place >= 2 * QUAD, from_previous, filler))
    return best.reshape(length)


def solution(mesh):
    devices = 1
    for axis in AXES:
        devices *= mesh.shape[axis]
    in_specs = (P(AXES, None), P())
    return jax.shard_map(functools.partial(local, devices), mesh=mesh, in_specs=in_specs, out_specs=P(AXES), check_vma=False)
```

time: 90.5 us -> 75.1 us (0.83)
  Pallas kernels: 27 us -> 11.5 us
  waiting for transfers between devices: 42 us -> 44.8 us
  starting transfers between devices: 18.1 us -> 16 us
    pallas_call x1, Pallas kernels: 18.9 us -> 5.31 us  [local(): pl.pallas_call(quad_kernel, out_shape=(line, jax.ShapeDtypeStruct((QUAD,...]
    ppermute x4, waiting for transfers between devices: 0.01 us -> 7.8 us  [shifted(): lax.ppermute(x, AXES, [(i, i + by) for i in range(devices) if 0 <= i + by...]
    ppermute x5, waiting for transfers between devices: 42 us -> 36.9 us  [swapped(): return lax.ppermute(x, AXES, [(i, i ^ bit) for i in range(devices)])]
    ppermute x4, starting transfers between devices: 13 us -> 10.9 us  [shifted(): lax.ppermute(x, AXES, [(i, i + by) for i in range(devices) if 0 <= i + by...]
    pallas_call x1 -> x2, Pallas kernels: 8.13 us -> 6.19 us  [the longest x1 3.42 us: local(): pl.pallas_call(chip_kernel, out_shape=line, in_specs=[SMEM, SMEM, ANY, AN...]
  transfers between devices with their start and end apart: 9 -> 9, of which waited for: 2 -> 4; matrix products, arithmetic and copies ran while one was open for 1% -> 0% of each run, Pallas kernels for 9% -> 5%
where the time goes in v2:
time: 75.1 us; the launch traced here: 74.8 us
  waiting for transfers between devices  44.8 us (60%)
  starting transfers between devices  16 us (21%)
  Pallas kernels  11.5 us (15%)
  local copies, waits for them, and re-layouts  1.66 us (2%)
  other arithmetic  0.76 us (1%)
    ppermute x5, waiting for transfers between devices, swapped(): return lax.ppermute(x, AXES, [(i, i ^ bit) for i in range(devices)])  36.9 us
    ppermute x4, starting transfers between devices, shifted(): lax.ppermute(x, AXES, [(i, i + by) for i in range(devices) if 0 <= i + by...  10.9 us
    ppermute x4, waiting for transfers between devices, shifted(): lax.ppermute(x, AXES, [(i, i + by) for i in range(devices) if 0 <= i + by...  7.8 us
    pallas_call x1, Pallas kernels, local(): pl.pallas_call(quad_kernel, out_shape=(line, jax.ShapeDtypeStruct((QUAD,...  5.31 us
    ppermute x5, starting transfers between devices, swapped(): return lax.ppermute(x, AXES, [(i, i ^ bit) for i in range(devices)])  5.16 us
    pallas_call x1, Pallas kernels, local(): pl.pallas_call(chip_kernel, out_shape=line, in_specs=[SMEM, SMEM, ANY, AN...  3.42 us
    pallas_call x1, Pallas kernels, local(): pl.pallas_call(normalize_kernel, out_shape=block, in_specs=[ANY], out_spe...  2.77 us
    unnamed x6, local copies, waits for them, and re-layouts  1.6 us
  transfers between devices with their start and end apart: 9, of which 4 were waited for; matrix products, arithmetic and copies ran while one was open for 0% of the time, Pallas kernels for 5%

profile of v2, /device:TPU:0, one launch (start us, length us, event | category | flops | bytes accessed | tf_op | source)
XLA Modules:
  0.0 74.8 jit_solution(13556178639689868983)
XLA Ops:
  0.0 0.0 copy-start.2
  0.0 2.8 %shard_map.28.own_hbm.refs_0_ = bf16[256,4096]{1,0:T(8,128)(2,1)} custom-call(bf16[256,4096]{1,0:T(8,128)(2,1)} %raw_hbm.1), custom_call_target="tpu_custom_call" | custom-call | bytes 4194304 | tf_op jit(solution)/shard_map/pallas_call | solution.py:156
  2.8 0.5 collective-permute-start
  3.3 2.6 %collective-permute-start.1 = (bf16[256,4096]{1,0:T(8,128)(2,1)}, bf16[256,4096]{1,0:T(8,128)(2,1)}, u32[]{:S(2)}, u32[]{:S(2)}) collective-permute-start(bf16[256,4096]{1,0:T(8,128)(2,1)} %shard_map.28.own_hbm.refs_0_), channel_id=1, source_target_pairs={{0,2},{1,3},{2,0},{3,1},{4,6},{5,7},{6,4},{7,5},{8,10},{9,11},{10,... | collective-permute-start | bytes 6291464 | tf_op jit(solution)/shard_map/ppermute | solution.py:18
  5.9 4.7 %collective-permute-start.3 = (bf16[256,4096]{1,0:T(8,128)(2,1)}, bf16[256,4096]{1,0:T(8,128)(2,1)}, u32[]{:S(2)}, u32[]{:S(2)}) collective-permute-start(bf16[256,4096]{1,0:T(8,128)(2,1)} %shard_map.28.own_hbm.refs_0_), channel_id=1, source_target_pairs={{0,4},{1,5},{2,6},{3,7},{4,8},{5,9},{6,10},{7,11},{8,12},{9,13},{1... | collective-permute-start | bytes 6291464 | tf_op jit(solution)/shard_map/ppermute | solution.py:22
  10.6 1.3 %collective-permute-start.4 = (bf16[256,4096]{1,0:T(8,128)(2,1)}, bf16[256,4096]{1,0:T(8,128)(2,1)}, u32[]{:S(2)}, u32[]{:S(2)}) collective-permute-start(bf16[256,4096]{1,0:T(8,128)(2,1)} %shard_map.28.own_hbm.refs_0_), channel_id=1, source_target_pairs={{8,0},{9,1},{10,2},{11,3},{12,4},{13,5},{14,6},{15,7},{16,8},{17,9... | collective-permute-start | bytes 6291464 | tf_op jit(solution)/shard_map/ppermute | solution.py:22
  11.9 0.0 copy-done.2
  11.9 0.2 reduce-window.9
  12.1 0.0 collective-permute-done.near_hbm.refs_1_
  12.1 0.0 copy-start
  12.1 1.6 %copy-done = bf16[256,4096]{1,0:T(8,128)(2,1)S(1)} copy-done((bf16[256,4096]{1,0:T(8,128)(2,1)S(1)}, bf16[256,4096]{1,0:T(8,128)(2,1)}, u32[]{:S(2)}) %copy-start) | copy-done | bytes 2097176
  13.7 0.0 copy-start.1
  13.7 3.4 %shard_map.29.refs_6_ = f32[1,256]{1,0:T(1,128)S(1)} custom-call(s32[8]{0:T(128)S(1)} %bitcast.4, s32[1]{0:T(128)} %bitcast.2.place_ref, bf16[256,4096]{1,0:T(8,128)(2,1)S(1)} %copy-done, bf16[256,4096]{1,0:T(8,128)(2,1)S(1)} %collective-permute-done.near_hbm.refs_1_), custom_call_target="tpu_custom_call" | custom-call | flops 1073741824 | bytes 8388608 | tf_op jit(solution)/shard_map/pallas_call | solution.py:171
  17.1 35.3 %collective-permute-done.1.refs_2_ = bf16[256,4096]{1,0:T(8,128)(2,1)} collective-permute-done((bf16[256,4096]{1,0:T(8,128)(2,1)}, bf16[256,4096]{1,0:T(8,128)(2,1)}, u32[]{:S(2)}, u32[]{:S(2)}) %collective-permute-start.1) | collective-permute-done | bytes 2097184 | tf_op jit(solution)/shard_map/ppermute | solution.py:18
  52.4 0.0 collective-permute-start.2
  52.4 2.4 %collective-permute-done.3.refs_4_ = bf16[256,4096]{1,0:T(8,128)(2,1)} collective-permute-done((bf16[256,4096]{1,0:T(8,128)(2,1)}, bf16[256,4096]{1,0:T(8,128)(2,1)}, u32[]{:S(2)}, u32[]{:S(2)}) %collective-permute-start.3) | collective-permute-done | bytes 2097184 | tf_op jit(solution)/shard_map/ppermute | solution.py:22
  54.8 5.4 %collective-permute-done.4.refs_5_ = bf16[256,4096]{1,0:T(8,128)(2,1)} collective-permute-done((bf16[256,4096]{1,0:T(8,128)(2,1)}, bf16[256,4096]{1,0:T(8,128)(2,1)}, u32[]{:S(2)}, u32[]{:S(2)}) %collective-permute-start.4) | collective-permute-done | bytes 2097184 | tf_op jit(solution)/shard_map/ppermute | solution.py:22
  60.2 0.0 collective-permute-done.2.refs_3_
  60.2 0.0 copy-done.1
  60.2 5.3 %shard_map.30 = (f32[1,256]{1,0:T(1,128)S(1)}, f32[4,256]{1,0:T(4,128)S(1)}, f32[1,256]{1,0:T(1,128)S(1)}, f32[1,256]{1,0:T(1,128)S(1)}) custom-call(s32[8]{0:T(128)S(1)} %bitcast.5, s32[1]{0:T(128)} %bitcast.2.place_ref, bf16[256,4096]{1,0:T(8,128)(2,1)S(1)} %copy-done.1, bf16[256,4096]{1,0:T(8,128)(2,1)S(1)} %collective-permute-done.near_hbm.refs_1_, ...), custom_call_target="tpu_custom_call" | custom-call | flops 5368709120 | bytes 12582912 | tf_op jit(solution)/shard_map/pallas_call | solution.py:184
  65.6 0.1 collective-permute-start.5
  65.7 1.3 %collective-permute-start.7 = (f32[1,256]{1,0:T(1,128)S(1)}, f32[1,256]{1,0:T(1,128)S(1)}, u32[]{:S(2)}, u32[]{:S(2)}) collective-permute-start(f32[1,256]{1,0:T(1,128)S(1)} %get-tuple-element.15), channel_id=1, source_target_pairs={{4,0},{5,1},{6,2},{7,3},{8,4},{9,5},{10,6},{11,7},{12,8},{13,9},{1... | collective-permute-start | bytes 3080 | tf_op jit(solution)/shard_map/ppermute | solution.py:22
  67.0 3.6 %collective-permute-start.8 = (f32[1,256]{1,0:T(1,128)S(1)}, f32[1,256]{1,0:T(1,128)S(1)}, u32[]{:S(2)}, u32[]{:S(2)}) collective-permute-start(f32[1,256]{1,0:T(1,128)S(1)} %get-tuple-element.16), channel_id=1, source_target_pairs={{0,8},{1,9},{2,10},{3,11},{4,12},{5,13},{6,14},{7,15},{8,16},{9,17... | collective-permute-start | bytes 3080 | tf_op jit(solution)/shard_map/ppermute | solution.py:22
  70.6 0.0 collective-permute-done.5
  70.6 2.0 %collective-permute-start.6 = (f32[1,256]{1,0:T(1,128)S(1)}, f32[1,256]{1,0:T(1,128)S(1)}, u32[]{:S(2)}, u32[]{:S(2)}) collective-permute-start(f32[1,256]{1,0:T(1,128)S(1)} %slice.17), channel_id=1, source_target_pairs={{0,2},{1,3},{2,0},{3,1},{4,6},{5,7},{6,4},{7,5},{8,10},{9,11},{10,... | collective-permute-start | bytes 3080 | tf_op jit(solution)/shard_map/ppermute | solution.py:18
  72.6 0.0 collective-permute-done.7
  72.6 0.0 collective-permute-done.8
  72.6 1.6 %collective-permute-done.6 = f32[1,256]{1,0:T(1,128)S(1)} collective-permute-done((f32[1,256]{1,0:T(1,128)S(1)}, f32[1,256]{1,0:T(1,128)S(1)}, u32[]{:S(2)}, u32[]{:S(2)}) %collective-permute-start.6) | collective-permute-done | bytes 1056 | tf_op jit(solution)/shard_map/ppermute | solution.py:18
  74.2 0.6 fusion.1
  (4 shorter events, 0.1 us)
Async XLA Ops:
  0.0 11.9 %copy-start.2 = (s32[8]{0:T(128)S(1)}, s32[8]{0:T(128)}, u32[]{:S(2)}) copy-start(s32[8]{0:T(128)} %param.3) | copy-start | bytes 100
  2.8 9.3 %collective-permute-start = (bf16[256,4096]{1,0:T(8,128)(2,1)}, bf16[256,4096]{1,0:T(8,128)(2,1)S(1)}, u32[]{:S(2)}, u32[]{:S(2)}) collective-permute-start(bf16[256,4096]{1,0:T(8,128)(2,1)} %shard_map.28.own_hbm.refs_0_), channel_id=1, source_target_pairs={{0,1},{1,0},{2,3},{3,2},{4,5},{5,4},{6,7},{7,6},{8,9},{9,8},{10,11... | collective-permute-start | bytes 6291464 | tf_op jit(solution)/shard_map/ppermute | solution.py:18
  3.3 49.1 %collective-permute-start.1 = (bf16[256,4096]{1,0:T(8,128)(2,1)}, bf16[256,4096]{1,0:T(8,128)(2,1)}, u32[]{:S(2)}, u32[]{:S(2)}) collective-permute-start(bf16[256,4096]{1,0:T(8,128)(2,1)} %shard_map.28.own_hbm.refs_0_), channel_id=1, source_target_pairs={{0,2},{1,3},{2,0},{3,1},{4,6},{5,7},{6,4},{7,5},{8,10},{9,11},{10,... | collective-permute-start | bytes 6291464 | tf_op jit(solution)/shard_map/ppermute | solution.py:18
  5.9 48.9 %collective-permute-start.3 = (bf16[256,4096]{1,0:T(8,128)(2,1)}, bf16[256,4096]{1,0:T(8,128)(2,1)}, u32[]{:S(2)}, u32[]{:S(2)}) collective-permute-start(bf16[256,4096]{1,0:T(8,128)(2,1)} %shard_map.28.own_hbm.refs_0_), channel_id=1, source_target_pairs={{0,4},{1,5},{2,6},{3,7},{4,8},{5,9},{6,10},{7,11},{8,12},{9,13},{1... | collective-permute-start | bytes 6291464 | tf_op jit(solution)/shard_map/ppermute | solution.py:22
  10.6 49.6 %collective-permute-start.4 = (bf16[256,4096]{1,0:T(8,128)(2,1)}, bf16[256,4096]{1,0:T(8,128)(2,1)}, u32[]{:S(2)}, u32[]{:S(2)}) collective-permute-start(bf16[256,4096]{1,0:T(8,128)(2,1)} %shard_map.28.own_hbm.refs_0_), channel_id=1, source_target_pairs={{8,0},{9,1},{10,2},{11,3},{12,4},{13,5},{14,6},{15,7},{16,8},{17,9... | collective-permute-start | bytes 6291464 | tf_op jit(solution)/shard_map/ppermute | solution.py:22
  12.1 1.6 %copy-start = (bf16[256,4096]{1,0:T(8,128)(2,1)S(1)}, bf16[256,4096]{1,0:T(8,128)(2,1)}, u32[]{:S(2)}) copy-start(bf16[256,4096]{1,0:T(8,128)(2,1)} %shard_map.28.own_hbm.refs_0_) | copy-start | bytes 6291460
  13.7 46.5 %copy-start.1 = (bf16[256,4096]{1,0:T(8,128)(2,1)S(1)}, bf16[256,4096]{1,0:T(8,128)(2,1)}, u32[]{:S(2)}) copy-start(bf16[256,4096]{1,0:T(8,128)(2,1)} %shard_map.28.own_hbm.refs_0_) | copy-start | bytes 6291460
  52.4 7.8 %collective-permute-start.2 = (bf16[256,4096]{1,0:T(8,128)(2,1)}, bf16[256,4096]{1,0:T(8,128)(2,1)S(1)}, u32[]{:S(2)}, u32[]{:S(2)}) collective-permute-start(bf16[256,4096]{1,0:T(8,128)(2,1)} %collective-permute-done.1.refs_2_), channel_id=1, source_target_pairs={{0,1},{1,0},{2,3},{3,2},{4,5},{5,4},{6,7},{7,6},{8,9},{9,8},{10,11... | collective-permute-start | bytes 6291464 | tf_op jit(solution)/shard_map/ppermute | solution.py:18
  65.6 5.0 %collective-permute-start.5 = (f32[2,256]{1,0:T(2,128)S(1)}, f32[2,256]{1,0:T(2,128)S(1)}, u32[]{:S(2)}, u32[]{:S(2)}) collective-permute-start(f32[2,256]{1,0:T(2,128)S(1)} %slice.13), channel_id=1, source_target_pairs={{0,1},{1,0},{2,3},{3,2},{4,5},{5,4},{6,7},{7,6},{8,9},{9,8},{10,11... | collective-permute-start | bytes 6152 | tf_op jit(solution)/shard_map/ppermute | solution.py:18
  65.7 6.9 %collective-permute-start.7 = (f32[1,256]{1,0:T(1,128)S(1)}, f32[1,256]{1,0:T(1,128)S(1)}, u32[]{:S(2)}, u32[]{:S(2)}) collective-permute-start(f32[1,256]{1,0:T(1,128)S(1)} %get-tuple-element.15), channel_id=1, source_target_pairs={{4,0},{5,1},{6,2},{7,3},{8,4},{9,5},{10,6},{11,7},{12,8},{13,9},{1... | collective-permute-start | bytes 3080 | tf_op jit(solution)/shard_map/ppermute | solution.py:22
  67.0 5.6 %collective-permute-start.8 = (f32[1,256]{1,0:T(1,128)S(1)}, f32[1,256]{1,0:T(1,128)S(1)}, u32[]{:S(2)}, u32[]{:S(2)}) collective-permute-start(f32[1,256]{1,0:T(1,128)S(1)} %get-tuple-element.16), channel_id=1, source_target_pairs={{0,8},{1,9},{2,10},{3,11},{4,12},{5,13},{6,14},{7,15},{8,16},{9,17... | collective-permute-start | bytes 3080 | tf_op jit(solution)/shard_map/ppermute | solution.py:22
  70.6 3.6 %collective-permute-start.6 = (f32[1,256]{1,0:T(1,128)S(1)}, f32[1,256]{1,0:T(1,128)S(1)}, u32[]{:S(2)}, u32[]{:S(2)}) collective-permute-start(f32[1,256]{1,0:T(1,128)S(1)} %slice.17), channel_id=1, source_target_pairs={{0,2},{1,3},{2,0},{3,1},{4,6},{5,7},{6,4},{7,5},{8,10},{9,11},{10,... | collective-permute-start | bytes 3080 | tf_op jit(solution)/shard_map/ppermute | solution.py:18

commit v3 on v2

--- a/solution.py
+++ b/solution.py
@@ -18,8 +18,9 @@
     return lax.ppermute(x, AXES, [(i, i ^ bit) for i in range(devices)])
 
 
-def shifted(x, devices, by):
-    return lax.ppermute(x, AXES, [(i, i + by) for i in range(devices) if 0 <= i + by < devices])
+def shifted(x, devices, even, odd):
+    moves = [(i, i + (odd if i % 2 else even)) for i in range(devices)]
+    return lax.ppermute(x, AXES, [(i, j) for i, j in moves if 0 <= j < devices])
 
 
 def labels_of(bounds_ref, block, length, axis):
@@ -98,13 +99,15 @@
 
 
 def quad_kernel(bounds_ref, place_ref, *refs):
-    sources, (best_in, best_out, quad_out, below_out, above_out), held, (widest, sems) = refs[:6], refs[6:11], refs[11:17], refs[17:]
+    sources, (best_in, best_out, quad_out, first_out, second_out), held, (widest, sems) = refs[:6], refs[6:11], refs[11:17], refs[17:]
     length = held[0].shape[0]
     copies = [pltpu.make_async_copy(sources[i], held[i], sems.at[i]) for i in range(6)]
     for i in (4, 0, 1, 5, 2, 3):
         copies[i].start()
     place = place_ref[0]
-    outside = (place - QUAD, place + 2 * QUAD)
+    below, above = place - QUAD, place + 2 * QUAD
+    even = place % 2 == 0
+    outside = (jnp.where(even, below, above), jnp.where(even, above, below))
     outside_labels = [labels_of(bounds_ref, block, length, 0) for block in outside]
     widest[...] = jnp.full_like(widest, FILLER)
     quad_out[...] = jnp.full_like(quad_out, FILLER)
@@ -132,8 +135,8 @@
                 scores = masked_scores(held[b], held[0], labels_of(bounds_ref, block, length, 0), own_labels)
                 best_out[...] = jnp.maximum(best_out[...], over_rows(scores))
 
-    below_out[...] = over_rows(widest[0].T)
-    above_out[...] = over_rows(widest[1].T)
+    first_out[...] = over_rows(widest[0].T)
+    second_out[...] = over_rows(widest[1].T)
 
 
 ANY = pl.BlockSpec(memory_space=pl.ANY)
@@ -164,8 +167,9 @@
     )(embeddings)
 
     across = swapped(normed, devices, 2)
-    below = shifted(normed, devices, QUAD)
-    above = shifted(normed, devices, -2 * QUAD)
+    first = shifted(normed, devices, QUAD, -2 * QUAD)
+    second = shifted(normed, devices, -2 * QUAD, QUAD)
+
     near = swapped(normed, devices, 1)
 
     chip_best = pl.pallas_call(
@@ -181,7 +185,7 @@
     across, chip_best = lax.optimization_barrier((across, chip_best))
     across_near = swapped(across, devices, 1)
 
-    best, quad, to_below, to_above = pl.pallas_call(
+    best, quad, first_best, second_best = pl.pallas_call(
         quad_kernel,
         out_shape=(line, jax.ShapeDtypeStruct((QUAD, length), jnp.float32), line, line),
         in_specs=[SMEM, SMEM] + [ANY] * 6 + [VMEM],
@@ -190,17 +194,19 @@
         + [pltpu.VMEM((2, length, 128), jnp.float32), pltpu.SemaphoreType.DMA((6,))],
         compiler_params=pltpu.CompilerParams(vmem_limit_bytes=32 << 20),
         cost_estimate=cost(10, 6, length, width),
-    )(bounds, where, normed, near, across, across_near, below, above, chip_best)
-
-    filler = jnp.float32(FILLER)
-    from_next = shifted(to_below, devices, -QUAD)
-    from_previous = shifted(to_above, devices, 2 * QUAD)
+    )(bounds, where, normed, near, across, across_near, first, second, chip_best)
+
     swapped_chip = swapped(quad[1::2], devices, 1)
+    first_back = shifted(first_best, devices, -QUAD, 2 * QUAD)
+    second_back = shifted(second_best, devices, 2 * QUAD, -QUAD)
     own_chip = jnp.maximum(quad[0::2], swapped_chip)
     swapped_quad = swapped(own_chip[1:2], devices, 2)
     best = jnp.maximum(jnp.maximum(best, own_chip[0:1]), swapped_quad)
-    best = jnp.maximum(best, jnp.where(place + QUAD < devices, from_next, filler))
-    best = jnp.maximum(best, jnp.where(place >= 2 * QUAD, from_previous, filler))
+    even = place % 2 == 0
+    from_next, from_previous = place + QUAD < devices, place >= 2 * QUAD
+    filler = jnp.float32(FILLER)
+    best = jnp.maximum(best, jnp.where(jnp.where(even, from_next, from_previous), first_back, filler))
+    best = jnp.maximum(best, jnp.where(jnp.where(even, from_previous, from_next), second_back, filler))
     return best.reshape(length)
 
 

time: 75.1 us -> 74.4 us (level)
  waiting for transfers between devices: 44.8 us -> 41.2 us
  starting transfers between devices: 16 us -> 18.6 us
    ppermute x4, waiting for transfers between devices: 7.8 us -> 3.36 us  [shifted(): return lax.ppermute(x, AXES, [(i, j) for i, j in moves if 0 <= j < devices])]
    ppermute x4, starting transfers between devices: 10.9 us -> 12.5 us  [shifted(): return lax.ppermute(x, AXES, [(i, j) for i, j in moves if 0 <= j < devices])]
    ppermute x5, waiting for transfers between devices: 36.9 us -> 37.9 us  [swapped(): return lax.ppermute(x, AXES, [(i, i ^ bit) for i in range(devices)])]
    ppermute x5, starting transfers between devices: 5.16 us -> 6.06 us  [swapped(): return lax.ppermute(x, AXES, [(i, i ^ bit) for i in range(devices)])]
  transfers between devices with their start and end apart: 9 -> 9, of which waited for: 4 -> 5; matrix products, arithmetic and copies ran while one was open for 0% -> 0% of each run, Pallas kernels for 5% -> 5%
where the time goes in v3:
time: 74.4 us; the launch traced here: 73.8 us
  waiting for transfers between devices  41.2 us (55%)
  starting transfers between devices  18.6 us (25%)
  Pallas kernels  11.5 us (15%)
  local copies, waits for them, and re-layouts  1.66 us (2%)
  other arithmetic  0.76 us (1%)
    ppermute x5, waiting for transfers between devices, swapped(): return lax.ppermute(x, AXES, [(i, i ^ bit) for i in range(devices)])  37.9 us
    ppermute x4, starting transfers between devices, shifted(): return lax.ppermute(x, AXES, [(i, j) for i, j in moves if 0 <= j < devices])  12.5 us
    ppermute x5, starting transfers between devices, swapped(): return lax.ppermute(x, AXES, [(i, i ^ bit) for i in range(devices)])  6.06 us
    pallas_call x1, Pallas kernels, local(): pl.pallas_call(quad_kernel, out_shape=(line, jax.ShapeDtypeStruct((QUAD,...  5.31 us
    pallas_call x1, Pallas kernels, local(): pl.pallas_call(chip_kernel, out_shape=line, in_specs=[SMEM, SMEM, ANY, AN...  3.42 us
    ppermute x4, waiting for transfers between devices, shifted(): return lax.ppermute(x, AXES, [(i, j) for i, j in moves if 0 <= j < devices])  3.36 us
    pallas_call x1, Pallas kernels, local(): pl.pallas_call(normalize_kernel, out_shape=block, in_specs=[ANY], out_spe...  2.77 us
    unnamed x6, local copies, waits for them, and re-layouts  1.6 us
  transfers between devices with their start and end apart: 9, of which 5 were waited for; matrix products, arithmetic and copies ran while one was open for 0% of the time, Pallas kernels for 5%

profile of v3, /device:TPU:0, one launch (start us, length us, event | category | flops | bytes accessed | tf_op | source)
XLA Modules:
  0.0 73.8 jit_solution(10184676784208473763)
XLA Ops:
  0.0 0.0 copy-start.2
  0.0 2.8 %shard_map.28.own_hbm.refs_0_ = bf16[256,4096]{1,0:T(8,128)(2,1)} custom-call(bf16[256,4096]{1,0:T(8,128)(2,1)} %raw_hbm.1), custom_call_target="tpu_custom_call" | custom-call | bytes 4194304 | tf_op jit(solution)/shard_map/pallas_call | solution.py:159
  2.8 0.5 collective-permute-start
  3.3 2.6 %collective-permute-start.1 = (bf16[256,4096]{1,0:T(8,128)(2,1)}, bf16[256,4096]{1,0:T(8,128)(2,1)}, u32[]{:S(2)}, u32[]{:S(2)}) collective-permute-start(bf16[256,4096]{1,0:T(8,128)(2,1)} %shard_map.28.own_hbm.refs_0_), channel_id=1, source_target_pairs={{0,2},{1,3},{2,0},{3,1},{4,6},{5,7},{6,4},{7,5},{8,10},{9,11},{10,... | collective-permute-start | bytes 6291464 | tf_op jit(solution)/shard_map/ppermute | solution.py:18
  5.9 4.7 %collective-permute-start.3 = (bf16[256,4096]{1,0:T(8,128)(2,1)}, bf16[256,4096]{1,0:T(8,128)(2,1)}, u32[]{:S(2)}, u32[]{:S(2)}) collective-permute-start(bf16[256,4096]{1,0:T(8,128)(2,1)} %shard_map.28.own_hbm.refs_0_), channel_id=1, source_target_pairs={{0,4},{2,6},{4,8},{6,10},{8,12},{9,1},{10,14},{11,3},{12,16},{13,5... | collective-permute-start | bytes 6291464 | tf_op jit(solution)/shard_map/ppermute | solution.py:23
  10.6 1.3 %collective-permute-start.4 = (bf16[256,4096]{1,0:T(8,128)(2,1)}, bf16[256,4096]{1,0:T(8,128)(2,1)}, u32[]{:S(2)}, u32[]{:S(2)}) collective-permute-start(bf16[256,4096]{1,0:T(8,128)(2,1)} %shard_map.28.own_hbm.refs_0_), channel_id=1, source_target_pairs={{1,5},{3,7},{5,9},{7,11},{8,0},{9,13},{10,2},{11,15},{12,4},{13,17... | collective-permute-start | bytes 6291464 | tf_op jit(solution)/shard_map/ppermute | solution.py:23
  11.9 0.0 copy-done.2
  11.9 0.2 reduce-window.9
  12.1 0.0 collective-permute-done.near_hbm.refs_1_
  12.1 0.0 copy-start
  12.1 1.6 %copy-done = bf16[256,4096]{1,0:T(8,128)(2,1)S(1)} copy-done((bf16[256,4096]{1,0:T(8,128)(2,1)S(1)}, bf16[256,4096]{1,0:T(8,128)(2,1)}, u32[]{:S(2)}) %copy-start) | copy-done | bytes 2097176
  13.7 0.0 copy-start.1
  13.7 3.4 %shard_map.29.refs_6_ = f32[1,256]{1,0:T(1,128)S(1)} custom-call(s32[8]{0:T(128)S(1)} %bitcast.4, s32[1]{0:T(128)} %bitcast.2.place_ref, bf16[256,4096]{1,0:T(8,128)(2,1)S(1)} %copy-done, bf16[256,4096]{1,0:T(8,128)(2,1)S(1)} %collective-permute-done.near_hbm.refs_1_), custom_call_target="tpu_custom_call" | custom-call | flops 1073741824 | bytes 8388608 | tf_op jit(solution)/shard_map/pallas_call | solution.py:175
  17.1 35.3 %collective-permute-done.1.refs_2_ = bf16[256,4096]{1,0:T(8,128)(2,1)} collective-permute-done((bf16[256,4096]{1,0:T(8,128)(2,1)}, bf16[256,4096]{1,0:T(8,128)(2,1)}, u32[]{:S(2)}, u32[]{:S(2)}) %collective-permute-start.1) | collective-permute-done | bytes 2097184 | tf_op jit(solution)/shard_map/ppermute | solution.py:18
  52.4 0.0 collective-permute-start.2
  52.4 2.7 %collective-permute-done.3.refs_4_ = bf16[256,4096]{1,0:T(8,128)(2,1)} collective-permute-done((bf16[256,4096]{1,0:T(8,128)(2,1)}, bf16[256,4096]{1,0:T(8,128)(2,1)}, u32[]{:S(2)}, u32[]{:S(2)}) %collective-permute-start.3) | collective-permute-done | bytes 2097184 | tf_op jit(solution)/shard_map/ppermute | solution.py:23
  55.2 0.6 collective-permute-done.4.refs_5_
  55.8 1.0 %collective-permute-done.2.refs_3_ = bf16[256,4096]{1,0:T(8,128)(2,1)S(1)} collective-permute-done((bf16[256,4096]{1,0:T(8,128)(2,1)}, bf16[256,4096]{1,0:T(8,128)(2,1)S(1)}, u32[]{:S(2)}, u32[]{:S(2)}) %collective-permute-start.2) | collective-permute-done | bytes 2097184 | tf_op jit(solution)/shard_map/ppermute | solution.py:18
  56.8 0.0 copy-done.1
  56.8 5.3 %shard_map.30 = (f32[1,256]{1,0:T(1,128)S(1)}, f32[4,256]{1,0:T(4,128)S(1)}, f32[1,256]{1,0:T(1,128)S(1)}, f32[1,256]{1,0:T(1,128)S(1)}) custom-call(s32[8]{0:T(128)S(1)} %bitcast.5, s32[1]{0:T(128)} %bitcast.2.place_ref, bf16[256,4096]{1,0:T(8,128)(2,1)S(1)} %copy-done.1, bf16[256,4096]{1,0:T(8,128)(2,1)S(1)} %collective-permute-done.near_hbm.refs_1_, ...), custom_call_target="tpu_custom_call" | custom-call | flops 5368709120 | bytes 12582912 | tf_op jit(solution)/shard_map/pallas_call | solution.py:188
  62.2 0.2 collective-permute-start.5
  62.4 1.3 %collective-permute-start.7 = (f32[1,256]{1,0:T(1,128)S(1)}, f32[1,256]{1,0:T(1,128)S(1)}, u32[]{:S(2)}, u32[]{:S(2)}) collective-permute-start(f32[1,256]{1,0:T(1,128)S(1)} %get-tuple-element.15), channel_id=1, source_target_pairs={{1,9},{3,11},{4,0},{5,13},{6,2},{7,15},{8,4},{9,17},{10,6},{11,19}... | collective-permute-start | bytes 3080 | tf_op jit(solution)/shard_map/ppermute | solution.py:23
  63.7 5.2 %collective-permute-start.8 = (f32[1,256]{1,0:T(1,128)S(1)}, f32[1,256]{1,0:T(1,128)S(1)}, u32[]{:S(2)}, u32[]{:S(2)}) collective-permute-start(f32[1,256]{1,0:T(1,128)S(1)} %get-tuple-element.16), channel_id=1, source_target_pairs={{0,8},{2,10},{4,12},{5,1},{6,14},{7,3},{8,16},{9,5},{10,18},{11,7}... | collective-permute-start | bytes 3080 | tf_op jit(solution)/shard_map/ppermute | solution.py:23
  68.9 0.0 collective-permute-done.5
  68.9 2.8 %collective-permute-start.6 = (f32[1,256]{1,0:T(1,128)S(1)}, f32[1,256]{1,0:T(1,128)S(1)}, u32[]{:S(2)}, u32[]{:S(2)}) collective-permute-start(f32[1,256]{1,0:T(1,128)S(1)} %slice.17), channel_id=1, source_target_pairs={{0,2},{1,3},{2,0},{3,1},{4,6},{5,7},{6,4},{7,5},{8,10},{9,11},{10,... | collective-permute-start | bytes 3080 | tf_op jit(solution)/shard_map/ppermute | solution.py:18
  71.7 0.0 collective-permute-done.7
  71.7 0.0 collective-permute-done.8
  71.7 1.5 %collective-permute-done.6 = f32[1,256]{1,0:T(1,128)S(1)} collective-permute-done((f32[1,256]{1,0:T(1,128)S(1)}, f32[1,256]{1,0:T(1,128)S(1)}, u32[]{:S(2)}, u32[]{:S(2)}) %collective-permute-start.6) | collective-permute-done | bytes 1056 | tf_op jit(solution)/shard_map/ppermute | solution.py:18
  73.2 0.6 fusion.1
  (4 shorter events, 0.1 us)
Async XLA Ops:
  0.0 11.9 %copy-start.2 = (s32[8]{0:T(128)S(1)}, s32[8]{0:T(128)}, u32[]{:S(2)}) copy-start(s32[8]{0:T(128)} %param.3) | copy-start | bytes 100
  2.8 9.3 %collective-permute-start = (bf16[256,4096]{1,0:T(8,128)(2,1)}, bf16[256,4096]{1,0:T(8,128)(2,1)S(1)}, u32[]{:S(2)}, u32[]{:S(2)}) collective-permute-start(bf16[256,4096]{1,0:T(8,128)(2,1)} %shard_map.28.own_hbm.refs_0_), channel_id=1, source_target_pairs={{0,1},{1,0},{2,3},{3,2},{4,5},{5,4},{6,7},{7,6},{8,9},{9,8},{10,11... | collective-permute-start | bytes 6291464 | tf_op jit(solution)/shard_map/ppermute | solution.py:18
  3.3 49.1 %collective-permute-start.1 = (bf16[256,4096]{1,0:T(8,128)(2,1)}, bf16[256,4096]{1,0:T(8,128)(2,1)}, u32[]{:S(2)}, u32[]{:S(2)}) collective-permute-start(bf16[256,4096]{1,0:T(8,128)(2,1)} %shard_map.28.own_hbm.refs_0_), channel_id=1, source_target_pairs={{0,2},{1,3},{2,0},{3,1},{4,6},{5,7},{6,4},{7,5},{8,10},{9,11},{10,... | collective-permute-start | bytes 6291464 | tf_op jit(solution)/shard_map/ppermute | solution.py:18
  5.9 49.3 %collective-permute-start.3 = (bf16[256,4096]{1,0:T(8,128)(2,1)}, bf16[256,4096]{1,0:T(8,128)(2,1)}, u32[]{:S(2)}, u32[]{:S(2)}) collective-permute-start(bf16[256,4096]{1,0:T(8,128)(2,1)} %shard_map.28.own_hbm.refs_0_), channel_id=1, source_target_pairs={{0,4},{2,6},{4,8},{6,10},{8,12},{9,1},{10,14},{11,3},{12,16},{13,5... | collective-permute-start | bytes 6291464 | tf_op jit(solution)/shard_map/ppermute | solution.py:23
  10.6 45.2 %collective-permute-start.4 = (bf16[256,4096]{1,0:T(8,128)(2,1)}, bf16[256,4096]{1,0:T(8,128)(2,1)}, u32[]{:S(2)}, u32[]{:S(2)}) collective-permute-start(bf16[256,4096]{1,0:T(8,128)(2,1)} %shard_map.28.own_hbm.refs_0_), channel_id=1, source_target_pairs={{1,5},{3,7},{5,9},{7,11},{8,0},{9,13},{10,2},{11,15},{12,4},{13,17... | collective-permute-start | bytes 6291464 | tf_op jit(solution)/shard_map/ppermute | solution.py:23
  12.1 1.6 %copy-start = (bf16[256,4096]{1,0:T(8,128)(2,1)S(1)}, bf16[256,4096]{1,0:T(8,128)(2,1)}, u32[]{:S(2)}) copy-start(bf16[256,4096]{1,0:T(8,128)(2,1)} %shard_map.28.own_hbm.refs_0_) | copy-start | bytes 6291460
  13.7 43.1 %copy-start.1 = (bf16[256,4096]{1,0:T(8,128)(2,1)S(1)}, bf16[256,4096]{1,0:T(8,128)(2,1)}, u32[]{:S(2)}) copy-start(bf16[256,4096]{1,0:T(8,128)(2,1)} %shard_map.28.own_hbm.refs_0_) | copy-start | bytes 6291460
  52.4 4.4 %collective-permute-start.2 = (bf16[256,4096]{1,0:T(8,128)(2,1)}, bf16[256,4096]{1,0:T(8,128)(2,1)S(1)}, u32[]{:S(2)}, u32[]{:S(2)}) collective-permute-start(bf16[256,4096]{1,0:T(8,128)(2,1)} %collective-permute-done.1.refs_2_), channel_id=1, source_target_pairs={{0,1},{1,0},{2,3},{3,2},{4,5},{5,4},{6,7},{7,6},{8,9},{9,8},{10,11... | collective-permute-start | bytes 6291464 | tf_op jit(solution)/shard_map/ppermute | solution.py:18
  62.2 6.7 %collective-permute-start.5 = (f32[2,256]{1,0:T(2,128)S(1)}, f32[2,256]{1,0:T(2,128)S(1)}, u32[]{:S(2)}, u32[]{:S(2)}) collective-permute-start(f32[2,256]{1,0:T(2,128)S(1)} %slice.13), channel_id=1, source_target_pairs={{0,1},{1,0},{2,3},{3,2},{4,5},{5,4},{6,7},{7,6},{8,9},{9,8},{10,11... | collective-permute-start | bytes 6152 | tf_op jit(solution)/shard_map/ppermute | solution.py:18
  62.4 9.3 %collective-permute-start.7 = (f32[1,256]{1,0:T(1,128)S(1)}, f32[1,256]{1,0:T(1,128)S(1)}, u32[]{:S(2)}, u32[]{:S(2)}) collective-permute-start(f32[1,256]{1,0:T(1,128)S(1)} %get-tuple-element.15), channel_id=1, source_target_pairs={{1,9},{3,11},{4,0},{5,13},{6,2},{7,15},{8,4},{9,17},{10,6},{11,19}... | collective-permute-start | bytes 3080 | tf_op jit(solution)/shard_map/ppermute | solution.py:23
  63.7 8.0 %collective-permute-start.8 = (f32[1,256]{1,0:T(1,128)S(1)}, f32[1,256]{1,0:T(1,128)S(1)}, u32[]{:S(2)}, u32[]{:S(2)}) collective-permute-start(f32[1,256]{1,0:T(1,128)S(1)} %get-tuple-element.16), channel_id=1, source_target_pairs={{0,8},{2,10},{4,12},{5,1},{6,14},{7,3},{8,16},{9,5},{10,18},{11,7}... | collective-permute-start | bytes 3080 | tf_op jit(solution)/shard_map/ppermute | solution.py:23
  68.9 4.3 %collective-permute-start.6 = (f32[1,256]{1,0:T(1,128)S(1)}, f32[1,256]{1,0:T(1,128)S(1)}, u32[]{:S(2)}, u32[]{:S(2)}) collective-permute-start(f32[1,256]{1,0:T(1,128)S(1)} %slice.17), channel_id=1, source_target_pairs={{0,2},{1,3},{2,0},{3,1},{4,6},{5,7},{6,4},{7,5},{8,10},{9,11},{10,... | collective-permute-start | bytes 3080 | tf_op jit(solution)/shard_map/ppermute | solution.py:18

commit v4 on v3

v4 whole, which is shorter than its diff:
```python
import functools

import jax
import jax.numpy as jnp
from jax import lax
from jax.experimental import pallas as pl
from jax.experimental.pallas import tpu as pltpu
from jax.sharding import PartitionSpec as P

AXES = ("row", "col")
QUAD = 4
STRIP = 16
FILLER = -2.0
IN_QUAD = ("own", "near", "across", "across_near")
NT = (((1,), (1,)), ((), ()))


def swapped(x, devices, bit):
    return lax.ppermute(x, AXES, [(i, i ^ bit) for i in range(devices)])


def shifted(x, devices, even, odd):
    moves = [(i, i + (odd if i % 2 else even)) for i in range(devices)]
    return lax.ppermute(x, AXES, [(i, j) for i, j in moves if 0 <= j < devices])


def labels_of(bounds_ref, block, length, axis):
    shape = (length, 1) if axis == 0 else (1, length)
    positions = block * length + lax.broadcasted_iota(jnp.int32, shape, axis)
    labels = jnp.where(positions < 0, -1, 0)
    for c in range(bounds_ref.shape[0]):
        labels = labels + (bounds_ref[c] <= positions).astype(jnp.int32)
    return labels


def label_at(bounds_ref, row):
    label = jnp.where(row < 0, -1, 0)
    for c in range(bounds_ref.shape[0]):
        label = label + jnp.where(bounds_ref[c] <= row, 1, 0)
    return label


def touch(bounds_ref, one, other, length):
    lower, upper = jnp.minimum(one, other), jnp.maximum(one, other)
    return label_at(bounds_ref, (lower + 1) * length - 1) == label_at(bounds_ref, upper * length)


def masked_scores(left, right, left_labels, right_labels):
    scores = lax.dot_general(left[...], right[...], NT, preferred_element_type=jnp.float32)
    return jnp.where(left_labels == right_labels, scores, FILLER)


def folded(masked):
    result = masked[:, :128]
    for i in range(128, masked.shape[1], 128):
        result = jnp.maximum(result, masked[:, i:i + 128])
    return result


def over_rows(masked):
    return jnp.max(masked, axis=0, keepdims=True)


def normalize_kernel(raw_hbm, normed_hbm, raw, normed, in_sems, out_sems):
    pieces = in_sems.shape[0]
    length = raw.shape[0] // pieces
    incoming, outgoing = [], []
    for i in range(pieces):
        rows = pl.ds(i * length, length)
        incoming.append(pltpu.make_async_copy(raw_hbm.at[rows], raw.at[rows], in_sems.at[i]))
        outgoing.append(pltpu.make_async_copy(normed.at[rows], normed_hbm.at[rows], out_sems.at[i]))
    for copy in incoming:
        copy.start()
    for i in range(pieces):
        incoming[i].wait()
        for j in range(0, length, STRIP):
            rows = pl.ds(i * length + j, STRIP)
            widened = raw[rows, :].astype(jnp.float32)
            squares = jnp.sum(widened * widened, axis=1, keepdims=True) + 1e-06
            normed[rows, :] = (widened * lax.rsqrt(squares)).astype(jnp.bfloat16)
        outgoing[i].start()
    for copy in outgoing:
        copy.wait()


def products_kernel(names, pairs, starts, ends, bounds_ref, place_ref, *refs):
    sources, refs = refs[:len(names)], refs[len(names):]
    if not starts:
        entering, refs = refs[:3], refs[3:]
    (quad_out, first_out, second_out), held, refs = refs[:3], refs[3:3 + len(names)], refs[3 + len(names):]
    widest = dict(zip(("first", "second"), refs[:2] if ends else (first_out, second_out)))
    sems = refs[-1]
    length = held[0].shape[0]
    copies = [pltpu.make_async_copy(sources[i], held[i], sems.at[i]) for i in range(len(names))]
    for copy in copies:
        copy.start()
    for i, ref in enumerate((quad_out, widest["first"], widest["second"])):
        ref[...] = jnp.full_like(ref, FILLER) if starts else entering[i][...]
    place = place_ref[0]
    below, above = place - QUAD, place + 2 * QUAD
    even = place % 2 == 0
    blocks = {name: place ^ b for b, name in enumerate(IN_QUAD)}
    blocks["first"], blocks["second"] = jnp.where(even, below, above), jnp.where(even, above, below)
    landed = set()
    for left, right in pairs:
        for name in (left, right):
            if name not in landed:
                copies[names.index(name)].wait()
                landed.add(name)

        def multiply(left=left, right=right):
            left_labels = labels_of(bounds_ref, blocks[left], length, 0)
            right_labels = labels_of(bounds_ref, blocks[right], length, 1)
            scores = masked_scores(held[names.index(left)], held[names.index(right)], left_labels, right_labels)
            if left == right:
                rows = lax.broadcasted_iota(jnp.int32, scores.shape, 0)
                columns = lax.broadcasted_iota(jnp.int32, scores.shape, 1)
                scores = jnp.where(rows == columns, FILLER, scores)
            b = IN_QUAD.index(right)
            quad_out[b:b + 1, :] = jnp.maximum(quad_out[b:b + 1, :], over_rows(scores))
            if left in widest:
                widest[left][...] = jnp.maximum(widest[left][...], folded(scores))

        if left == right:
            multiply()
        else:
            pl.when(touch(bounds_ref, blocks[left], blocks[right], length))(multiply)
    if ends:
        first_out[...] = over_rows(widest["first"][...].T)
        second_out[...] = over_rows(widest["second"][...].T)


ANY = pl.BlockSpec(memory_space=pl.ANY)
VMEM = pl.BlockSpec(memory_space=pltpu.VMEM)
SMEM = pl.BlockSpec(memory_space=pltpu.SMEM)


def products(bounds, where, blocks, pairs, state=None, ends=False):
    names = tuple(blocks)
    length, width = blocks[names[0]].shape
    folds = jax.ShapeDtypeStruct((length, 128), jnp.float32)
    line = jax.ShapeDtypeStruct((1, length), jnp.float32)
    scratch = [pltpu.VMEM((length, width), jnp.bfloat16)] * len(names)
    if ends:
        scratch += [pltpu.VMEM((length, 128), jnp.float32)] * 2
    entering = () if state is None else state
    return pl.pallas_call(
        functools.partial(products_kernel, names, pairs, state is None, ends),
        out_shape=(jax.ShapeDtypeStruct((QUAD, length), jnp.float32),) + ((line, line) if ends else (folds, folds)),
        in_specs=[SMEM, SMEM] + [ANY] * len(names) + [VMEM] * len(entering),
        out_specs=(VMEM,) * 3,
        scratch_shapes=scratch + [pltpu.SemaphoreType.DMA((len(names),))],
        compiler_params=pltpu.CompilerParams(vmem_limit_bytes=24 << 20),
        cost_estimate=pl.CostEstimate(
            flops=2 * len(pairs) * length * length * width,
            bytes_accessed=2 * len(names) * length * width,
            transcendentals=0,
        ),
    )(bounds, where, *blocks.values(), *entering)


def local(devices, embeddings, cluster_sizes):
    length, width = embeddings.shape
    block = jax.ShapeDtypeStruct((length, width), jnp.bfloat16)
    place = lax.axis_index(AXES).astype(jnp.int32)
    bounds = jnp.cumsum(cluster_sizes).astype(jnp.int32)
    where = place.reshape(1)

    normed = pl.pallas_call(
        normalize_kernel,
        out_shape=block,
        in_specs=[ANY],
        out_specs=ANY,
        scratch_shapes=[pltpu.VMEM((length, width), jnp.bfloat16)] * 2 + [pltpu.SemaphoreType.DMA((4,))] * 2,
        compiler_params=pltpu.CompilerParams(vmem_limit_bytes=60 << 20),
        cost_estimate=pl.CostEstimate(flops=0, bytes_accessed=4 * length * width, transcendentals=0),
    )(embeddings)

    near = swapped(normed, devices, 1)
    across = swapped(normed, devices, 2)
    first = shifted(normed, devices, QUAD, -2 * QUAD)
    held = {"own": normed, "near": near}
    state = products(bounds, where, held, (("own", "own"), ("near", "own")))

    later, *state = lax.optimization_barrier((normed, *state))
    second = shifted(later, devices, -2 * QUAD, QUAD)
    held["first"] = first
    state = products(bounds, where, held, (("first", "own"), ("first", "near")), state)

    across, *state = lax.optimization_barrier((across, *state))
    across_near = swapped(across, devices, 1)
    held["across"], held["second"] = across, second
    pairs = (("across", "own"), ("first", "across"), ("second", "own"), ("second", "near"), ("second", "across"))
    state = products(bounds, where, held, pairs, state)

    held = {"across_near": across_near, "own": normed, "first": first, "second": second}
    pairs = tuple((name, "across_near") for name in ("first", "second"))
    pairs = (("across_near", "own"),) + pairs
    quad, first_best, second_best = products(bounds, where, held, pairs, state, True)

    swapped_chip = swapped(quad[1::2], devices, 1)
    first_back = shifted(first_best, devices, -QUAD, 2 * QUAD)
    second_back = shifted(second_best, devices, 2 * QUAD, -QUAD)
    own_chip = jnp.maximum(quad[0::2], swapped_chip)
    swapped_quad = swapped(own_chip[1:2], devices, 2)
    best = jnp.maximum(own_chip[0:1], swapped_quad)
    even = place % 2 == 0
    from_next, from_previous = place + QUAD < devices, place >= 2 * QUAD
    filler = jnp.float32(FILLER)
    best = jnp.maximum(best, jnp.where(jnp.where(even, from_next, from_previous), first_back, filler))
    best = jnp.maximum(best, jnp.where(jnp.where(even, from_previous, from_next), second_back, filler))
    return best.reshape(length)


def solution(mesh):
    devices = 1
    for axis in AXES:
        devices *= mesh.shape[axis]
    in_specs = (P(AXES, None), P())
    return jax.shard_map(functools.partial(local, devices), mesh=mesh, in_specs=in_specs, out_specs=P(AXES), check_vma=False)
```

time: 74.4 us -> 77 us (1.035); the launches traced: 73.8 us -> 77.4 us
  Pallas kernels: 11.5 us -> 17 us
  waiting for transfers between devices: 41.2 us -> 38.5 us
  starting transfers between devices: 18.6 us -> 21 us
  local copies, waits for them, and re-layouts: 1.66 us -> 0.06 us
    ppermute x5, waiting for transfers between devices: 37.9 us -> 6.65 us  [swapped(): return lax.ppermute(x, AXES, [(i, i ^ bit) for i in range(devices)])]
    ppermute x4, waiting for transfers between devices: 3.36 us -> 31.8 us  [shifted(): return lax.ppermute(x, AXES, [(i, j) for i, j in moves if 0 <= j < devices])]
    ppermute x4, starting transfers between devices: 12.5 us -> 18.1 us  [shifted(): return lax.ppermute(x, AXES, [(i, j) for i, j in moves if 0 <= j < devices])]
    pallas_call x2 -> x4, Pallas kernels: 8.73 us -> 14.2 us  [products(): pl.pallas_call(functools.partial(products_kernel, names, pairs, state is...]
    ppermute x5, starting transfers between devices: 6.06 us -> 2.94 us  [swapped(): return lax.ppermute(x, AXES, [(i, i ^ bit) for i in range(devices)])]
    unnamed x6 -> x2, local copies, waits for them, and re-layouts: 1.6 us -> 0.01 us
  transfers between devices with their start and end apart: 9 -> 9, of which waited for: 5 -> 5; matrix products, arithmetic and copies ran while one was open for 0% -> 0% of each run, Pallas kernels for 5% -> 14%
where the time goes in v4:
time: 77 us; the launch traced here: 77.4 us
  waiting for transfers between devices  38.5 us (50%)
  starting transfers between devices  21 us (27%)
  Pallas kernels  17 us (22%)
    ppermute x4, waiting for transfers between devices, shifted(): return lax.ppermute(x, AXES, [(i, j) for i, j in moves if 0 <= j < devices])  31.8 us
    ppermute x4, starting transfers between devices, shifted(): return lax.ppermute(x, AXES, [(i, j) for i, j in moves if 0 <= j < devices])  18.1 us
    pallas_call x4, Pallas kernels, products(): pl.pallas_call(functools.partial(products_kernel, names, pairs, state is...  14.2 us
    ppermute x5, waiting for transfers between devices, swapped(): return lax.ppermute(x, AXES, [(i, i ^ bit) for i in range(devices)])  6.65 us
    ppermute x5, starting transfers between devices, swapped(): return lax.ppermute(x, AXES, [(i, i ^ bit) for i in range(devices)])  2.94 us
    pallas_call x1, Pallas kernels, local(): pl.pallas_call(normalize_kernel, out_shape=block, in_specs=[ANY], out_spe...  2.76 us
  transfers between devices with their start and end apart: 9, of which 5 were waited for; matrix products, arithmetic and copies ran while one was open for 0% of the time, Pallas kernels for 14%

profile of v4, /device:TPU:0, one launch (start us, length us, event | category | flops | bytes accessed | tf_op | source)
XLA Modules:
  0.0 77.4 jit_solution(18332104102345959408)
XLA Ops:
  0.0 0.0 copy-start
  0.0 2.8 %shard_map.28.refs_0_.refs_1_ = bf16[256,4096]{1,0:T(8,128)(2,1)} custom-call(bf16[256,4096]{1,0:T(8,128)(2,1)} %raw_hbm.1), custom_call_target="tpu_custom_call" | custom-call | bytes 4194304 | tf_op jit(solution)/shard_map/pallas_call | solution.py:169
  2.8 0.5 collective-permute-start.1
  3.3 5.7 %collective-permute-start.2 = (bf16[256,4096]{1,0:T(8,128)(2,1)}, bf16[256,4096]{1,0:T(8,128)(2,1)}, u32[]{:S(2)}, u32[]{:S(2)}) collective-permute-start(bf16[256,4096]{1,0:T(8,128)(2,1)} %shard_map.28.refs_0_.refs_1_), channel_id=1, source_target_pairs={{0,4},{2,6},{4,8},{6,10},{8,12},{9,1},{10,14},{11,3},{12,16},{13,5... | collective-permute-start | bytes 6291464 | tf_op jit(solution)/shard_map/ppermute | solution.py:24
  9.0 1.5 %collective-permute-start = (bf16[256,4096]{1,0:T(8,128)(2,1)}, bf16[256,4096]{1,0:T(8,128)(2,1)}, u32[]{:S(2)}, u32[]{:S(2)}) collective-permute-start(bf16[256,4096]{1,0:T(8,128)(2,1)} %shard_map.28.refs_0_.refs_1_), channel_id=1, source_target_pairs={{0,2},{1,3},{2,0},{3,1},{4,6},{5,7},{6,4},{7,5},{8,10},{9,11},{10,... | collective-permute-start | bytes 6291464 | tf_op jit(solution)/shard_map/ppermute | solution.py:19
  10.5 0.0 copy-done
  10.5 0.2 reduce-window.9
  10.7 0.0 collective-permute-done.1.refs_1_
  10.7 3.7 %shard_map.29 = (f32[4,256]{1,0:T(4,128)S(1)}, f32[256,128]{1,0:T(8,128)S(1)}, f32[256,128]{1,0:T(8,128)S(1)}) custom-call(s32[8]{0:T(128)S(1)} %bitcast.4, s32[1]{0:T(128)} %bitcast.2.place_ref, bf16[256,4096]{1,0:T(8,128)(2,1)} %shard_map.28.refs_0_.refs_1_, bf16[256,4096]{1,0:T(8,128)(2,1)S(1)} %collective-permute-done.1.refs_1_), custom_call_target="tpu_custom_call" | custom-call | flops 1073741824 | bytes 4194304 | tf_op jit(solution)/shard_map/pallas_call | solution.py:147
  14.5 1.3 %collective-permute-start.4 = (bf16[256,4096]{1,0:T(8,128)(2,1)}, bf16[256,4096]{1,0:T(8,128)(2,1)S(1)}, u32[]{:S(2)}, u32[]{:S(2)}) collective-permute-start(bf16[256,4096]{1,0:T(8,128)(2,1)} %shard_map.28.refs_0_.refs_1_), channel_id=1, source_target_pairs={{1,5},{3,7},{5,9},{7,11},{8,0},{9,13},{10,2},{11,15},{12,4},{13,17... | collective-permute-start | bytes 6291464 | tf_op jit(solution)/shard_map/ppermute | solution.py:24
  15.8 30.9 %collective-permute-done.2.refs_2_ = bf16[256,4096]{1,0:T(8,128)(2,1)} collective-permute-done((bf16[256,4096]{1,0:T(8,128)(2,1)}, bf16[256,4096]{1,0:T(8,128)(2,1)}, u32[]{:S(2)}, u32[]{:S(2)}) %collective-permute-start.2) | collective-permute-done | bytes 2097184 | tf_op jit(solution)/shard_map/ppermute | solution.py:24
  46.7 2.8 %shard_map.30 = (f32[4,256]{1,0:T(4,128)S(1)}, f32[256,128]{1,0:T(8,128)S(1)}, f32[256,128]{1,0:T(8,128)S(1)}) custom-call(s32[8]{0:T(128)S(1)} %bitcast.5, s32[1]{0:T(128)} %bitcast.2.place_ref, bf16[256,4096]{1,0:T(8,128)(2,1)} %shard_map.28.refs_0_.refs_1_, bf16[256,4096]{1,0:T(8,128)(2,1)S(1)} %collective-permute-done.1.refs_1_, ...), custom_call_target="tpu_custom_call" | custom-call | flops 1073741824 | bytes 6291456 | tf_op jit(solution)/shard_map/pallas_call | solution.py:147
  49.5 4.3 %collective-permute-done.refs_3_ = bf16[256,4096]{1,0:T(8,128)(2,1)} collective-permute-done((bf16[256,4096]{1,0:T(8,128)(2,1)}, bf16[256,4096]{1,0:T(8,128)(2,1)}, u32[]{:S(2)}, u32[]{:S(2)}) %collective-permute-start) | collective-permute-done | bytes 2097184 | tf_op jit(solution)/shard_map/ppermute | solution.py:19
  53.8 0.0 collective-permute-start.3
  53.8 0.5 collective-permute-done.4.refs_4_.refs_3_
  54.3 4.4 %shard_map.31 = (f32[4,256]{1,0:T(4,128)S(1)}, f32[256,128]{1,0:T(8,128)S(1)}, f32[256,128]{1,0:T(8,128)S(1)}) custom-call(s32[8]{0:T(128)S(1)} %bitcast.6, s32[1]{0:T(128)} %bitcast.2.place_ref, bf16[256,4096]{1,0:T(8,128)(2,1)} %shard_map.28.refs_0_.refs_1_, bf16[256,4096]{1,0:T(8,128)(2,1)S(1)} %collective-permute-done.1.refs_1_, ...), custom_call_target="tpu_custom_call" | custom-call | flops 2684354560 | bytes 10485760 | tf_op jit(solution)/shard_map/pallas_call | solution.py:147
  58.6 0.0 collective-permute-done.3.refs_0_
  58.6 3.3 %shard_map.32 = (f32[4,256]{1,0:T(4,128)S(1)}, f32[1,256]{1,0:T(1,128)S(1)}, f32[1,256]{1,0:T(1,128)S(1)}) custom-call(s32[8]{0:T(128)S(1)} %bitcast.7, s32[1]{0:T(128)} %bitcast.2.place_ref, bf16[256,4096]{1,0:T(8,128)(2,1)S(1)} %collective-permute-done.3.refs_0_, bf16[256,4096]{1,0:T(8,128)(2,1)} %shard_map.28.refs_0_.refs_1_, ...), custom_call_target="tpu_custom_call" | custom-call | flops 1610612736 | bytes 8388608 | tf_op jit(solution)/shard_map/pallas_call | solution.py:147
  62.0 0.1 collective-permute-start.5
  62.1 1.3 %collective-permute-start.7 = (f32[1,256]{1,0:T(1,128)S(1)}, f32[1,256]{1,0:T(1,128)S(1)}, u32[]{:S(2)}, u32[]{:S(2)}) collective-permute-start(f32[1,256]{1,0:T(1,128)S(1)} %get-tuple-element.43), channel_id=1, source_target_pairs={{1,9},{3,11},{4,0},{5,13},{6,2},{7,15},{8,4},{9,17},{10,6},{11,19}... | collective-permute-start | bytes 3080 | tf_op jit(solution)/shard_map/ppermute | solution.py:24
  63.4 9.8 %collective-permute-start.8 = (f32[1,256]{1,0:T(1,128)S(1)}, f32[1,256]{1,0:T(1,128)S(1)}, u32[]{:S(2)}, u32[]{:S(2)}) collective-permute-start(f32[1,256]{1,0:T(1,128)S(1)} %get-tuple-element.44), channel_id=1, source_target_pairs={{0,8},{2,10},{4,12},{5,1},{6,14},{7,3},{8,16},{9,5},{10,18},{11,7}... | collective-permute-start | bytes 3080 | tf_op jit(solution)/shard_map/ppermute | solution.py:24
  73.1 0.0 collective-permute-done.5
  73.2 0.8 %collective-permute-start.6 = (f32[1,256]{1,0:T(1,128)S(1)}, f32[1,256]{1,0:T(1,128)S(1)}, u32[]{:S(2)}, u32[]{:S(2)}) collective-permute-start(f32[1,256]{1,0:T(1,128)S(1)} %slice.17), channel_id=1, source_target_pairs={{0,2},{1,3},{2,0},{3,1},{4,6},{5,7},{6,4},{7,5},{8,10},{9,11},{10,... | collective-permute-start | bytes 3080 | tf_op jit(solution)/shard_map/ppermute | solution.py:19
  74.0 0.0 collective-permute-done.7
  74.0 0.4 collective-permute-done.8
  74.4 2.4 %collective-permute-done.6 = f32[1,256]{1,0:T(1,128)S(1)} collective-permute-done((f32[1,256]{1,0:T(1,128)S(1)}, f32[1,256]{1,0:T(1,128)S(1)}, u32[]{:S(2)}, u32[]{:S(2)}) %collective-permute-start.6) | collective-permute-done | bytes 1056 | tf_op jit(solution)/shard_map/ppermute | solution.py:19
  76.8 0.6 fusion.1
  (4 shorter events, 0.1 us)
Async XLA Ops:
  0.0 10.5 %copy-start = (s32[8]{0:T(128)S(1)}, s32[8]{0:T(128)}, u32[]{:S(2)}) copy-start(s32[8]{0:T(128)} %param.3) | copy-start | bytes 100
  2.8 8.0 %collective-permute-start.1 = (bf16[256,4096]{1,0:T(8,128)(2,1)}, bf16[256,4096]{1,0:T(8,128)(2,1)S(1)}, u32[]{:S(2)}, u32[]{:S(2)}) collective-permute-start(bf16[256,4096]{1,0:T(8,128)(2,1)} %shard_map.28.refs_0_.refs_1_), channel_id=1, source_target_pairs={{0,1},{1,0},{2,3},{3,2},{4,5},{5,4},{6,7},{7,6},{8,9},{9,8},{10,11... | collective-permute-start | bytes 6291464 | tf_op jit(solution)/shard_map/ppermute | solution.py:19
  3.3 43.4 %collective-permute-start.2 = (bf16[256,4096]{1,0:T(8,128)(2,1)}, bf16[256,4096]{1,0:T(8,128)(2,1)}, u32[]{:S(2)}, u32[]{:S(2)}) collective-permute-start(bf16[256,4096]{1,0:T(8,128)(2,1)} %shard_map.28.refs_0_.refs_1_), channel_id=1, source_target_pairs={{0,4},{2,6},{4,8},{6,10},{8,12},{9,1},{10,14},{11,3},{12,16},{13,5... | collective-permute-start | bytes 6291464 | tf_op jit(solution)/shard_map/ppermute | solution.py:24
  9.0 44.8 %collective-permute-start = (bf16[256,4096]{1,0:T(8,128)(2,1)}, bf16[256,4096]{1,0:T(8,128)(2,1)}, u32[]{:S(2)}, u32[]{:S(2)}) collective-permute-start(bf16[256,4096]{1,0:T(8,128)(2,1)} %shard_map.28.refs_0_.refs_1_), channel_id=1, source_target_pairs={{0,2},{1,3},{2,0},{3,1},{4,6},{5,7},{6,4},{7,5},{8,10},{9,11},{10,... | collective-permute-start | bytes 6291464 | tf_op jit(solution)/shard_map/ppermute | solution.py:19
  14.5 39.8 %collective-permute-start.4 = (bf16[256,4096]{1,0:T(8,128)(2,1)}, bf16[256,4096]{1,0:T(8,128)(2,1)S(1)}, u32[]{:S(2)}, u32[]{:S(2)}) collective-permute-start(bf16[256,4096]{1,0:T(8,128)(2,1)} %shard_map.28.refs_0_.refs_1_), channel_id=1, source_target_pairs={{1,5},{3,7},{5,9},{7,11},{8,0},{9,13},{10,2},{11,15},{12,4},{13,17... | collective-permute-start | bytes 6291464 | tf_op jit(solution)/shard_map/ppermute | solution.py:24
  53.8 4.9 %collective-permute-start.3 = (bf16[256,4096]{1,0:T(8,128)(2,1)}, bf16[256,4096]{1,0:T(8,128)(2,1)S(1)}, u32[]{:S(2)}, u32[]{:S(2)}) collective-permute-start(bf16[256,4096]{1,0:T(8,128)(2,1)} %collective-permute-done.refs_3_), channel_id=1, source_target_pairs={{0,1},{1,0},{2,3},{3,2},{4,5},{5,4},{6,7},{7,6},{8,9},{9,8},{10,11... | collective-permute-start | bytes 6291464 | tf_op jit(solution)/shard_map/ppermute | solution.py:19
  62.0 11.2 %collective-permute-start.5 = (f32[2,256]{1,0:T(2,128)S(1)}, f32[2,256]{1,0:T(2,128)S(1)}, u32[]{:S(2)}, u32[]{:S(2)}) collective-permute-start(f32[2,256]{1,0:T(2,128)S(1)} %slice.13), channel_id=1, source_target_pairs={{0,1},{1,0},{2,3},{3,2},{4,5},{5,4},{6,7},{7,6},{8,9},{9,8},{10,11... | collective-permute-start | bytes 6152 | tf_op jit(solution)/shard_map/ppermute | solution.py:19
  62.1 11.9 %collective-permute-start.7 = (f32[1,256]{1,0:T(1,128)S(1)}, f32[1,256]{1,0:T(1,128)S(1)}, u32[]{:S(2)}, u32[]{:S(2)}) collective-permute-start(f32[1,256]{1,0:T(1,128)S(1)} %get-tuple-element.43), channel_id=1, source_target_pairs={{1,9},{3,11},{4,0},{5,13},{6,2},{7,15},{8,4},{9,17},{10,6},{11,19}... | collective-permute-start | bytes 3080 | tf_op jit(solution)/shard_map/ppermute | solution.py:24
  63.4 11.1 %collective-permute-start.8 = (f32[1,256]{1,0:T(1,128)S(1)}, f32[1,256]{1,0:T(1,128)S(1)}, u32[]{:S(2)}, u32[]{:S(2)}) collective-permute-start(f32[1,256]{1,0:T(1,128)S(1)} %get-tuple-element.44), channel_id=1, source_target_pairs={{0,8},{2,10},{4,12},{5,1},{6,14},{7,3},{8,16},{9,5},{10,18},{11,7}... | collective-permute-start | bytes 3080 | tf_op jit(solution)/shard_map/ppermute | solution.py:24
  73.2 3.6 %collective-permute-start.6 = (f32[1,256]{1,0:T(1,128)S(1)}, f32[1,256]{1,0:T(1,128)S(1)}, u32[]{:S(2)}, u32[]{:S(2)}) collective-permute-start(f32[1,256]{1,0:T(1,128)S(1)} %slice.17), channel_id=1, source_target_pairs={{0,2},{1,3},{2,0},{3,1},{4,6},{5,7},{6,4},{7,5},{8,10},{9,11},{10,... | collective-permute-start | bytes 3080 | tf_op jit(solution)/shard_map/ppermute | solution.py:19

commit v5 on v4

v5 whole, which is shorter than its diff:
```python
import functools

import jax
import jax.numpy as jnp
from jax import lax
from jax.experimental import pallas as pl
from jax.experimental.pallas import tpu as pltpu
from jax.sharding import PartitionSpec as P

AXES = ("row", "col")
QUAD = 4
STRIP = 16
FILLER = -2.0
IN_QUAD = ("own", "near", "across", "across_near")
NT = (((1,), (1,)), ((), ()))


def swapped(x, devices, bit):
    return lax.ppermute(x, AXES, [(i, i ^ bit) for i in range(devices)])


def shifted(x, devices, even, odd):
    moves = [(i, i + (odd if i % 2 else even)) for i in range(devices)]
    return lax.ppermute(x, AXES, [(i, j) for i, j in moves if 0 <= j < devices])


def labels_of(bounds_ref, block, length, axis):
    shape = (length, 1) if axis == 0 else (1, length)
    positions = block * length + lax.broadcasted_iota(jnp.int32, shape, axis)
    labels = jnp.where(positions < 0, -1, 0)
    for c in range(bounds_ref.shape[0]):
        labels = labels + (bounds_ref[c] <= positions).astype(jnp.int32)
    return labels


def label_at(bounds_ref, row):
    label = jnp.where(row < 0, -1, 0)
    for c in range(bounds_ref.shape[0]):
        label = label + jnp.where(bounds_ref[c] <= row, 1, 0)
    return label


def touch(bounds_ref, one, other, length):
    lower, upper = jnp.minimum(one, other), jnp.maximum(one, other)
    return label_at(bounds_ref, (lower + 1) * length - 1) == label_at(bounds_ref, upper * length)


def masked_scores(left, right, left_labels, right_labels):
    scores = lax.dot_general(left[...], right[...], NT, preferred_element_type=jnp.float32)
    return jnp.where(left_labels == right_labels, scores, FILLER)


def folded(masked):
    result = masked[:, :128]
    for i in range(128, masked.shape[1], 128):
        result = jnp.maximum(result, masked[:, i:i + 128])
    return result


def over_rows(masked):
    return jnp.max(masked, axis=0, keepdims=True)


def normalize(raw_ref, normed_ref, scales_ref):
    for i in range(0, raw_ref.shape[0], STRIP):
        rows = pl.ds(i, STRIP)
        widened = raw_ref[rows, :].astype(jnp.float32)
        scales = lax.rsqrt(jnp.sum(widened * widened, axis=1, keepdims=True) + 1e-06)
        normed_ref[rows, :] = (widened * scales).astype(jnp.bfloat16)
        scales_ref[rows, :] = jnp.broadcast_to(scales, (STRIP, scales_ref.shape[1]))


def rescale(raw_ref, normed_ref, scales_ref, line_ref):
    scales_ref[...] = jnp.broadcast_to(line_ref[...], scales_ref.shape[::-1]).T
    for i in range(0, raw_ref.shape[0], STRIP):
        rows = pl.ds(i, STRIP)
        normed_ref[rows, :] = (raw_ref[rows, :].astype(jnp.float32) * scales_ref[rows, :1]).astype(jnp.bfloat16)


def products_kernel(names, pairs, raw, scaled, starts, ends, bounds_ref, place_ref, *refs):
    take = iter(refs)
    sources = {name: next(take) for name in names}
    lines = {name: next(take) for name in scaled}
    entering = [] if starts else [next(take) for unused in range(3)]
    quad_out, first_out, second_out = (next(take) for unused in range(3))
    normed = {name: next(take) for name in raw}
    line_out = {name: next(take) for name in raw if name not in scaled}
    scales = next(take)
    widest = dict(zip(("first", "second"), take if ends else (first_out, second_out)))
    length = sources[names[0]].shape[0]
    for i, ref in enumerate((quad_out, widest["first"], widest["second"])):
        ref[...] = jnp.full_like(ref, FILLER) if starts else entering[i][...]
    for name in raw:
        if name in scaled:
            rescale(sources[name], normed[name], scales, lines[name])
        else:
            normalize(sources[name], normed[name], scales)
            line_out[name][...] = scales[...].T[:1]
        sources[name] = normed[name]
    place = place_ref[0]
    below, above = place - QUAD, place + 2 * QUAD
    even = place % 2 == 0
    blocks = {name: place ^ b for b, name in enumerate(IN_QUAD)}
    blocks["first"], blocks["second"] = jnp.where(even, below, above), jnp.where(even, above, below)
    for left, right in pairs:

        def multiply(left=left, right=right):
            left_labels = labels_of(bounds_ref, blocks[left], length, 0)
            right_labels = labels_of(bounds_ref, blocks[right], length, 1)
            scores = masked_scores(sources[left], sources[right], left_labels, right_labels)
            if left == right:
                rows = lax.broadcasted_iota(jnp.int32, scores.shape, 0)
                columns = lax.broadcasted_iota(jnp.int32, scores.shape, 1)
                scores = jnp.where(rows == columns, FILLER, scores)
            b = IN_QUAD.index(right)
            quad_out[b:b + 1, :] = jnp.maximum(quad_out[b:b + 1, :], over_rows(scores))
            if left in widest:
                widest[left][...] = jnp.maximum(widest[left][...], folded(scores))

        if left == right:
            multiply()
        else:
            pl.when(touch(bounds_ref, blocks[left], blocks[right], length))(multiply)
    if ends:
        first_out[...] = over_rows(widest["first"][...].T)
        second_out[...] = over_rows(widest["second"][...].T)


VMEM = pl.BlockSpec(memory_space=pltpu.VMEM)
SMEM = pl.BlockSpec(memory_space=pltpu.SMEM)


def products(bounds, where, blocks, pairs, raw, scaled, state=(), ends=False):
    names = tuple(blocks)
    length, width = blocks[names[0]].shape
    folds = jax.ShapeDtypeStruct((length, 128), jnp.float32)
    line = jax.ShapeDtypeStruct((1, length), jnp.float32)
    block = jax.ShapeDtypeStruct((length, width), jnp.bfloat16)
    unscaled = [name for name in raw if name not in scaled]
    out_shape = [jax.ShapeDtypeStruct((QUAD, length), jnp.float32)] + [line if ends else folds] * 2
    out_shape += [block] * len(raw) + [line] * len(unscaled)
    results = pl.pallas_call(
        functools.partial(products_kernel, names, pairs, raw, tuple(scaled), not state, ends),
        out_shape=out_shape,
        in_specs=[SMEM, SMEM] + [VMEM] * (len(names) + len(scaled) + len(state)),
        out_specs=[VMEM] * len(out_shape),
        scratch_shapes=[pltpu.VMEM((length, 128), jnp.float32)] * (3 if ends else 1),
        compiler_params=pltpu.CompilerParams(vmem_limit_bytes=24 << 20),
        cost_estimate=pl.CostEstimate(
            flops=2 * len(pairs) * length * length * width,
            bytes_accessed=2 * len(names) * length * width,
            transcendentals=0,
        ),
    )(bounds, where, *blocks.values(), *scaled.values(), *state)
    normed = dict(zip(raw, results[3:]))
    return results[:3], {**blocks, **normed}, results[3 + len(raw):]


def local(devices, embeddings, cluster_sizes):
    length = embeddings.shape[0]
    place = lax.axis_index(AXES).astype(jnp.int32)
    bounds = jnp.cumsum(cluster_sizes).astype(jnp.int32)
    where = place.reshape(1)

    near = swapped(embeddings, devices, 1)
    across = swapped(embeddings, devices, 2)
    first = shifted(embeddings, devices, QUAD, -2 * QUAD)
    held = {"own": embeddings, "near": near}
    pairs = (("own", "own"), ("near", "own"))
    state, held, (own_scales, near_scales) = products(bounds, where, held, pairs, ("own", "near"), {})

    later, own_scales = lax.optimization_barrier((embeddings, own_scales))
    second = shifted(later, devices, -2 * QUAD, QUAD)
    second_scales = shifted(own_scales, devices, -2 * QUAD, QUAD)
    across_scales = swapped(jnp.concatenate([own_scales, near_scales]), devices, 2)
    first, second_scales, across_scales = lax.optimization_barrier((first, second_scales, across_scales))

    pairs = (("first", "own"), ("first", "near"))
    state, held, unused = products(bounds, where, {**held, "first": first}, pairs, ("first",), {}, state)

    across, *state = lax.optimization_barrier((across, *state))
    across_near = swapped(across, devices, 1)
    held["across"], held["second"] = across, second
    pairs = (("across", "own"), ("first", "across"), ("second", "own"), ("second", "near"), ("second", "across"))
    scales = {"across": across_scales[:1], "second": second_scales}
    state, held, unused = products(bounds, where, held, pairs, ("across", "second"), scales, state)

    held = {name: held[name] for name in ("own", "first", "second")}
    held["across_near"] = across_near
    pairs = (("across_near", "own"), ("first", "across_near"), ("second", "across_near"))
    scales = {"across_near": across_scales[1:]}
    state, unused, unused = products(bounds, where, held, pairs, ("across_near",), scales, state, True)
    quad, first_best, second_best = state

    swapped_chip = swapped(quad[1::2], devices, 1)
    first_back = shifted(first_best, devices, -QUAD, 2 * QUAD)
    second_back = shifted(second_best, devices, 2 * QUAD, -QUAD)
    own_chip = jnp.maximum(quad[0::2], swapped_chip)
    swapped_quad = swapped(own_chip[1:2], devices, 2)
    best = jnp.maximum(own_chip[0:1], swapped_quad)
    even = place % 2 == 0
    from_next, from_previous = place + QUAD < devices, place >= 2 * QUAD
    filler = jnp.float32(FILLER)
    best = jnp.maximum(best, jnp.where(jnp.where(even, from_next, from_previous), first_back, filler))
    best = jnp.maximum(best, jnp.where(jnp.where(even, from_previous, from_next), second_back, filler))
    return best.reshape(length)


def solution(mesh):
    devices = 1
    for axis in AXES:
        devices *= mesh.shape[axis]
    in_specs = (P(AXES, None), P())
    return jax.shard_map(functools.partial(local, devices), mesh=mesh, in_specs=in_specs, out_specs=P(AXES), check_vma=False)
```

time: 77 us -> 77 us (level)
  Pallas kernels: 17 us -> 13.9 us
  waiting for transfers between devices: 38.5 us -> 39.9 us
    ppermute x4 -> x5, waiting for transfers between devices: 31.8 us -> 39.9 us  [shifted(): return lax.ppermute(x, AXES, [(i, j) for i, j in moves if 0 <= j < devices])]
    ppermute x5 -> x6, waiting for transfers between devices: 6.65 us -> 0.02 us  [swapped(): return lax.ppermute(x, AXES, [(i, i ^ bit) for i in range(devices)])]
    ppermute x5 -> x6, starting transfers between devices: 2.94 us -> 8.09 us  [swapped(): return lax.ppermute(x, AXES, [(i, i ^ bit) for i in range(devices)])]
    ppermute x4 -> x5, starting transfers between devices: 18.1 us -> 13.2 us  [shifted(): return lax.ppermute(x, AXES, [(i, j) for i, j in moves if 0 <= j < devices])]
    pallas_call x5 -> x4, Pallas kernels: 17 us -> 13.9 us  [products(): pl.pallas_call(functools.partial(products_kernel, names, pairs, raw, tupl...]
  transfers between devices with their start and end apart: 9 -> 11, of which waited for: 5 -> 3; matrix products, arithmetic and copies ran while one was open for 0% -> 1% of each run, Pallas kernels for 14% -> 15%
where the time goes in v5:
time: 77 us; the launch traced here: 76.6 us
  waiting for transfers between devices  39.9 us (52%)
  starting transfers between devices  21.3 us (28%)
  Pallas kernels  13.9 us (18%)
  other arithmetic  1.41 us (2%)
    ppermute x5, waiting for transfers between devices, shifted(): return lax.ppermute(x, AXES, [(i, j) for i, j in moves if 0 <= j < devices])  39.9 us
    pallas_call x4, Pallas kernels, products(): pl.pallas_call(functools.partial(products_kernel, names, pairs, raw, tupl...  13.9 us
    ppermute x5, starting transfers between devices, shifted(): return lax.ppermute(x, AXES, [(i, j) for i, j in moves if 0 <= j < devices])  13.2 us
    ppermute x6, starting transfers between devices, swapped(): return lax.ppermute(x, AXES, [(i, i ^ bit) for i in range(devices)])  8.09 us
  transfers between devices with their start and end apart: 11, of which 3 were waited for; matrix products, arithmetic and copies ran while one was open for 1% of the time, Pallas kernels for 15%

profile of v5, /device:TPU:0, one launch (start us, length us, event | category | flops | bytes accessed | tf_op | source)
XLA Modules:
  0.0 76.6 jit_solution(1678894350643426947)
XLA Ops:
  0.0 0.5 collective-permute-start
  0.5 4.5 %collective-permute-start.1 = (bf16[256,4096]{1,0:T(8,128)(2,1)}, bf16[256,4096]{1,0:T(8,128)(2,1)S(1)}, u32[]{:S(2)}, u32[]{:S(2)}) collective-permute-start(bf16[256,4096]{1,0:T(8,128)(2,1)} %refs_0_.1), channel_id=1, source_target_pairs={{0,4},{2,6},{4,8},{6,10},{8,12},{9,1},{10,14},{11,3},{12,16},{13,5... | collective-permute-start | bytes 6291464 | tf_op jit(solution)/shard_map/ppermute | solution.py:24
  5.0 1.6 %collective-permute-start.4 = (bf16[256,4096]{1,0:T(8,128)(2,1)}, bf16[256,4096]{1,0:T(8,128)(2,1)}, u32[]{:S(2)}, u32[]{:S(2)}) collective-permute-start(bf16[256,4096]{1,0:T(8,128)(2,1)} %refs_0_.1), channel_id=1, source_target_pairs={{0,2},{1,3},{2,0},{3,1},{4,6},{5,7},{6,4},{7,5},{8,10},{9,11},{10,... | collective-permute-start | bytes 6291464 | tf_op jit(solution)/shard_map/ppermute | solution.py:19
  6.6 0.8 %reduce-window.9 = s32[8,1]{0,1:T(1,128)S(1)} reduce-window(s32[8,1]{0,1:T(1,128)} %bitcast.8, s32[]{:T(128)} %constant.24.clone.1), window={size=8x1 pad=7_0x0_0}, to_apply=%region_0.0 | reduce-window | flops 56 | bytes 68 | tf_op jit(solution)/shard_map/reduce-window.4
  7.4 0.0 collective-permute-done.refs_1_
  7.4 5.0 %shard_map.28 = (f32[4,256]{1,0:T(4,128)S(1)}, f32[256,128]{1,0:T(8,128)S(1)}, f32[256,128]{1,0:T(8,128)S(1)}, bf16[256,4096]{1,0:T(8,128)(2,1)S(1)}, bf16[256,4...) custom-call(s32[8]{0:T(128)S(1)} %bitcast.4, s32[1]{0:T(128)} %bitcast.2.place_ref, ...), custom_call_target="tpu_custom_call" | custom-call | flops 1073741824 | bytes 4194304 | tf_op jit(solution)/shard_map/pallas_call | solution.py:142
  12.4 1.3 %collective-permute-start.5 = (bf16[256,4096]{1,0:T(8,128)(2,1)}, bf16[256,4096]{1,0:T(8,128)(2,1)S(1)}, u32[]{:S(2)}, u32[]{:S(2)}) collective-permute-start(bf16[256,4096]{1,0:T(8,128)(2,1)} %refs_0_.1), channel_id=1, source_target_pairs={{1,5},{3,7},{5,9},{7,11},{8,0},{9,13},{10,2},{11,15},{12,4},{13,17... | collective-permute-start | bytes 6291464 | tf_op jit(solution)/shard_map/ppermute | solution.py:24
  13.7 0.6 collective-permute-start.3
  14.3 1.3 %collective-permute-start.2 = (f32[1,256]{1,0:T(1,128)S(1)}, f32[1,256]{1,0:T(1,128)S(1)}, u32[]{:S(2)}, u32[]{:S(2)}) collective-permute-start(f32[1,256]{1,0:T(1,128)S(1)} %get-tuple-element.35), channel_id=1, source_target_pairs={{1,5},{3,7},{5,9},{7,11},{8,0},{9,13},{10,2},{11,15},{12,4},{13,17... | collective-permute-start | bytes 3080 | tf_op jit(solution)/shard_map/ppermute | solution.py:24
  15.6 26.9 %collective-permute-done.1.refs_2_ = bf16[256,4096]{1,0:T(8,128)(2,1)S(1)} collective-permute-done((bf16[256,4096]{1,0:T(8,128)(2,1)}, bf16[256,4096]{1,0:T(8,128)(2,1)S(1)}, u32[]{:S(2)}, u32[]{:S(2)}) %collective-permute-start.1) | collective-permute-done | bytes 2097184 | tf_op jit(solution)/shard_map/ppermute | solution.py:24
  42.4 9.1 %collective-permute-done.2.refs_6_ = f32[1,256]{1,0:T(1,128)S(1)} collective-permute-done((f32[1,256]{1,0:T(1,128)S(1)}, f32[1,256]{1,0:T(1,128)S(1)}, u32[]{:S(2)}, u32[]{:S(2)}) %collective-permute-start.2) | collective-permute-done | bytes 1056 | tf_op jit(solution)/shard_map/ppermute | solution.py:24
  51.5 0.0 collective-permute-done.3
  51.5 1.9 %shard_map.29 = (f32[4,256]{1,0:T(4,128)S(1)}, f32[256,128]{1,0:T(8,128)S(1)}, f32[256,128]{1,0:T(8,128)S(1)}, bf16[256,4096]{1,0:T(8,128)(2,1)S(1)}, f32[1,256]{1,0:T(1,128)}) custom-call(s32[8]{0:T(128)S(1)} %bitcast.5, s32[1]{0:T(128)} %bitcast.2.place_ref, bf16[256,4096]{1,0:T(8,128)(2,1)S(1)} %get-tuple-element.32.refs_0_, ...), custom_call_target="tpu_custom_call" | custom-call | flops 1073741824 | bytes 6291456 | tf_op jit(solution)/shard_map/pallas_call | solution.py:142
  53.3 0.0 collective-permute-done.4.refs_3_
  53.3 0.0 collective-permute-start.6
  53.3 0.0 collective-permute-done.5.refs_4_
  53.4 4.6 %shard_map.30 = (f32[4,256]{1,0:T(4,128)S(1)}, f32[256,128]{1,0:T(8,128)S(1)}, f32[256,128]{1,0:T(8,128)S(1)}, bf16[256,4096]{1,0:T(8,128)(2,1)}, bf16[256,4096]{1,0:T(8,128)(2,1)S(1)}) custom-call(s32[8]{0:T(128)S(1)} %bitcast.6, s32[1]{0:T(128)} %bitcast.2.place_ref, bf16[256,4096]{1,0:T(8,128)(2,1)S(1)} %get-tuple-element.32.refs_0_, ...), custom_call_target="tpu_custom_call" | custom-call | flops 2684354560 | bytes 10485760 | tf_op jit(solution)/shard_map/pallas_call | solution.py:142
  58.0 0.0 collective-permute-done.6.refs_3_
  58.0 2.4 %shard_map.31 = (f32[4,256]{1,0:T(4,128)S(1)}, f32[1,256]{1,0:T(1,128)S(1)}, f32[1,256]{1,0:T(1,128)S(1)}, bf16[256,4096]{1,0:T(8,128)(2,1)}) custom-call(s32[8]{0:T(128)S(1)} %bitcast.7, s32[1]{0:T(128)} %bitcast.2.place_ref, bf16[256,4096]{1,0:T(8,128)(2,1)S(1)} %get-tuple-element.32.refs_0_, bf16[256,4096]{1,0:T(8,128)(2,1)S(1)} %get-tuple-element.41.refs_2_.refs_1_, ...), custom_call_target="tpu_custom_call" | custom-call | flops 1610612736 | bytes 8388608 | tf_op jit(solution)/shard_map/pallas_call | solution.py:142
  60.4 0.8 %collective-permute-start.7 = (f32[2,256]{1,0:T(2,128)S(1)}, f32[2,256]{1,0:T(2,128)S(1)}, u32[]{:S(2)}, u32[]{:S(2)}) collective-permute-start(f32[2,256]{1,0:T(2,128)S(1)} %slice.21), channel_id=1, source_target_pairs={{0,1},{1,0},{2,3},{3,2},{4,5},{5,4},{6,7},{7,6},{8,9},{9,8},{10,11... | collective-permute-start | bytes 6152 | tf_op jit(solution)/shard_map/ppermute | solution.py:19
  61.3 4.8 %collective-permute-start.10 = (f32[1,256]{1,0:T(1,128)S(1)}, f32[1,256]{1,0:T(1,128)S(1)}, u32[]{:S(2)}, u32[]{:S(2)}) collective-permute-start(f32[1,256]{1,0:T(1,128)S(1)} %get-tuple-element.58), channel_id=1, source_target_pairs={{0,8},{2,10},{4,12},{5,1},{6,14},{7,3},{8,16},{9,5},{10,18},{11,7}... | collective-permute-start | bytes 3080 | tf_op jit(solution)/shard_map/ppermute | solution.py:24
  66.1 1.3 %collective-permute-start.9 = (f32[1,256]{1,0:T(1,128)S(1)}, f32[1,256]{1,0:T(1,128)S(1)}, u32[]{:S(2)}, u32[]{:S(2)}) collective-permute-start(f32[1,256]{1,0:T(1,128)S(1)} %get-tuple-element.57), channel_id=1, source_target_pairs={{1,9},{3,11},{4,0},{5,13},{6,2},{7,15},{8,4},{9,17},{10,6},{11,19}... | collective-permute-start | bytes 3080 | tf_op jit(solution)/shard_map/ppermute | solution.py:24
  67.4 0.0 collective-permute-done.7
  67.4 4.7 %collective-permute-start.8 = (f32[1,256]{1,0:T(1,128)S(1)}, f32[1,256]{1,0:T(1,128)S(1)}, u32[]{:S(2)}, u32[]{:S(2)}) collective-permute-start(f32[1,256]{1,0:T(1,128)S(1)} %slice.25), channel_id=1, source_target_pairs={{0,2},{1,3},{2,0},{3,1},{4,6},{5,7},{6,4},{7,5},{8,10},{9,11},{10,... | collective-permute-start | bytes 3080 | tf_op jit(solution)/shard_map/ppermute | solution.py:19
  72.1 0.0 collective-permute-done.10
  72.1 4.0 %collective-permute-done.9 = f32[1,256]{1,0:T(1,128)S(1)} collective-permute-done((f32[1,256]{1,0:T(1,128)S(1)}, f32[1,256]{1,0:T(1,128)S(1)}, u32[]{:S(2)}, u32[]{:S(2)}) %collective-permute-start.9) | collective-permute-done | bytes 1056 | tf_op jit(solution)/shard_map/ppermute | solution.py:24
  76.1 0.0 collective-permute-done.8
  76.1 0.6 fusion.1
  (6 shorter events, 0.1 us)
Async XLA Ops:
  0.0 7.4 %collective-permute-start = (bf16[256,4096]{1,0:T(8,128)(2,1)}, bf16[256,4096]{1,0:T(8,128)(2,1)}, u32[]{:S(2)}, u32[]{:S(2)}) collective-permute-start(bf16[256,4096]{1,0:T(8,128)(2,1)} %refs_0_.1), channel_id=1, source_target_pairs={{0,1},{1,0},{2,3},{3,2},{4,5},{5,4},{6,7},{7,6},{8,9},{9,8},{10,11... | collective-permute-start | bytes 6291464 | tf_op jit(solution)/shard_map/ppermute | solution.py:19
  0.5 42.0 %collective-permute-start.1 = (bf16[256,4096]{1,0:T(8,128)(2,1)}, bf16[256,4096]{1,0:T(8,128)(2,1)S(1)}, u32[]{:S(2)}, u32[]{:S(2)}) collective-permute-start(bf16[256,4096]{1,0:T(8,128)(2,1)} %refs_0_.1), channel_id=1, source_target_pairs={{0,4},{2,6},{4,8},{6,10},{8,12},{9,1},{10,14},{11,3},{12,16},{13,5... | collective-permute-start | bytes 6291464 | tf_op jit(solution)/shard_map/ppermute | solution.py:24
  5.0 48.4 %collective-permute-start.4 = (bf16[256,4096]{1,0:T(8,128)(2,1)}, bf16[256,4096]{1,0:T(8,128)(2,1)}, u32[]{:S(2)}, u32[]{:S(2)}) collective-permute-start(bf16[256,4096]{1,0:T(8,128)(2,1)} %refs_0_.1), channel_id=1, source_target_pairs={{0,2},{1,3},{2,0},{3,1},{4,6},{5,7},{6,4},{7,5},{8,10},{9,11},{10,... | collective-permute-start | bytes 6291464 | tf_op jit(solution)/shard_map/ppermute | solution.py:19
  12.4 41.0 %collective-permute-start.5 = (bf16[256,4096]{1,0:T(8,128)(2,1)}, bf16[256,4096]{1,0:T(8,128)(2,1)S(1)}, u32[]{:S(2)}, u32[]{:S(2)}) collective-permute-start(bf16[256,4096]{1,0:T(8,128)(2,1)} %refs_0_.1), channel_id=1, source_target_pairs={{1,5},{3,7},{5,9},{7,11},{8,0},{9,13},{10,2},{11,15},{12,4},{13,17... | collective-permute-start | bytes 6291464 | tf_op jit(solution)/shard_map/ppermute | solution.py:24
  13.7 37.8 %collective-permute-start.3 = (f32[2,256]{1,0:T(2,128)S(1)}, f32[2,256]{1,0:T(2,128)S(1)}, u32[]{:S(2)}, u32[]{:S(2)}) collective-permute-start(f32[2,256]{1,0:T(2,128)S(1)} %pad_maximum_fusion), channel_id=1, source_target_pairs={{0,2},{1,3},{2,0},{3,1},{4,6},{5,7},{6,4},{7,5},{8,10},{9,11},{10,... | collective-permute-start | bytes 6152 | tf_op jit(solution)/shard_map/ppermute | solution.py:19
  14.3 37.2 %collective-permute-start.2 = (f32[1,256]{1,0:T(1,128)S(1)}, f32[1,256]{1,0:T(1,128)S(1)}, u32[]{:S(2)}, u32[]{:S(2)}) collective-permute-start(f32[1,256]{1,0:T(1,128)S(1)} %get-tuple-element.35), channel_id=1, source_target_pairs={{1,5},{3,7},{5,9},{7,11},{8,0},{9,13},{10,2},{11,15},{12,4},{13,17... | collective-permute-start | bytes 3080 | tf_op jit(solution)/shard_map/ppermute | solution.py:24
  53.3 4.7 %collective-permute-start.6 = (bf16[256,4096]{1,0:T(8,128)(2,1)}, bf16[256,4096]{1,0:T(8,128)(2,1)S(1)}, u32[]{:S(2)}, u32[]{:S(2)}) collective-permute-start(bf16[256,4096]{1,0:T(8,128)(2,1)} %collective-permute-done.4.refs_3_), channel_id=1, source_target_pairs={{0,1},{1,0},{2,3},{3,2},{4,5},{5,4},{6,7},{7,6},{8,9},{9,8},{10,11... | collective-permute-start | bytes 6291464 | tf_op jit(solution)/shard_map/ppermute | solution.py:19
  60.4 7.0 %collective-permute-start.7 = (f32[2,256]{1,0:T(2,128)S(1)}, f32[2,256]{1,0:T(2,128)S(1)}, u32[]{:S(2)}, u32[]{:S(2)}) collective-permute-start(f32[2,256]{1,0:T(2,128)S(1)} %slice.21), channel_id=1, source_target_pairs={{0,1},{1,0},{2,3},{3,2},{4,5},{5,4},{6,7},{7,6},{8,9},{9,8},{10,11... | collective-permute-start | bytes 6152 | tf_op jit(solution)/shard_map/ppermute | solution.py:19
  61.3 10.8 %collective-permute-start.10 = (f32[1,256]{1,0:T(1,128)S(1)}, f32[1,256]{1,0:T(1,128)S(1)}, u32[]{:S(2)}, u32[]{:S(2)}) collective-permute-start(f32[1,256]{1,0:T(1,128)S(1)} %get-tuple-element.58), channel_id=1, source_target_pairs={{0,8},{2,10},{4,12},{5,1},{6,14},{7,3},{8,16},{9,5},{10,18},{11,7}... | collective-permute-start | bytes 3080 | tf_op jit(solution)/shard_map/ppermute | solution.py:24
  66.1 10.0 %collective-permute-start.9 = (f32[1,256]{1,0:T(1,128)S(1)}, f32[1,256]{1,0:T(1,128)S(1)}, u32[]{:S(2)}, u32[]{:S(2)}) collective-permute-start(f32[1,256]{1,0:T(1,128)S(1)} %get-tuple-element.57), channel_id=1, source_target_pairs={{1,9},{3,11},{4,0},{5,13},{6,2},{7,15},{8,4},{9,17},{10,6},{11,19}... | collective-permute-start | bytes 3080 | tf_op jit(solution)/shard_map/ppermute | solution.py:24
  67.4 8.6 %collective-permute-start.8 = (f32[1,256]{1,0:T(1,128)S(1)}, f32[1,256]{1,0:T(1,128)S(1)}, u32[]{:S(2)}, u32[]{:S(2)}) collective-permute-start(f32[1,256]{1,0:T(1,128)S(1)} %slice.25), channel_id=1, source_target_pairs={{0,2},{1,3},{2,0},{3,1},{4,6},{5,7},{6,4},{7,5},{8,10},{9,11},{10,... | collective-permute-start | bytes 3080 | tf_op jit(solution)/shard_map/ppermute | solution.py:19

commit v6 on v4

--- a/solution.py
+++ b/solution.py
@@ -61,39 +61,31 @@
     return jnp.max(masked, axis=0, keepdims=True)
 
 
-def normalize_kernel(raw_hbm, normed_hbm, raw, normed, in_sems, out_sems):
-    pieces = in_sems.shape[0]
+def normalize_kernel(raw_hbm, normed, raw, sems):
+    pieces = sems.shape[0]
     length = raw.shape[0] // pieces
-    incoming, outgoing = [], []
+    copies = []
     for i in range(pieces):
         rows = pl.ds(i * length, length)
-        incoming.append(pltpu.make_async_copy(raw_hbm.at[rows], raw.at[rows], in_sems.at[i]))
-        outgoing.append(pltpu.make_async_copy(normed.at[rows], normed_hbm.at[rows], out_sems.at[i]))
-    for copy in incoming:
+        copies.append(pltpu.make_async_copy(raw_hbm.at[rows], raw.at[rows], sems.at[i]))
+    for copy in copies:
         copy.start()
     for i in range(pieces):
-        incoming[i].wait()
+        copies[i].wait()
         for j in range(0, length, STRIP):
             rows = pl.ds(i * length + j, STRIP)
             widened = raw[rows, :].astype(jnp.float32)
             squares = jnp.sum(widened * widened, axis=1, keepdims=True) + 1e-06
             normed[rows, :] = (widened * lax.rsqrt(squares)).astype(jnp.bfloat16)
-        outgoing[i].start()
-    for copy in outgoing:
-        copy.wait()
 
 
 def products_kernel(names, pairs, starts, ends, bounds_ref, place_ref, *refs):
     sources, refs = refs[:len(names)], refs[len(names):]
     if not starts:
         entering, refs = refs[:3], refs[3:]
-    (quad_out, first_out, second_out), held, refs = refs[:3], refs[3:3 + len(names)], refs[3 + len(names):]
-    widest = dict(zip(("first", "second"), refs[:2] if ends else (first_out, second_out)))
-    sems = refs[-1]
-    length = held[0].shape[0]
-    copies = [pltpu.make_async_copy(sources[i], held[i], sems.at[i]) for i in range(len(names))]
-    for copy in copies:
-        copy.start()
+    quad_out, first_out, second_out = refs[:3]
+    widest = dict(zip(("first", "second"), refs[3:] if ends else (first_out, second_out)))
+    length = sources[0].shape[0]
     for i, ref in enumerate((quad_out, widest["first"], widest["second"])):
         ref[...] = jnp.full_like(ref, FILLER) if starts else entering[i][...]
     place = place_ref[0]
@@ -101,17 +93,13 @@
     even = place % 2 == 0
     blocks = {name: place ^ b for b, name in enumerate(IN_QUAD)}
     blocks["first"], blocks["second"] = jnp.where(even, below, above), jnp.where(even, above, below)
-    landed = set()
+    left_labels = {name: labels_of(bounds_ref, blocks[name], length, 0) for name in {pair[0]: 0 for pair in pairs}}
+    right_labels = {name: labels_of(bounds_ref, blocks[name], length, 1) for name in {pair[1]: 0 for pair in pairs}}
     for left, right in pairs:
-        for name in (left, right):
-            if name not in landed:
-                copies[names.index(name)].wait()
-                landed.add(name)
 
         def multiply(left=left, right=right):
-            left_labels = labels_of(bounds_ref, blocks[left], length, 0)
-            right_labels = labels_of(bounds_ref, blocks[right], length, 1)
-            scores = masked_scores(held[names.index(left)], held[names.index(right)], left_labels, right_labels)
+            pair = sources[names.index(left)], sources[names.index(right)]
+            scores = masked_scores(*pair, left_labels[left], right_labels[right])
             if left == right:
                 rows = lax.broadcasted_iota(jnp.int32, scores.shape, 0)
                 columns = lax.broadcasted_iota(jnp.int32, scores.shape, 1)
@@ -130,7 +118,7 @@
         second_out[...] = over_rows(widest["second"][...].T)
 
 
-ANY = pl.BlockSpec(memory_space=pl.ANY)
+HBM = pl.BlockSpec(memory_space=pltpu.HBM)
 VMEM = pl.BlockSpec(memory_space=pltpu.VMEM)
 SMEM = pl.BlockSpec(memory_space=pltpu.SMEM)
 
@@ -140,16 +128,13 @@
     length, width = blocks[names[0]].shape
     folds = jax.ShapeDtypeStruct((length, 128), jnp.float32)
     line = jax.ShapeDtypeStruct((1, length), jnp.float32)
-    scratch = [pltpu.VMEM((length, width), jnp.bfloat16)] * len(names)
-    if ends:
-        scratch += [pltpu.VMEM((length, 128), jnp.float32)] * 2
     entering = () if state is None else state
     return pl.pallas_call(
         functools.partial(products_kernel, names, pairs, state is None, ends),
         out_shape=(jax.ShapeDtypeStruct((QUAD, length), jnp.float32),) + ((line, line) if ends else (folds, folds)),
-        in_specs=[SMEM, SMEM] + [ANY] * len(names) + [VMEM] * len(entering),
+        in_specs=[SMEM, SMEM] + [VMEM] * (len(names) + len(entering)),
         out_specs=(VMEM,) * 3,
-        scratch_shapes=scratch + [pltpu.SemaphoreType.DMA((len(names),))],
+        scratch_shapes=[pltpu.VMEM((length, 128), jnp.float32)] * (2 if ends else 0),
         compiler_params=pltpu.CompilerParams(vmem_limit_bytes=24 << 20),
         cost_estimate=pl.CostEstimate(
             flops=2 * len(pairs) * length * length * width,
@@ -161,18 +146,17 @@
 
 def local(devices, embeddings, cluster_sizes):
     length, width = embeddings.shape
-    block = jax.ShapeDtypeStruct((length, width), jnp.bfloat16)
     place = lax.axis_index(AXES).astype(jnp.int32)
     bounds = jnp.cumsum(cluster_sizes).astype(jnp.int32)
     where = place.reshape(1)
 
     normed = pl.pallas_call(
         normalize_kernel,
-        out_shape=block,
-        in_specs=[ANY],
-        out_specs=ANY,
-        scratch_shapes=[pltpu.VMEM((length, width), jnp.bfloat16)] * 2 + [pltpu.SemaphoreType.DMA((4,))] * 2,
-        compiler_params=pltpu.CompilerParams(vmem_limit_bytes=60 << 20),
+        out_shape=jax.ShapeDtypeStruct((length, width), jnp.bfloat16),
+        in_specs=[HBM],
+        out_specs=VMEM,
+        scratch_shapes=[pltpu.VMEM((length, width), jnp.bfloat16), pltpu.SemaphoreType.DMA((4,))],
+        compiler_params=pltpu.CompilerParams(vmem_limit_bytes=50 << 20),
         cost_estimate=pl.CostEstimate(flops=0, bytes_accessed=4 * length * width, transcendentals=0),
     )(embeddings)
 

time: 77 us -> 74.3 us (0.965); the launches traced: 77.4 us -> 73.9 us
  Pallas kernels: 17 us -> 14.7 us
    ppermute x4, starting transfers between devices: 18.1 us -> 15.7 us  [shifted(): return lax.ppermute(x, AXES, [(i, j) for i, j in moves if 0 <= j < devices])]
    ppermute x5, starting transfers between devices: 2.94 us -> 4.73 us  [swapped(): return lax.ppermute(x, AXES, [(i, i ^ bit) for i in range(devices)])]
    pallas_call x4, Pallas kernels: 14.2 us -> 12.7 us  [products(): pl.pallas_call(functools.partial(products_kernel, names, pairs, state is...]
    ppermute x5, waiting for transfers between devices: 6.65 us -> 5.75 us  [swapped(): return lax.ppermute(x, AXES, [(i, i ^ bit) for i in range(devices)])]
    pallas_call x1, Pallas kernels: 2.76 us -> 1.93 us  [local(): pl.pallas_call(normalize_kernel, out_shape=jax.ShapeDtypeStruct((length,...]
  transfers between devices with their start and end apart: 9 -> 9, of which waited for: 5 -> 4; matrix products, arithmetic and copies ran while one was open for 0% -> 0% of each run, Pallas kernels for 14% -> 13%
where the time goes in v6:
time: 74.3 us; the launch traced here: 73.9 us
  waiting for transfers between devices  37.9 us (51%)
  starting transfers between devices  20.4 us (27%)
  Pallas kernels  14.7 us (20%)
  other arithmetic  0.75 us (1%)
    ppermute x4, waiting for transfers between devices, shifted(): return lax.ppermute(x, AXES, [(i, j) for i, j in moves if 0 <= j < devices])  32.2 us
    ppermute x4, starting transfers between devices, shifted(): return lax.ppermute(x, AXES, [(i, j) for i, j in moves if 0 <= j < devices])  15.7 us
    pallas_call x4, Pallas kernels, products(): pl.pallas_call(functools.partial(products_kernel, names, pairs, state is...  12.7 us
    ppermute x5, waiting for transfers between devices, swapped(): return lax.ppermute(x, AXES, [(i, i ^ bit) for i in range(devices)])  5.75 us
    ppermute x5, starting transfers between devices, swapped(): return lax.ppermute(x, AXES, [(i, i ^ bit) for i in range(devices)])  4.73 us
    pallas_call x1, Pallas kernels, local(): pl.pallas_call(normalize_kernel, out_shape=jax.ShapeDtypeStruct((length,...  1.93 us
  transfers between devices with their start and end apart: 9, of which 4 were waited for; matrix products, arithmetic and copies ran while one was open for 0% of the time, Pallas kernels for 13%

profile of v6, /device:TPU:0, one launch (start us, length us, event | category | flops | bytes accessed | tf_op | source)
XLA Modules:
  0.0 73.9 jit_solution(13713063411461788012)
XLA Ops:
  0.0 0.0 copy-start
  0.0 1.9 %shard_map.28.refs_0_.refs_1_ = bf16[256,4096]{1,0:T(8,128)(2,1)S(1)} custom-call(bf16[256,4096]{1,0:T(8,128)(2,1)} %raw_hbm.1), custom_call_target="tpu_custom_call" | custom-call | bytes 4194304 | tf_op jit(solution)/shard_map/pallas_call | solution.py:153
  1.9 0.5 collective-permute-start.1
  2.5 5.7 %collective-permute-start.2 = (bf16[256,4096]{1,0:T(8,128)(2,1)S(1)}, bf16[256,4096]{1,0:T(8,128)(2,1)}, u32[]{:S(2)}, u32[]{:S(2)}) collective-permute-start(bf16[256,4096]{1,0:T(8,128)(2,1)S(1)} %shard_map.28.refs_0_.refs_1_), channel_id=1, source_target_pairs={{0,4},{2,6},{4,8},{6,10},{8,12},{9,1},{10,14},{11,3},{12,16},{13,5... | collective-permute-start | bytes 6291464 | tf_op jit(solution)/shard_map/ppermute | solution.py:24
  8.2 1.5 %collective-permute-start = (bf16[256,4096]{1,0:T(8,128)(2,1)S(1)}, bf16[256,4096]{1,0:T(8,128)(2,1)}, u32[]{:S(2)}, u32[]{:S(2)}) collective-permute-start(bf16[256,4096]{1,0:T(8,128)(2,1)S(1)} %shard_map.28.refs_0_.refs_1_), channel_id=1, source_target_pairs={{0,2},{1,3},{2,0},{3,1},{4,6},{5,7},{6,4},{7,5},{8,10},{9,11},{10,... | collective-permute-start | bytes 6291464 | tf_op jit(solution)/shard_map/ppermute | solution.py:19
  9.7 0.0 copy-done
  9.7 0.2 reduce-window.9
  9.9 0.0 collective-permute-done.1.refs_1_
  9.9 3.2 %shard_map.29 = (f32[4,256]{1,0:T(4,128)S(1)}, f32[256,128]{1,0:T(8,128)S(1)}, f32[256,128]{1,0:T(8,128)S(1)}) custom-call(s32[8]{0:T(128)S(1)} %bitcast.4, s32[1]{0:T(128)} %bitcast.2.place_ref, bf16[256,4096]{1,0:T(8,128)(2,1)S(1)} %shard_map.28.refs_0_.refs_1_, bf16[256,4096]{1,0:T(8,128)(2,1)} %collective-permute-done.1.refs_1_), custom_call_target="tpu_custom_call" | custom-call | flops 1073741824 | bytes 4194304 | tf_op jit(solution)/shard_map/pallas_call | solution.py:132
  13.2 1.3 %collective-permute-start.4 = (bf16[256,4096]{1,0:T(8,128)(2,1)S(1)}, bf16[256,4096]{1,0:T(8,128)(2,1)S(1)}, u32[]{:S(2)}, u32[]{:S(2)}) collective-permute-start(bf16[256,4096]{1,0:T(8,128)(2,1)S(1)} %shard_map.28.refs_0_.refs_1_), channel_id=1, source_target_pairs={{1,5},{3,7},{5,9},{7,11},{8,0},{9,13},{10,2},{11,15},{12,4},{13,17... | collective-permute-start | bytes 6291464 | tf_op jit(solution)/shard_map/ppermute | solution.py:24
  14.5 31.7 %collective-permute-done.2.refs_2_ = bf16[256,4096]{1,0:T(8,128)(2,1)} collective-permute-done((bf16[256,4096]{1,0:T(8,128)(2,1)S(1)}, bf16[256,4096]{1,0:T(8,128)(2,1)}, u32[]{:S(2)}, u32[]{:S(2)}) %collective-permute-start.2) | collective-permute-done | bytes 2097184 | tf_op jit(solution)/shard_map/ppermute | solution.py:24
  46.1 2.4 %shard_map.30 = (f32[4,256]{1,0:T(4,128)S(1)}, f32[256,128]{1,0:T(8,128)S(1)}, f32[256,128]{1,0:T(8,128)S(1)}) custom-call(s32[8]{0:T(128)S(1)} %bitcast.5, s32[1]{0:T(128)} %bitcast.2.place_ref, bf16[256,4096]{1,0:T(8,128)(2,1)S(1)} %shard_map.28.refs_0_.refs_1_, bf16[256,4096]{1,0:T(8,128)(2,1)} %collective-permute-done.1.refs_1_, ...), custom_call_target="tpu_custom_call" | custom-call | flops 1073741824 | bytes 6291456 | tf_op jit(solution)/shard_map/pallas_call | solution.py:132
  48.5 4.2 %collective-permute-done.refs_3_ = bf16[256,4096]{1,0:T(8,128)(2,1)} collective-permute-done((bf16[256,4096]{1,0:T(8,128)(2,1)S(1)}, bf16[256,4096]{1,0:T(8,128)(2,1)}, u32[]{:S(2)}, u32[]{:S(2)}) %collective-permute-start) | collective-permute-done | bytes 2097184 | tf_op jit(solution)/shard_map/ppermute | solution.py:19
  52.7 0.0 collective-permute-start.3
  52.7 0.5 collective-permute-done.4.refs_4_.refs_3_
  53.2 4.1 %shard_map.31 = (f32[4,256]{1,0:T(4,128)S(1)}, f32[256,128]{1,0:T(8,128)S(1)}, f32[256,128]{1,0:T(8,128)S(1)}) custom-call(s32[8]{0:T(128)S(1)} %bitcast.6, s32[1]{0:T(128)} %bitcast.2.place_ref, bf16[256,4096]{1,0:T(8,128)(2,1)S(1)} %shard_map.28.refs_0_.refs_1_, bf16[256,4096]{1,0:T(8,128)(2,1)} %collective-permute-done.1.refs_1_, ...), custom_call_target="tpu_custom_call" | custom-call | flops 2684354560 | bytes 10485760 | tf_op jit(solution)/shard_map/pallas_call | solution.py:132
  57.4 0.0 collective-permute-done.3.refs_0_
  57.4 2.9 %shard_map.32 = (f32[4,256]{1,0:T(4,128)S(1)}, f32[1,256]{1,0:T(1,128)S(1)}, f32[1,256]{1,0:T(1,128)S(1)}) custom-call(s32[8]{0:T(128)S(1)} %bitcast.7, s32[1]{0:T(128)} %bitcast.2.place_ref, bf16[256,4096]{1,0:T(8,128)(2,1)S(1)} %collective-permute-done.3.refs_0_, bf16[256,4096]{1,0:T(8,128)(2,1)S(1)} %shard_map.28.refs_0_.refs_1_, ...), custom_call_target="tpu_custom_call" | custom-call | flops 1610612736 | bytes 8388608 | tf_op jit(solution)/shard_map/pallas_call | solution.py:132
  60.4 0.1 collective-permute-start.5
  60.5 1.3 %collective-permute-start.7 = (f32[1,256]{1,0:T(1,128)S(1)}, f32[1,256]{1,0:T(1,128)S(1)}, u32[]{:S(2)}, u32[]{:S(2)}) collective-permute-start(f32[1,256]{1,0:T(1,128)S(1)} %get-tuple-element.43), channel_id=1, source_target_pairs={{1,9},{3,11},{4,0},{5,13},{6,2},{7,15},{8,4},{9,17},{10,6},{11,19}... | collective-permute-start | bytes 3080 | tf_op jit(solution)/shard_map/ppermute | solution.py:24
  61.7 7.4 %collective-permute-start.8 = (f32[1,256]{1,0:T(1,128)S(1)}, f32[1,256]{1,0:T(1,128)S(1)}, u32[]{:S(2)}, u32[]{:S(2)}) collective-permute-start(f32[1,256]{1,0:T(1,128)S(1)} %get-tuple-element.44), channel_id=1, source_target_pairs={{0,8},{2,10},{4,12},{5,1},{6,14},{7,3},{8,16},{9,5},{10,18},{11,7}... | collective-permute-start | bytes 3080 | tf_op jit(solution)/shard_map/ppermute | solution.py:24
  69.1 0.0 collective-permute-done.5
  69.2 2.6 %collective-permute-start.6 = (f32[1,256]{1,0:T(1,128)S(1)}, f32[1,256]{1,0:T(1,128)S(1)}, u32[]{:S(2)}, u32[]{:S(2)}) collective-permute-start(f32[1,256]{1,0:T(1,128)S(1)} %slice.17), channel_id=1, source_target_pairs={{0,2},{1,3},{2,0},{3,1},{4,6},{5,7},{6,4},{7,5},{8,10},{9,11},{10,... | collective-permute-start | bytes 3080 | tf_op jit(solution)/shard_map/ppermute | solution.py:19
  71.8 0.0 collective-permute-done.7
  71.8 0.0 collective-permute-done.8
  71.8 1.5 %collective-permute-done.6 = f32[1,256]{1,0:T(1,128)S(1)} collective-permute-done((f32[1,256]{1,0:T(1,128)S(1)}, f32[1,256]{1,0:T(1,128)S(1)}, u32[]{:S(2)}, u32[]{:S(2)}) %collective-permute-start.6) | collective-permute-done | bytes 1056 | tf_op jit(solution)/shard_map/ppermute | solution.py:19
  73.3 0.6 fusion.1
  (4 shorter events, 0.1 us)
Async XLA Ops:
  0.0 9.7 %copy-start = (s32[8]{0:T(128)S(1)}, s32[8]{0:T(128)}, u32[]{:S(2)}) copy-start(s32[8]{0:T(128)} %param.3) | copy-start | bytes 100
  1.9 8.0 %collective-permute-start.1 = (bf16[256,4096]{1,0:T(8,128)(2,1)S(1)}, bf16[256,4096]{1,0:T(8,128)(2,1)}, u32[]{:S(2)}, u32[]{:S(2)}) collective-permute-start(bf16[256,4096]{1,0:T(8,128)(2,1)S(1)} %shard_map.28.refs_0_.refs_1_), channel_id=1, source_target_pairs={{0,1},{1,0},{2,3},{3,2},{4,5},{5,4},{6,7},{7,6},{8,9},{9,8},{10,11... | collective-permute-start | bytes 6291464 | tf_op jit(solution)/shard_map/ppermute | solution.py:19
  2.5 43.7 %collective-permute-start.2 = (bf16[256,4096]{1,0:T(8,128)(2,1)S(1)}, bf16[256,4096]{1,0:T(8,128)(2,1)}, u32[]{:S(2)}, u32[]{:S(2)}) collective-permute-start(bf16[256,4096]{1,0:T(8,128)(2,1)S(1)} %shard_map.28.refs_0_.refs_1_), channel_id=1, source_target_pairs={{0,4},{2,6},{4,8},{6,10},{8,12},{9,1},{10,14},{11,3},{12,16},{13,5... | collective-permute-start | bytes 6291464 | tf_op jit(solution)/shard_map/ppermute | solution.py:24
  8.2 44.5 %collective-permute-start = (bf16[256,4096]{1,0:T(8,128)(2,1)S(1)}, bf16[256,4096]{1,0:T(8,128)(2,1)}, u32[]{:S(2)}, u32[]{:S(2)}) collective-permute-start(bf16[256,4096]{1,0:T(8,128)(2,1)S(1)} %shard_map.28.refs_0_.refs_1_), channel_id=1, source_target_pairs={{0,2},{1,3},{2,0},{3,1},{4,6},{5,7},{6,4},{7,5},{8,10},{9,11},{10,... | collective-permute-start | bytes 6291464 | tf_op jit(solution)/shard_map/ppermute | solution.py:19
  13.2 40.1 %collective-permute-start.4 = (bf16[256,4096]{1,0:T(8,128)(2,1)S(1)}, bf16[256,4096]{1,0:T(8,128)(2,1)S(1)}, u32[]{:S(2)}, u32[]{:S(2)}) collective-permute-start(bf16[256,4096]{1,0:T(8,128)(2,1)S(1)} %shard_map.28.refs_0_.refs_1_), channel_id=1, source_target_pairs={{1,5},{3,7},{5,9},{7,11},{8,0},{9,13},{10,2},{11,15},{12,4},{13,17... | collective-permute-start | bytes 6291464 | tf_op jit(solution)/shard_map/ppermute | solution.py:24
  52.7 4.6 %collective-permute-start.3 = (bf16[256,4096]{1,0:T(8,128)(2,1)}, bf16[256,4096]{1,0:T(8,128)(2,1)S(1)}, u32[]{:S(2)}, u32[]{:S(2)}) collective-permute-start(bf16[256,4096]{1,0:T(8,128)(2,1)} %collective-permute-done.refs_3_), channel_id=1, source_target_pairs={{0,1},{1,0},{2,3},{3,2},{4,5},{5,4},{6,7},{7,6},{8,9},{9,8},{10,11... | collective-permute-start | bytes 6291464 | tf_op jit(solution)/shard_map/ppermute | solution.py:19
  60.4 8.8 %collective-permute-start.5 = (f32[2,256]{1,0:T(2,128)S(1)}, f32[2,256]{1,0:T(2,128)S(1)}, u32[]{:S(2)}, u32[]{:S(2)}) collective-permute-start(f32[2,256]{1,0:T(2,128)S(1)} %slice.13), channel_id=1, source_target_pairs={{0,1},{1,0},{2,3},{3,2},{4,5},{5,4},{6,7},{7,6},{8,9},{9,8},{10,11... | collective-permute-start | bytes 6152 | tf_op jit(solution)/shard_map/ppermute | solution.py:19
  60.5 11.3 %collective-permute-start.7 = (f32[1,256]{1,0:T(1,128)S(1)}, f32[1,256]{1,0:T(1,128)S(1)}, u32[]{:S(2)}, u32[]{:S(2)}) collective-permute-start(f32[1,256]{1,0:T(1,128)S(1)} %get-tuple-element.43), channel_id=1, source_target_pairs={{1,9},{3,11},{4,0},{5,13},{6,2},{7,15},{8,4},{9,17},{10,6},{11,19}... | collective-permute-start | bytes 3080 | tf_op jit(solution)/shard_map/ppermute | solution.py:24
  61.7 10.1 %collective-permute-start.8 = (f32[1,256]{1,0:T(1,128)S(1)}, f32[1,256]{1,0:T(1,128)S(1)}, u32[]{:S(2)}, u32[]{:S(2)}) collective-permute-start(f32[1,256]{1,0:T(1,128)S(1)} %get-tuple-element.44), channel_id=1, source_target_pairs={{0,8},{2,10},{4,12},{5,1},{6,14},{7,3},{8,16},{9,5},{10,18},{11,7}... | collective-permute-start | bytes 3080 | tf_op jit(solution)/shard_map/ppermute | solution.py:24
  69.2 4.2 %collective-permute-start.6 = (f32[1,256]{1,0:T(1,128)S(1)}, f32[1,256]{1,0:T(1,128)S(1)}, u32[]{:S(2)}, u32[]{:S(2)}) collective-permute-start(f32[1,256]{1,0:T(1,128)S(1)} %slice.17), channel_id=1, source_target_pairs={{0,2},{1,3},{2,0},{3,1},{4,6},{5,7},{6,4},{7,5},{8,10},{9,11},{10,... | collective-permute-start | bytes 3080 | tf_op jit(solution)/shard_map/ppermute | solution.py:19

commit v7 on v6

--- a/solution.py
+++ b/solution.py
@@ -79,12 +79,12 @@
             normed[rows, :] = (widened * lax.rsqrt(squares)).astype(jnp.bfloat16)
 
 
-def products_kernel(names, pairs, starts, ends, bounds_ref, place_ref, *refs):
+def products_kernel(names, pairs, keep, starts, ends, bounds_ref, place_ref, *refs):
     sources, refs = refs[:len(names)], refs[len(names):]
     if not starts:
         entering, refs = refs[:3], refs[3:]
-    quad_out, first_out, second_out = refs[:3]
-    widest = dict(zip(("first", "second"), refs[3:] if ends else (first_out, second_out)))
+    (quad_out, first_out, second_out), kept, refs = refs[:3], refs[3:3 + len(keep)], refs[3 + len(keep):]
+    widest = dict(zip(("first", "second"), refs if ends else (first_out, second_out)))
     length = sources[0].shape[0]
     for i, ref in enumerate((quad_out, widest["first"], widest["second"])):
         ref[...] = jnp.full_like(ref, FILLER) if starts else entering[i][...]
@@ -113,6 +113,8 @@
             multiply()
         else:
             pl.when(touch(bounds_ref, blocks[left], blocks[right], length))(multiply)
+    for name, ref in zip(keep, kept):
+        ref[...] = sources[names.index(name)][...]
     if ends:
         first_out[...] = over_rows(widest["first"][...].T)
         second_out[...] = over_rows(widest["second"][...].T)
@@ -123,25 +125,27 @@
 SMEM = pl.BlockSpec(memory_space=pltpu.SMEM)
 
 
-def products(bounds, where, blocks, pairs, state=None, ends=False):
+def products(bounds, where, blocks, pairs, state=None, ends=False, keep=()):
     names = tuple(blocks)
     length, width = blocks[names[0]].shape
     folds = jax.ShapeDtypeStruct((length, 128), jnp.float32)
     line = jax.ShapeDtypeStruct((1, length), jnp.float32)
+    block = jax.ShapeDtypeStruct((length, width), jnp.bfloat16)
     entering = () if state is None else state
-    return pl.pallas_call(
-        functools.partial(products_kernel, names, pairs, state is None, ends),
-        out_shape=(jax.ShapeDtypeStruct((QUAD, length), jnp.float32),) + ((line, line) if ends else (folds, folds)),
+    results = pl.pallas_call(
+        functools.partial(products_kernel, names, pairs, keep, state is None, ends),
+        out_shape=(jax.ShapeDtypeStruct((QUAD, length), jnp.float32),) + ((line, line) if ends else (folds, folds)) + (block,) * len(keep),
         in_specs=[SMEM, SMEM] + [VMEM] * (len(names) + len(entering)),
-        out_specs=(VMEM,) * 3,
+        out_specs=(VMEM,) * (3 + len(keep)),
         scratch_shapes=[pltpu.VMEM((length, 128), jnp.float32)] * (2 if ends else 0),
         compiler_params=pltpu.CompilerParams(vmem_limit_bytes=24 << 20),
         cost_estimate=pl.CostEstimate(
-            flops=2 * len(pairs) * length * length * width,
-            bytes_accessed=2 * len(names) * length * width,
+            flops=0,
+            bytes_accessed=0,
             transcendentals=0,
         ),
     )(bounds, where, *blocks.values(), *entering)
+    return results[:3], {**blocks, **dict(zip(keep, results[3:]))}
 
 
 def local(devices, embeddings, cluster_sizes):
@@ -163,24 +167,26 @@
     near = swapped(normed, devices, 1)
     across = swapped(normed, devices, 2)
     first = shifted(normed, devices, QUAD, -2 * QUAD)
-    held = {"own": normed, "near": near}
-    state = products(bounds, where, held, (("own", "own"), ("near", "own")))
+    pairs = (("own", "own"), ("near", "own"))
+    state, held = products(bounds, where, {"own": normed, "near": near}, pairs, keep=("near",))
 
     later, *state = lax.optimization_barrier((normed, *state))
     second = shifted(later, devices, -2 * QUAD, QUAD)
-    held["first"] = first
-    state = products(bounds, where, held, (("first", "own"), ("first", "near")), state)
 
     across, *state = lax.optimization_barrier((across, *state))
     across_near = swapped(across, devices, 1)
-    held["across"], held["second"] = across, second
-    pairs = (("across", "own"), ("first", "across"), ("second", "own"), ("second", "near"), ("second", "across"))
-    state = products(bounds, where, held, pairs, state)
-
-    held = {"across_near": across_near, "own": normed, "first": first, "second": second}
-    pairs = tuple((name, "across_near") for name in ("first", "second"))
-    pairs = (("across_near", "own"),) + pairs
-    quad, first_best, second_best = products(bounds, where, held, pairs, state, True)
+    held["across"], held["first"] = across, first
+    pairs = (("across", "own"), ("first", "own"), ("first", "near"), ("first", "across"))
+    state, held = products(bounds, where, held, pairs, state, keep=("across", "first"))
+
+    held["second"] = second
+    pairs = (("second", "own"), ("second", "near"), ("second", "across"))
+    state, held = products(bounds, where, held, pairs, state)
+
+    held["across_near"] = across_near
+    del held["near"], held["across"]
+    pairs = (("across_near", "own"), ("first", "across_near"), ("second", "across_near"))
+    (quad, first_best, second_best), unused = products(bounds, where, held, pairs, state, ends=True)
 
     swapped_chip = swapped(quad[1::2], devices, 1)
     first_back = shifted(first_best, devices, -QUAD, 2 * QUAD)

time: 74.3 us -> 73.2 us (0.985)
  Pallas kernels: 14.7 us -> 11.6 us
  waiting for transfers between devices: 37.9 us -> 40.3 us
    ppermute x5, waiting for transfers between devices: 5.75 us -> 39.1 us  [swapped(): return lax.ppermute(x, AXES, [(i, i ^ bit) for i in range(devices)])]
    ppermute x4, waiting for transfers between devices: 32.2 us -> 1.15 us  [shifted(): return lax.ppermute(x, AXES, [(i, j) for i, j in moves if 0 <= j < devices])]
    pallas_call x4, Pallas kernels: 12.7 us -> 9.64 us  [products(): pl.pallas_call(functools.partial(products_kernel, names, pairs, keep, sta...]
    ppermute x4, starting transfers between devices: 15.7 us -> 16.7 us  [shifted(): return lax.ppermute(x, AXES, [(i, j) for i, j in moves if 0 <= j < devices])]
    ppermute x5, starting transfers between devices: 4.73 us -> 3.74 us  [swapped(): return lax.ppermute(x, AXES, [(i, i ^ bit) for i in range(devices)])]
  transfers between devices with their start and end apart: 9 -> 9, of which waited for: 4 -> 3; matrix products, arithmetic and copies ran while one was open for 0% -> 0% of each run, Pallas kernels for 13% -> 11%
where the time goes in v7:
time: 73.2 us; the launch traced here: 73.3 us
  waiting for transfers between devices  40.3 us (55%)
  starting transfers between devices  20.5 us (28%)
  Pallas kernels  11.6 us (16%)
  other arithmetic  0.75 us (1%)
    ppermute x5, waiting for transfers between devices, swapped(): return lax.ppermute(x, AXES, [(i, i ^ bit) for i in range(devices)])  39.1 us
    ppermute x4, starting transfers between devices, shifted(): return lax.ppermute(x, AXES, [(i, j) for i, j in moves if 0 <= j < devices])  16.7 us
    pallas_call x4, Pallas kernels, products(): pl.pallas_call(functools.partial(products_kernel, names, pairs, keep, sta...  9.64 us
    ppermute x5, starting transfers between devices, swapped(): return lax.ppermute(x, AXES, [(i, i ^ bit) for i in range(devices)])  3.74 us
    pallas_call x1, Pallas kernels, local(): pl.pallas_call(normalize_kernel, out_shape=jax.ShapeDtypeStruct((length,...  1.93 us
  transfers between devices with their start and end apart: 9, of which 3 were waited for; matrix products, arithmetic and copies ran while one was open for 0% of the time, Pallas kernels for 11%

profile of v7, /device:TPU:0, one launch (start us, length us, event | category | flops | bytes accessed | tf_op | source)
XLA Modules:
  0.0 73.3 jit_solution(9365403372144923814)
XLA Ops:
  0.0 0.0 copy-start
  0.0 1.9 %shard_map.28.refs_0_ = bf16[256,4096]{1,0:T(8,128)(2,1)S(1)} custom-call(bf16[256,4096]{1,0:T(8,128)(2,1)} %raw_hbm.1), custom_call_target="tpu_custom_call" | custom-call | bytes 4194304 | tf_op jit(solution)/shard_map/pallas_call | solution.py:157
  1.9 0.5 collective-permute-start
  2.5 2.6 %collective-permute-start.1 = (bf16[256,4096]{1,0:T(8,128)(2,1)S(1)}, bf16[256,4096]{1,0:T(8,128)(2,1)}, u32[]{:S(2)}, u32[]{:S(2)}) collective-permute-start(bf16[256,4096]{1,0:T(8,128)(2,1)S(1)} %shard_map.28.refs_0_), channel_id=1, source_target_pairs={{0,2},{1,3},{2,0},{3,1},{4,6},{5,7},{6,4},{7,5},{8,10},{9,11},{10,... | collective-permute-start | bytes 6291464 | tf_op jit(solution)/shard_map/ppermute | solution.py:19
  5.1 4.7 %collective-permute-start.2 = (bf16[256,4096]{1,0:T(8,128)(2,1)S(1)}, bf16[256,4096]{1,0:T(8,128)(2,1)}, u32[]{:S(2)}, u32[]{:S(2)}) collective-permute-start(bf16[256,4096]{1,0:T(8,128)(2,1)S(1)} %shard_map.28.refs_0_), channel_id=1, source_target_pairs={{0,4},{2,6},{4,8},{6,10},{8,12},{9,1},{10,14},{11,3},{12,16},{13,5... | collective-permute-start | bytes 6291464 | tf_op jit(solution)/shard_map/ppermute | solution.py:24
  9.8 0.0 copy-done
  9.8 0.2 reduce-window.9
  10.0 0.0 collective-permute-done.refs_1_
  10.0 3.4 %shard_map.29 = (f32[4,256]{1,0:T(4,128)S(1)}, f32[256,128]{1,0:T(8,128)S(1)}, f32[256,128]{1,0:T(8,128)S(1)}, bf16[256,4096]{1,0:T(8,128)(2,1)S(1)}) custom-call(s32[8]{0:T(128)S(1)} %bitcast.4, s32[1]{0:T(128)} %bitcast.2.place_ref, bf16[256,4096]{1,0:T(8,128)(2,1)S(1)} %shard_map.28.refs_0_, bf16[256,4096]{1,0:T(8,128)(2,1)} %collective-permute-done.refs_1_), custom_call_target="tpu_custom_call" | custom-call | tf_op jit(solution)/shard_map/pallas_call | solution.py:135
  13.3 1.3 %collective-permute-start.3 = (bf16[256,4096]{1,0:T(8,128)(2,1)S(1)}, bf16[256,4096]{1,0:T(8,128)(2,1)S(1)}, u32[]{:S(2)}, u32[]{:S(2)}) collective-permute-start(bf16[256,4096]{1,0:T(8,128)(2,1)S(1)} %shard_map.28.refs_0_), channel_id=1, source_target_pairs={{1,5},{3,7},{5,9},{7,11},{8,0},{9,13},{10,2},{11,15},{12,4},{13,17... | collective-permute-start | bytes 6291464 | tf_op jit(solution)/shard_map/ppermute | solution.py:24
  14.6 36.7 %collective-permute-done.1.refs_2_ = bf16[256,4096]{1,0:T(8,128)(2,1)} collective-permute-done((bf16[256,4096]{1,0:T(8,128)(2,1)S(1)}, bf16[256,4096]{1,0:T(8,128)(2,1)}, u32[]{:S(2)}, u32[]{:S(2)}) %collective-permute-start.1) | collective-permute-done | bytes 2097184 | tf_op jit(solution)/shard_map/ppermute | solution.py:19
  51.4 0.0 collective-permute-start.4
  51.4 0.0 collective-permute-done.2.refs_3_
  51.4 3.6 %shard_map.30 = (f32[4,256]{1,0:T(4,128)S(1)}, f32[256,128]{1,0:T(8,128)S(1)}, f32[256,128]{1,0:T(8,128)S(1)}, bf16[256,4096]{1,0:T(8,128)(2,1)S(1)}, bf16[256,4096]{1,0:T(8,128)(2,1)S(1)}) custom-call(s32[8]{0:T(128)S(1)} %bitcast.5, s32[1]{0:T(128)} %bitcast.2.place_ref, bf16[256,4096]{1,0:T(8,128)(2,1)S(1)} %shard_map.28.refs_0_, ...), custom_call_target="tpu_custom_call" | custom-call | tf_op jit(solution)/shard_map/pallas_call | solution.py:135
  55.0 0.0 collective-permute-done.3.refs_4_.refs_2_
  55.0 0.8 %shard_map.31 = (f32[4,256]{1,0:T(4,128)S(1)}, f32[256,128]{1,0:T(8,128)S(1)}, f32[256,128]{1,0:T(8,128)S(1)}) custom-call(s32[8]{0:T(128)S(1)} %bitcast.6, s32[1]{0:T(128)} %bitcast.2.place_ref, bf16[256,4096]{1,0:T(8,128)(2,1)S(1)} %shard_map.28.refs_0_, bf16[256,4096]{1,0:T(8,128)(2,1)S(1)} %get-tuple-element.28.refs_1_, ...), custom_call_target="tpu_custom_call" | custom-call | tf_op jit(solution)/shard_map/pallas_call | solution.py:135
  55.8 0.0 collective-permute-done.4.refs_3_
  55.8 1.9 %shard_map.32 = (f32[4,256]{1,0:T(4,128)S(1)}, f32[1,256]{1,0:T(1,128)S(1)}, f32[1,256]{1,0:T(1,128)S(1)}) custom-call(s32[8]{0:T(128)S(1)} %bitcast.7, s32[1]{0:T(128)} %bitcast.2.place_ref, bf16[256,4096]{1,0:T(8,128)(2,1)S(1)} %shard_map.28.refs_0_, bf16[256,4096]{1,0:T(8,128)(2,1)S(1)} %get-tuple-element.39.refs_3_.refs_1_, ...), custom_call_target="tpu_custom_call" | custom-call | tf_op jit(solution)/shard_map/pallas_call | solution.py:135
  57.7 0.6 collective-permute-start.5
  58.3 1.3 %collective-permute-start.7 = (f32[1,256]{1,0:T(1,128)S(1)}, f32[1,256]{1,0:T(1,128)S(1)}, u32[]{:S(2)}, u32[]{:S(2)}) collective-permute-start(f32[1,256]{1,0:T(1,128)S(1)} %get-tuple-element.49), channel_id=1, source_target_pairs={{1,9},{3,11},{4,0},{5,13},{6,2},{7,15},{8,4},{9,17},{10,6},{11,19}... | collective-permute-start | bytes 3080 | tf_op jit(solution)/shard_map/ppermute | solution.py:24
  59.6 9.4 %collective-permute-start.8 = (f32[1,256]{1,0:T(1,128)S(1)}, f32[1,256]{1,0:T(1,128)S(1)}, u32[]{:S(2)}, u32[]{:S(2)}) collective-permute-start(f32[1,256]{1,0:T(1,128)S(1)} %get-tuple-element.50), channel_id=1, source_target_pairs={{0,8},{2,10},{4,12},{5,1},{6,14},{7,3},{8,16},{9,5},{10,18},{11,7}... | collective-permute-start | bytes 3080 | tf_op jit(solution)/shard_map/ppermute | solution.py:24
  69.0 0.0 collective-permute-done.5
  69.1 0.1 collective-permute-start.6
  69.2 0.0 collective-permute-done.7
  69.2 1.1 %collective-permute-done.8 = f32[1,256]{1,0:T(1,128)S(1)} collective-permute-done((f32[1,256]{1,0:T(1,128)S(1)}, f32[1,256]{1,0:T(1,128)S(1)}, u32[]{:S(2)}, u32[]{:S(2)}) %collective-permute-start.8) | collective-permute-done | bytes 1056 | tf_op jit(solution)/shard_map/ppermute | solution.py:24
  70.3 2.4 %collective-permute-done.6 = f32[1,256]{1,0:T(1,128)S(1)} collective-permute-done((f32[1,256]{1,0:T(1,128)S(1)}, f32[1,256]{1,0:T(1,128)S(1)}, u32[]{:S(2)}, u32[]{:S(2)}) %collective-permute-start.6) | collective-permute-done | bytes 1056 | tf_op jit(solution)/shard_map/ppermute | solution.py:19
  72.7 0.6 fusion.1
  (4 shorter events, 0.1 us)
Async XLA Ops:
  0.0 9.8 %copy-start = (s32[8]{0:T(128)S(1)}, s32[8]{0:T(128)}, u32[]{:S(2)}) copy-start(s32[8]{0:T(128)} %param.3) | copy-start | bytes 100
  1.9 8.0 %collective-permute-start = (bf16[256,4096]{1,0:T(8,128)(2,1)S(1)}, bf16[256,4096]{1,0:T(8,128)(2,1)}, u32[]{:S(2)}, u32[]{:S(2)}) collective-permute-start(bf16[256,4096]{1,0:T(8,128)(2,1)S(1)} %shard_map.28.refs_0_), channel_id=1, source_target_pairs={{0,1},{1,0},{2,3},{3,2},{4,5},{5,4},{6,7},{7,6},{8,9},{9,8},{10,11... | collective-permute-start | bytes 6291464 | tf_op jit(solution)/shard_map/ppermute | solution.py:19
  2.5 48.9 %collective-permute-start.1 = (bf16[256,4096]{1,0:T(8,128)(2,1)S(1)}, bf16[256,4096]{1,0:T(8,128)(2,1)}, u32[]{:S(2)}, u32[]{:S(2)}) collective-permute-start(bf16[256,4096]{1,0:T(8,128)(2,1)S(1)} %shard_map.28.refs_0_), channel_id=1, source_target_pairs={{0,2},{1,3},{2,0},{3,1},{4,6},{5,7},{6,4},{7,5},{8,10},{9,11},{10,... | collective-permute-start | bytes 6291464 | tf_op jit(solution)/shard_map/ppermute | solution.py:19
  5.1 46.3 %collective-permute-start.2 = (bf16[256,4096]{1,0:T(8,128)(2,1)S(1)}, bf16[256,4096]{1,0:T(8,128)(2,1)}, u32[]{:S(2)}, u32[]{:S(2)}) collective-permute-start(bf16[256,4096]{1,0:T(8,128)(2,1)S(1)} %shard_map.28.refs_0_), channel_id=1, source_target_pairs={{0,4},{2,6},{4,8},{6,10},{8,12},{9,1},{10,14},{11,3},{12,16},{13,5... | collective-permute-start | bytes 6291464 | tf_op jit(solution)/shard_map/ppermute | solution.py:24
  13.3 41.7 %collective-permute-start.3 = (bf16[256,4096]{1,0:T(8,128)(2,1)S(1)}, bf16[256,4096]{1,0:T(8,128)(2,1)S(1)}, u32[]{:S(2)}, u32[]{:S(2)}) collective-permute-start(bf16[256,4096]{1,0:T(8,128)(2,1)S(1)} %shard_map.28.refs_0_), channel_id=1, source_target_pairs={{1,5},{3,7},{5,9},{7,11},{8,0},{9,13},{10,2},{11,15},{12,4},{13,17... | collective-permute-start | bytes 6291464 | tf_op jit(solution)/shard_map/ppermute | solution.py:24
  51.4 4.4 %collective-permute-start.4 = (bf16[256,4096]{1,0:T(8,128)(2,1)}, bf16[256,4096]{1,0:T(8,128)(2,1)S(1)}, u32[]{:S(2)}, u32[]{:S(2)}) collective-permute-start(bf16[256,4096]{1,0:T(8,128)(2,1)} %collective-permute-done.1.refs_2_), channel_id=1, source_target_pairs={{0,1},{1,0},{2,3},{3,2},{4,5},{5,4},{6,7},{7,6},{8,9},{9,8},{10,11... | collective-permute-start | bytes 6291464 | tf_op jit(solution)/shard_map/ppermute | solution.py:19
  57.7 11.3 %collective-permute-start.5 = (f32[2,256]{1,0:T(2,128)S(1)}, f32[2,256]{1,0:T(2,128)S(1)}, u32[]{:S(2)}, u32[]{:S(2)}) collective-permute-start(f32[2,256]{1,0:T(2,128)S(1)} %slice.13), channel_id=1, source_target_pairs={{0,1},{1,0},{2,3},{3,2},{4,5},{5,4},{6,7},{7,6},{8,9},{9,8},{10,11... | collective-permute-start | bytes 6152 | tf_op jit(solution)/shard_map/ppermute | solution.py:19
  58.3 10.9 %collective-permute-start.7 = (f32[1,256]{1,0:T(1,128)S(1)}, f32[1,256]{1,0:T(1,128)S(1)}, u32[]{:S(2)}, u32[]{:S(2)}) collective-permute-start(f32[1,256]{1,0:T(1,128)S(1)} %get-tuple-element.49), channel_id=1, source_target_pairs={{1,9},{3,11},{4,0},{5,13},{6,2},{7,15},{8,4},{9,17},{10,6},{11,19}... | collective-permute-start | bytes 3080 | tf_op jit(solution)/shard_map/ppermute | solution.py:24
  59.6 10.7 %collective-permute-start.8 = (f32[1,256]{1,0:T(1,128)S(1)}, f32[1,256]{1,0:T(1,128)S(1)}, u32[]{:S(2)}, u32[]{:S(2)}) collective-permute-start(f32[1,256]{1,0:T(1,128)S(1)} %get-tuple-element.50), channel_id=1, source_target_pairs={{0,8},{2,10},{4,12},{5,1},{6,14},{7,3},{8,16},{9,5},{10,18},{11,7}... | collective-permute-start | bytes 3080 | tf_op jit(solution)/shard_map/ppermute | solution.py:24
  69.1 3.6 %collective-permute-start.6 = (f32[1,256]{1,0:T(1,128)S(1)}, f32[1,256]{1,0:T(1,128)S(1)}, u32[]{:S(2)}, u32[]{:S(2)}) collective-permute-start(f32[1,256]{1,0:T(1,128)S(1)} %slice.17), channel_id=1, source_target_pairs={{0,2},{1,3},{2,0},{3,1},{4,6},{5,7},{6,4},{7,5},{8,10},{9,11},{10,... | collective-permute-start | bytes 3080 | tf_op jit(solution)/shard_map/ppermute | solution.py:19

commit v8 on v7

--- a/solution.py
+++ b/solution.py
@@ -188,17 +188,15 @@
     pairs = (("across_near", "own"), ("first", "across_near"), ("second", "across_near"))
     (quad, first_best, second_best), unused = products(bounds, where, held, pairs, state, ends=True)
 
-    swapped_chip = swapped(quad[1::2], devices, 1)
-    first_back = shifted(first_best, devices, -QUAD, 2 * QUAD)
-    second_back = shifted(second_best, devices, 2 * QUAD, -QUAD)
-    own_chip = jnp.maximum(quad[0::2], swapped_chip)
-    swapped_quad = swapped(own_chip[1:2], devices, 2)
-    best = jnp.maximum(own_chip[0:1], swapped_quad)
+    received = swapped(jnp.concatenate([quad[1::2], second_best]), devices, 1)
+    own_chip = jnp.maximum(quad[0::2], received[:2])
+    outside = shifted(jnp.concatenate([first_best, received[2:]]), devices, -QUAD, 2 * QUAD)
+    swapped_quad = swapped(own_chip[1:], devices, 2)
     even = place % 2 == 0
-    from_next, from_previous = place + QUAD < devices, place >= 2 * QUAD
-    filler = jnp.float32(FILLER)
-    best = jnp.maximum(best, jnp.where(jnp.where(even, from_next, from_previous), first_back, filler))
-    best = jnp.maximum(best, jnp.where(jnp.where(even, from_previous, from_next), second_back, filler))
+    landed = jnp.where(even, place + QUAD < devices, place >= 2 * QUAD)
+    outside = jnp.where(landed, outside, jnp.float32(FILLER))
+    swapped_outside = swapped(outside[1:], devices, 1)
+    best = jnp.maximum(jnp.maximum(own_chip[:1], swapped_quad), jnp.maximum(outside[:1], swapped_outside))
     return best.reshape(length)
 
 

time: 73.2 us -> 69.3 us (0.947)
  starting transfers between devices: 20.5 us -> 15.9 us
    ppermute x4 -> x3, starting transfers between devices: 16.7 us -> 7.3 us  [shifted(): return lax.ppermute(x, AXES, [(i, j) for i, j in moves if 0 <= j < devices])]
    ppermute x5 -> x6, starting transfers between devices: 3.74 us -> 8.6 us  [swapped(): return lax.ppermute(x, AXES, [(i, i ^ bit) for i in range(devices)])]
    ppermute x4 -> x3, waiting for transfers between devices: 1.15 us -> 2.33 us  [shifted(): return lax.ppermute(x, AXES, [(i, j) for i, j in moves if 0 <= j < devices])]
    ppermute x5 -> x6, waiting for transfers between devices: 39.1 us -> 38.4 us  [swapped(): return lax.ppermute(x, AXES, [(i, i ^ bit) for i in range(devices)])]
  transfers between devices with their start and end apart: 9 -> 9, of which waited for: 3 -> 4; matrix products, arithmetic and copies ran while one was open for 0% -> 0% of each run, Pallas kernels for 11% -> 11%
where the time goes in v8:
time: 69.3 us; the launch traced here: 69.1 us
  waiting for transfers between devices  40.7 us (59%)
  starting transfers between devices  15.9 us (23%)
  Pallas kernels  11.6 us (17%)
  other arithmetic  0.78 us (1%)
    ppermute x6, waiting for transfers between devices, swapped(): return lax.ppermute(x, AXES, [(i, i ^ bit) for i in range(devices)])  38.4 us
    pallas_call x4, Pallas kernels, products(): pl.pallas_call(functools.partial(products_kernel, names, pairs, keep, sta...  9.64 us
    ppermute x6, starting transfers between devices, swapped(): return lax.ppermute(x, AXES, [(i, i ^ bit) for i in range(devices)])  8.6 us
    ppermute x3, starting transfers between devices, shifted(): return lax.ppermute(x, AXES, [(i, j) for i, j in moves if 0 <= j < devices])  7.3 us
    ppermute x3, waiting for transfers between devices, shifted(): return lax.ppermute(x, AXES, [(i, j) for i, j in moves if 0 <= j < devices])  2.33 us
    pallas_call x1, Pallas kernels, local(): pl.pallas_call(normalize_kernel, out_shape=jax.ShapeDtypeStruct((length,...  1.93 us
  transfers between devices with their start and end apart: 9, of which 4 were waited for; matrix products, arithmetic and copies ran while one was open for 0% of the time, Pallas kernels for 11%

profile of v8, /device:TPU:0, one launch (start us, length us, event | category | flops | bytes accessed | tf_op | source)
XLA Modules:
  0.0 69.1 jit_solution(17497523379930923588)
XLA Ops:
  0.0 0.0 copy-start
  0.0 1.9 %shard_map.28.refs_0_ = bf16[256,4096]{1,0:T(8,128)(2,1)S(1)} custom-call(bf16[256,4096]{1,0:T(8,128)(2,1)} %raw_hbm.1), custom_call_target="tpu_custom_call" | custom-call | bytes 4194304 | tf_op jit(solution)/shard_map/pallas_call | solution.py:157
  1.9 0.5 collective-permute-start
  2.5 2.6 %collective-permute-start.1 = (bf16[256,4096]{1,0:T(8,128)(2,1)S(1)}, bf16[256,4096]{1,0:T(8,128)(2,1)}, u32[]{:S(2)}, u32[]{:S(2)}) collective-permute-start(bf16[256,4096]{1,0:T(8,128)(2,1)S(1)} %shard_map.28.refs_0_), channel_id=1, source_target_pairs={{0,2},{1,3},{2,0},{3,1},{4,6},{5,7},{6,4},{7,5},{8,10},{9,11},{10,... | collective-permute-start | bytes 6291464 | tf_op jit(solution)/shard_map/ppermute | solution.py:19
  5.1 4.7 %collective-permute-start.2 = (bf16[256,4096]{1,0:T(8,128)(2,1)S(1)}, bf16[256,4096]{1,0:T(8,128)(2,1)}, u32[]{:S(2)}, u32[]{:S(2)}) collective-permute-start(bf16[256,4096]{1,0:T(8,128)(2,1)S(1)} %shard_map.28.refs_0_), channel_id=1, source_target_pairs={{0,4},{2,6},{4,8},{6,10},{8,12},{9,1},{10,14},{11,3},{12,16},{13,5... | collective-permute-start | bytes 6291464 | tf_op jit(solution)/shard_map/ppermute | solution.py:24
  9.8 0.0 copy-done
  9.8 0.2 reduce-window.9
  10.0 0.0 collective-permute-done.refs_1_
  10.0 3.4 %shard_map.29 = (f32[4,256]{1,0:T(4,128)S(1)}, f32[256,128]{1,0:T(8,128)S(1)}, f32[256,128]{1,0:T(8,128)S(1)}, bf16[256,4096]{1,0:T(8,128)(2,1)S(1)}) custom-call(s32[8]{0:T(128)S(1)} %bitcast.4, s32[1]{0:T(128)} %bitcast.2.place_ref, bf16[256,4096]{1,0:T(8,128)(2,1)S(1)} %shard_map.28.refs_0_, bf16[256,4096]{1,0:T(8,128)(2,1)} %collective-permute-done.refs_1_), custom_call_target="tpu_custom_call" | custom-call | tf_op jit(solution)/shard_map/pallas_call | solution.py:135
  13.3 1.3 %collective-permute-start.3 = (bf16[256,4096]{1,0:T(8,128)(2,1)S(1)}, bf16[256,4096]{1,0:T(8,128)(2,1)S(1)}, u32[]{:S(2)}, u32[]{:S(2)}) collective-permute-start(bf16[256,4096]{1,0:T(8,128)(2,1)S(1)} %shard_map.28.refs_0_), channel_id=1, source_target_pairs={{1,5},{3,7},{5,9},{7,11},{8,0},{9,13},{10,2},{11,15},{12,4},{13,17... | collective-permute-start | bytes 6291464 | tf_op jit(solution)/shard_map/ppermute | solution.py:24
  14.6 36.7 %collective-permute-done.1.refs_2_ = bf16[256,4096]{1,0:T(8,128)(2,1)} collective-permute-done((bf16[256,4096]{1,0:T(8,128)(2,1)S(1)}, bf16[256,4096]{1,0:T(8,128)(2,1)}, u32[]{:S(2)}, u32[]{:S(2)}) %collective-permute-start.1) | collective-permute-done | bytes 2097184 | tf_op jit(solution)/shard_map/ppermute | solution.py:19
  51.4 0.0 collective-permute-start.4
  51.4 0.0 collective-permute-done.2.refs_3_
  51.4 3.6 %shard_map.30 = (f32[4,256]{1,0:T(4,128)S(1)}, f32[256,128]{1,0:T(8,128)S(1)}, f32[256,128]{1,0:T(8,128)S(1)}, bf16[256,4096]{1,0:T(8,128)(2,1)S(1)}, bf16[256,4096]{1,0:T(8,128)(2,1)S(1)}) custom-call(s32[8]{0:T(128)S(1)} %bitcast.5, s32[1]{0:T(128)} %bitcast.2.place_ref, bf16[256,4096]{1,0:T(8,128)(2,1)S(1)} %shard_map.28.refs_0_, ...), custom_call_target="tpu_custom_call" | custom-call | tf_op jit(solution)/shard_map/pallas_call | solution.py:135
  55.0 0.0 collective-permute-done.3.refs_4_.refs_2_
  55.0 0.8 %shard_map.31 = (f32[4,256]{1,0:T(4,128)S(1)}, f32[256,128]{1,0:T(8,128)S(1)}, f32[256,128]{1,0:T(8,128)S(1)}) custom-call(s32[8]{0:T(128)S(1)} %bitcast.6, s32[1]{0:T(128)} %bitcast.2.place_ref, bf16[256,4096]{1,0:T(8,128)(2,1)S(1)} %shard_map.28.refs_0_, bf16[256,4096]{1,0:T(8,128)(2,1)S(1)} %get-tuple-element.28.refs_1_, ...), custom_call_target="tpu_custom_call" | custom-call | tf_op jit(solution)/shard_map/pallas_call | solution.py:135
  55.8 0.0 collective-permute-done.4.refs_3_
  55.8 1.9 %shard_map.32 = (f32[4,256]{1,0:T(4,128)S(1)}, f32[1,256]{1,0:T(1,128)S(1)}, f32[1,256]{1,0:T(1,128)S(1)}) custom-call(s32[8]{0:T(128)S(1)} %bitcast.7, s32[1]{0:T(128)} %bitcast.2.place_ref, bf16[256,4096]{1,0:T(8,128)(2,1)S(1)} %shard_map.28.refs_0_, bf16[256,4096]{1,0:T(8,128)(2,1)S(1)} %get-tuple-element.39.refs_3_.refs_1_, ...), custom_call_target="tpu_custom_call" | custom-call | tf_op jit(solution)/shard_map/pallas_call | solution.py:135
  57.7 0.6 collective-permute-start.5
  58.3 0.8 %collective-permute-done.5 = f32[3,256]{1,0:T(4,128)S(1)} collective-permute-done((f32[3,256]{1,0:T(4,128)S(1)}, f32[3,256]{1,0:T(4,128)S(1)}, u32[]{:S(2)}, u32[]{:S(2)}) %collective-permute-start.5) | collective-permute-done | bytes 3104 | tf_op jit(solution)/shard_map/ppermute | solution.py:19
  59.1 1.3 %collective-permute-start.7 = (f32[2,256]{1,0:T(2,128)S(1)}, f32[2,256]{1,0:T(2,128)S(1)}, u32[]{:S(2)}, u32[]{:S(2)}) collective-permute-start(f32[2,256]{1,0:T(2,128)S(1)} %pad_maximum_fusion.1), channel_id=1, source_target_pairs={{1,9},{3,11},{4,0},{5,13},{6,2},{7,15},{8,4},{9,17},{10,6},{11,19}... | collective-permute-start | bytes 6152 | tf_op jit(solution)/shard_map/ppermute | solution.py:24
  60.5 1.8 %collective-permute-start.6 = (f32[1,256]{1,0:T(1,128)S(1)}, f32[1,256]{1,0:T(1,128)S(1)}, u32[]{:S(2)}, u32[]{:S(2)}) collective-permute-start(f32[1,256]{1,0:T(1,128)S(1)} %slice.34), channel_id=1, source_target_pairs={{0,2},{1,3},{2,0},{3,1},{4,6},{5,7},{6,4},{7,5},{8,10},{9,11},{10,... | collective-permute-start | bytes 3080 | tf_op jit(solution)/shard_map/ppermute | solution.py:19
  62.3 2.3 %collective-permute-done.7 = f32[2,256]{1,0:T(2,128)S(1)} collective-permute-done((f32[2,256]{1,0:T(2,128)S(1)}, f32[2,256]{1,0:T(2,128)S(1)}, u32[]{:S(2)}, u32[]{:S(2)}) %collective-permute-start.7) | collective-permute-done | bytes 2080 | tf_op jit(solution)/shard_map/ppermute | solution.py:24
  64.6 3.1 %collective-permute-start.8 = (f32[1,256]{1,0:T(1,128)S(1)}, f32[1,256]{1,0:T(1,128)S(1)}, u32[]{:S(2)}, u32[]{:S(2)}) collective-permute-start(f32[1,256]{1,0:T(1,128)S(1)} %slice.37), channel_id=1, source_target_pairs={{0,1},{1,0},{2,3},{3,2},{4,5},{5,4},{6,7},{7,6},{8,9},{9,8},{10,11... | collective-permute-start | bytes 3080 | tf_op jit(solution)/shard_map/ppermute | solution.py:19
  67.7 0.0 collective-permute-done.6
  67.7 0.8 %collective-permute-done.8 = f32[1,256]{1,0:T(1,128)S(1)} collective-permute-done((f32[1,256]{1,0:T(1,128)S(1)}, f32[1,256]{1,0:T(1,128)S(1)}, u32[]{:S(2)}, u32[]{:S(2)}) %collective-permute-start.8) | collective-permute-done | bytes 1056 | tf_op jit(solution)/shard_map/ppermute | solution.py:19
  68.5 0.6 fusion
  (9 shorter events, 0.1 us)
Async XLA Ops:
  0.0 9.8 %copy-start = (s32[8]{0:T(128)S(1)}, s32[8]{0:T(128)}, u32[]{:S(2)}) copy-start(s32[8]{0:T(128)} %param.3) | copy-start | bytes 100
  1.9 8.0 %collective-permute-start = (bf16[256,4096]{1,0:T(8,128)(2,1)S(1)}, bf16[256,4096]{1,0:T(8,128)(2,1)}, u32[]{:S(2)}, u32[]{:S(2)}) collective-permute-start(bf16[256,4096]{1,0:T(8,128)(2,1)S(1)} %shard_map.28.refs_0_), channel_id=1, source_target_pairs={{0,1},{1,0},{2,3},{3,2},{4,5},{5,4},{6,7},{7,6},{8,9},{9,8},{10,11... | collective-permute-start | bytes 6291464 | tf_op jit(solution)/shard_map/ppermute | solution.py:19
  2.5 48.9 %collective-permute-start.1 = (bf16[256,4096]{1,0:T(8,128)(2,1)S(1)}, bf16[256,4096]{1,0:T(8,128)(2,1)}, u32[]{:S(2)}, u32[]{:S(2)}) collective-permute-start(bf16[256,4096]{1,0:T(8,128)(2,1)S(1)} %shard_map.28.refs_0_), channel_id=1, source_target_pairs={{0,2},{1,3},{2,0},{3,1},{4,6},{5,7},{6,4},{7,5},{8,10},{9,11},{10,... | collective-permute-start | bytes 6291464 | tf_op jit(solution)/shard_map/ppermute | solution.py:19
  5.1 46.3 %collective-permute-start.2 = (bf16[256,4096]{1,0:T(8,128)(2,1)S(1)}, bf16[256,4096]{1,0:T(8,128)(2,1)}, u32[]{:S(2)}, u32[]{:S(2)}) collective-permute-start(bf16[256,4096]{1,0:T(8,128)(2,1)S(1)} %shard_map.28.refs_0_), channel_id=1, source_target_pairs={{0,4},{2,6},{4,8},{6,10},{8,12},{9,1},{10,14},{11,3},{12,16},{13,5... | collective-permute-start | bytes 6291464 | tf_op jit(solution)/shard_map/ppermute | solution.py:24
  13.3 41.7 %collective-permute-start.3 = (bf16[256,4096]{1,0:T(8,128)(2,1)S(1)}, bf16[256,4096]{1,0:T(8,128)(2,1)S(1)}, u32[]{:S(2)}, u32[]{:S(2)}) collective-permute-start(bf16[256,4096]{1,0:T(8,128)(2,1)S(1)} %shard_map.28.refs_0_), channel_id=1, source_target_pairs={{1,5},{3,7},{5,9},{7,11},{8,0},{9,13},{10,2},{11,15},{12,4},{13,17... | collective-permute-start | bytes 6291464 | tf_op jit(solution)/shard_map/ppermute | solution.py:24
  51.4 4.4 %collective-permute-start.4 = (bf16[256,4096]{1,0:T(8,128)(2,1)}, bf16[256,4096]{1,0:T(8,128)(2,1)S(1)}, u32[]{:S(2)}, u32[]{:S(2)}) collective-permute-start(bf16[256,4096]{1,0:T(8,128)(2,1)} %collective-permute-done.1.refs_2_), channel_id=1, source_target_pairs={{0,1},{1,0},{2,3},{3,2},{4,5},{5,4},{6,7},{7,6},{8,9},{9,8},{10,11... | collective-permute-start | bytes 6291464 | tf_op jit(solution)/shard_map/ppermute | solution.py:19
  57.7 1.4 %collective-permute-start.5 = (f32[3,256]{1,0:T(4,128)S(1)}, f32[3,256]{1,0:T(4,128)S(1)}, u32[]{:S(2)}, u32[]{:S(2)}) collective-permute-start(f32[3,256]{1,0:T(4,128)S(1)} %pad_maximum_fusion), channel_id=1, source_target_pairs={{0,1},{1,0},{2,3},{3,2},{4,5},{5,4},{6,7},{7,6},{8,9},{9,8},{10,11... | collective-permute-start | bytes 9224 | tf_op jit(solution)/shard_map/ppermute | solution.py:19
  59.1 5.5 %collective-permute-start.7 = (f32[2,256]{1,0:T(2,128)S(1)}, f32[2,256]{1,0:T(2,128)S(1)}, u32[]{:S(2)}, u32[]{:S(2)}) collective-permute-start(f32[2,256]{1,0:T(2,128)S(1)} %pad_maximum_fusion.1), channel_id=1, source_target_pairs={{1,9},{3,11},{4,0},{5,13},{6,2},{7,15},{8,4},{9,17},{10,6},{11,19}... | collective-permute-start | bytes 6152 | tf_op jit(solution)/shard_map/ppermute | solution.py:24
  60.5 7.3 %collective-permute-start.6 = (f32[1,256]{1,0:T(1,128)S(1)}, f32[1,256]{1,0:T(1,128)S(1)}, u32[]{:S(2)}, u32[]{:S(2)}) collective-permute-start(f32[1,256]{1,0:T(1,128)S(1)} %slice.34), channel_id=1, source_target_pairs={{0,2},{1,3},{2,0},{3,1},{4,6},{5,7},{6,4},{7,5},{8,10},{9,11},{10,... | collective-permute-start | bytes 3080 | tf_op jit(solution)/shard_map/ppermute | solution.py:19
  64.6 3.9 %collective-permute-start.8 = (f32[1,256]{1,0:T(1,128)S(1)}, f32[1,256]{1,0:T(1,128)S(1)}, u32[]{:S(2)}, u32[]{:S(2)}) collective-permute-start(f32[1,256]{1,0:T(1,128)S(1)} %slice.37), channel_id=1, source_target_pairs={{0,1},{1,0},{2,3},{3,2},{4,5},{5,4},{6,7},{7,6},{8,9},{9,8},{10,11... | collective-permute-start | bytes 3080 | tf_op jit(solution)/shard_map/ppermute | solution.py:19

commit v9 on v8

--- a/solution.py
+++ b/solution.py
@@ -24,13 +24,15 @@
     return lax.ppermute(x, AXES, [(i, j) for i, j in moves if 0 <= j < devices])
 
 
-def labels_of(bounds_ref, block, length, axis):
-    shape = (length, 1) if axis == 0 else (1, length)
-    positions = block * length + lax.broadcasted_iota(jnp.int32, shape, axis)
-    labels = jnp.where(positions < 0, -1, 0)
+def spans_of(bounds_ref, block, length):
+    positions = block * length + lax.broadcasted_iota(jnp.int32, (1, length), 1)
+    starts, ends = jnp.zeros_like(positions), jnp.full_like(positions, jnp.iinfo(jnp.int32).max)
     for c in range(bounds_ref.shape[0]):
-        labels = labels + (bounds_ref[c] <= positions).astype(jnp.int32)
-    return labels
+        bound = bounds_ref[c]
+        passed = bound <= positions
+        starts = jnp.where(passed, jnp.maximum(starts, bound), starts)
+        ends = jnp.where(passed, ends, jnp.minimum(ends, bound))
+    return starts, ends
 
 
 def label_at(bounds_ref, row):
@@ -45,9 +47,10 @@
     return label_at(bounds_ref, (lower + 1) * length - 1) == label_at(bounds_ref, upper * length)
 
 
-def masked_scores(left, right, left_labels, right_labels):
+def masked_scores(left, right, block, spans):
     scores = lax.dot_general(left[...], right[...], NT, preferred_element_type=jnp.float32)
-    return jnp.where(left_labels == right_labels, scores, FILLER)
+    positions = block * left.shape[0] + lax.broadcasted_iota(jnp.int32, scores.shape, 0)
+    return jnp.where((positions >= spans[0]) & (positions < spans[1]), scores, FILLER)
 
 
 def folded(masked):
@@ -93,13 +96,12 @@
     even = place % 2 == 0
     blocks = {name: place ^ b for b, name in enumerate(IN_QUAD)}
     blocks["first"], blocks["second"] = jnp.where(even, below, above), jnp.where(even, above, below)
-    left_labels = {name: labels_of(bounds_ref, blocks[name], length, 0) for name in {pair[0]: 0 for pair in pairs}}
-    right_labels = {name: labels_of(bounds_ref, blocks[name], length, 1) for name in {pair[1]: 0 for pair in pairs}}
+    spans = {name: spans_of(bounds_ref, blocks[name], length) for name in {pair[1]: 0 for pair in pairs}}
     for left, right in pairs:
 
         def multiply(left=left, right=right):
             pair = sources[names.index(left)], sources[names.index(right)]
-            scores = masked_scores(*pair, left_labels[left], right_labels[right])
+            scores = masked_scores(*pair, blocks[left], spans[right])
             if left == right:
                 rows = lax.broadcasted_iota(jnp.int32, scores.shape, 0)
                 columns = lax.broadcasted_iota(jnp.int32, scores.shape, 1)

time: 69.3 us -> 68.9 us (level)
  the two profiles are of different devices: /device:TPU:0 before, /device:TPU:17 now
where the time goes in v9:
time: 68.9 us; the launch traced here: 68.6 us
  waiting for transfers between devices  41.8 us (61%)
  Pallas kernels  13.9 us (20%)
  starting transfers between devices  11.9 us (17%)
  other arithmetic  0.78 us (1%)
    ppermute x6, waiting for transfers between devices, swapped(): return lax.ppermute(x, AXES, [(i, i ^ bit) for i in range(devices)])  39.4 us
    pallas_call x4, Pallas kernels, products(): pl.pallas_call(functools.partial(products_kernel, names, pairs, keep, sta...  11.9 us
    ppermute x3, starting transfers between devices, shifted(): return lax.ppermute(x, AXES, [(i, j) for i, j in moves if 0 <= j < devices])  7.1 us
    ppermute x6, starting transfers between devices, swapped(): return lax.ppermute(x, AXES, [(i, i ^ bit) for i in range(devices)])  4.83 us
    ppermute x3, waiting for transfers between devices, shifted(): return lax.ppermute(x, AXES, [(i, j) for i, j in moves if 0 <= j < devices])  2.46 us
    pallas_call x1, Pallas kernels, local(): pl.pallas_call(normalize_kernel, out_shape=jax.ShapeDtypeStruct((length,...  1.93 us
  transfers between devices with their start and end apart: 9, of which 6 were waited for; matrix products, arithmetic and copies ran while one was open for 0% of the time, Pallas kernels for 14%

profile of v9, /device:TPU:17, one launch (start us, length us, event | category | flops | bytes accessed | tf_op | source)
XLA Modules:
  0.0 68.6 jit_solution(7220977421558629650)
XLA Ops:
  0.0 0.0 copy-start
  0.0 1.9 %shard_map.28.refs_0_ = bf16[256,4096]{1,0:T(8,128)(2,1)S(1)} custom-call(bf16[256,4096]{1,0:T(8,128)(2,1)} %raw_hbm.1), custom_call_target="tpu_custom_call" | custom-call | bytes 4194304 | tf_op jit(solution)/shard_map/pallas_call | solution.py:159
  1.9 0.7 %collective-permute-start = (bf16[256,4096]{1,0:T(8,128)(2,1)S(1)}, bf16[256,4096]{1,0:T(8,128)(2,1)}, u32[]{:S(2)}, u32[]{:S(2)}) collective-permute-start(bf16[256,4096]{1,0:T(8,128)(2,1)S(1)} %shard_map.28.refs_0_), channel_id=1, source_target_pairs={{0,1},{1,0},{2,3},{3,2},{4,5},{5,4},{6,7},{7,6},{8,9},{9,8},{10,11... | collective-permute-start | bytes 6291464 | tf_op jit(solution)/shard_map/ppermute | solution.py:19
  2.7 1.3 %collective-permute-start.1 = (bf16[256,4096]{1,0:T(8,128)(2,1)S(1)}, bf16[256,4096]{1,0:T(8,128)(2,1)}, u32[]{:S(2)}, u32[]{:S(2)}) collective-permute-start(bf16[256,4096]{1,0:T(8,128)(2,1)S(1)} %shard_map.28.refs_0_), channel_id=1, source_target_pairs={{0,2},{1,3},{2,0},{3,1},{4,6},{5,7},{6,4},{7,5},{8,10},{9,11},{10,... | collective-permute-start | bytes 6291464 | tf_op jit(solution)/shard_map/ppermute | solution.py:19
  3.9 2.1 %collective-permute-start.2 = (bf16[256,4096]{1,0:T(8,128)(2,1)S(1)}, bf16[256,4096]{1,0:T(8,128)(2,1)}, u32[]{:S(2)}, u32[]{:S(2)}) collective-permute-start(bf16[256,4096]{1,0:T(8,128)(2,1)S(1)} %shard_map.28.refs_0_), channel_id=1, source_target_pairs={{0,4},{2,6},{4,8},{6,10},{8,12},{9,1},{10,14},{11,3},{12,16},{13,5... | collective-permute-start | bytes 6291464 | tf_op jit(solution)/shard_map/ppermute | solution.py:24
  6.0 0.0 copy-done
  6.0 0.2 reduce-window.9
  6.2 0.4 collective-permute-done.refs_1_
  6.6 3.2 %shard_map.29 = (f32[4,256]{1,0:T(4,128)S(1)}, f32[256,128]{1,0:T(8,128)S(1)}, f32[256,128]{1,0:T(8,128)S(1)}, bf16[256,4096]{1,0:T(8,128)(2,1)S(1)}) custom-call(s32[8]{0:T(128)S(1)} %bitcast.4, s32[1]{0:T(128)} %bitcast.2.place_ref, bf16[256,4096]{1,0:T(8,128)(2,1)S(1)} %shard_map.28.refs_0_, bf16[256,4096]{1,0:T(8,128)(2,1)} %collective-permute-done.refs_1_), custom_call_target="tpu_custom_call" | custom-call | tf_op jit(solution)/shard_map/pallas_call | solution.py:137
  9.8 3.1 %collective-permute-start.3 = (bf16[256,4096]{1,0:T(8,128)(2,1)S(1)}, bf16[256,4096]{1,0:T(8,128)(2,1)S(1)}, u32[]{:S(2)}, u32[]{:S(2)}) collective-permute-start(bf16[256,4096]{1,0:T(8,128)(2,1)S(1)} %shard_map.28.refs_0_), channel_id=1, source_target_pairs={{1,5},{3,7},{5,9},{7,11},{8,0},{9,13},{10,2},{11,15},{12,4},{13,17... | collective-permute-start | bytes 6291464 | tf_op jit(solution)/shard_map/ppermute | solution.py:24
  13.0 37.0 %collective-permute-done.1.refs_2_ = bf16[256,4096]{1,0:T(8,128)(2,1)} collective-permute-done((bf16[256,4096]{1,0:T(8,128)(2,1)S(1)}, bf16[256,4096]{1,0:T(8,128)(2,1)}, u32[]{:S(2)}, u32[]{:S(2)}) %collective-permute-start.1) | collective-permute-done | bytes 2097184 | tf_op jit(solution)/shard_map/ppermute | solution.py:19
  50.0 0.8 %collective-permute-start.4 = (bf16[256,4096]{1,0:T(8,128)(2,1)}, bf16[256,4096]{1,0:T(8,128)(2,1)S(1)}, u32[]{:S(2)}, u32[]{:S(2)}) collective-permute-start(bf16[256,4096]{1,0:T(8,128)(2,1)} %collective-permute-done.1.refs_2_), channel_id=1, source_target_pairs={{0,1},{1,0},{2,3},{3,2},{4,5},{5,4},{6,7},{7,6},{8,9},{9,8},{10,11... | collective-permute-start | bytes 6291464 | tf_op jit(solution)/shard_map/ppermute | solution.py:19
  50.8 0.0 collective-permute-done.2.refs_3_
  50.8 3.4 %shard_map.30 = (f32[4,256]{1,0:T(4,128)S(1)}, f32[256,128]{1,0:T(8,128)S(1)}, f32[256,128]{1,0:T(8,128)S(1)}, bf16[256,4096]{1,0:T(8,128)(2,1)S(1)}, bf16[256,4096]{1,0:T(8,128)(2,1)S(1)}) custom-call(s32[8]{0:T(128)S(1)} %bitcast.5, s32[1]{0:T(128)} %bitcast.2.place_ref, bf16[256,4096]{1,0:T(8,128)(2,1)S(1)} %shard_map.28.refs_0_, ...), custom_call_target="tpu_custom_call" | custom-call | tf_op jit(solution)/shard_map/pallas_call | solution.py:137
  54.3 0.6 collective-permute-done.3.refs_4_.refs_2_
  54.9 2.9 %shard_map.31 = (f32[4,256]{1,0:T(4,128)S(1)}, f32[256,128]{1,0:T(8,128)S(1)}, f32[256,128]{1,0:T(8,128)S(1)}) custom-call(s32[8]{0:T(128)S(1)} %bitcast.6, s32[1]{0:T(128)} %bitcast.2.place_ref, bf16[256,4096]{1,0:T(8,128)(2,1)S(1)} %shard_map.28.refs_0_, bf16[256,4096]{1,0:T(8,128)(2,1)S(1)} %get-tuple-element.28.refs_1_, ...), custom_call_target="tpu_custom_call" | custom-call | tf_op jit(solution)/shard_map/pallas_call | solution.py:137
  57.8 0.0 collective-permute-done.4.refs_3_
  57.8 2.4 %shard_map.32 = (f32[4,256]{1,0:T(4,128)S(1)}, f32[1,256]{1,0:T(1,128)S(1)}, f32[1,256]{1,0:T(1,128)S(1)}) custom-call(s32[8]{0:T(128)S(1)} %bitcast.7, s32[1]{0:T(128)} %bitcast.2.place_ref, bf16[256,4096]{1,0:T(8,128)(2,1)S(1)} %shard_map.28.refs_0_, bf16[256,4096]{1,0:T(8,128)(2,1)S(1)} %get-tuple-element.39.refs_3_.refs_1_, ...), custom_call_target="tpu_custom_call" | custom-call | tf_op jit(solution)/shard_map/pallas_call | solution.py:137
  60.3 0.1 collective-permute-start.5
  60.4 1.1 %collective-permute-done.5 = f32[3,256]{1,0:T(4,128)S(1)} collective-permute-done((f32[3,256]{1,0:T(4,128)S(1)}, f32[3,256]{1,0:T(4,128)S(1)}, u32[]{:S(2)}, u32[]{:S(2)}) %collective-permute-start.5) | collective-permute-done | bytes 3104 | tf_op jit(solution)/shard_map/ppermute | solution.py:19
  61.5 1.9 %collective-permute-start.7 = (f32[2,256]{1,0:T(2,128)S(1)}, f32[2,256]{1,0:T(2,128)S(1)}, u32[]{:S(2)}, u32[]{:S(2)}) collective-permute-start(f32[2,256]{1,0:T(2,128)S(1)} %pad_maximum_fusion.1), channel_id=1, source_target_pairs={{1,9},{3,11},{4,0},{5,13},{6,2},{7,15},{8,4},{9,17},{10,6},{11,19}... | collective-permute-start | bytes 6152 | tf_op jit(solution)/shard_map/ppermute | solution.py:24
  63.5 0.5 collective-permute-start.6
  64.0 1.8 %collective-permute-done.7 = f32[2,256]{1,0:T(2,128)S(1)} collective-permute-done((f32[2,256]{1,0:T(2,128)S(1)}, f32[2,256]{1,0:T(2,128)S(1)}, u32[]{:S(2)}, u32[]{:S(2)}) %collective-permute-start.7) | collective-permute-done | bytes 2080 | tf_op jit(solution)/shard_map/ppermute | solution.py:24
  65.8 1.4 %collective-permute-start.8 = (f32[1,256]{1,0:T(1,128)S(1)}, f32[1,256]{1,0:T(1,128)S(1)}, u32[]{:S(2)}, u32[]{:S(2)}) collective-permute-start(f32[1,256]{1,0:T(1,128)S(1)} %slice.37), channel_id=1, source_target_pairs={{0,1},{1,0},{2,3},{3,2},{4,5},{5,4},{6,7},{7,6},{8,9},{9,8},{10,11... | collective-permute-start | bytes 3080 | tf_op jit(solution)/shard_map/ppermute | solution.py:19
  67.2 0.0 collective-permute-done.6
  67.2 0.8 %collective-permute-done.8 = f32[1,256]{1,0:T(1,128)S(1)} collective-permute-done((f32[1,256]{1,0:T(1,128)S(1)}, f32[1,256]{1,0:T(1,128)S(1)}, u32[]{:S(2)}, u32[]{:S(2)}) %collective-permute-start.8) | collective-permute-done | bytes 1056 | tf_op jit(solution)/shard_map/ppermute | solution.py:19
  68.0 0.6 fusion
  (9 shorter events, 0.1 us)
Async XLA Ops:
  0.0 6.0 %copy-start = (s32[8]{0:T(128)S(1)}, s32[8]{0:T(128)}, u32[]{:S(2)}) copy-start(s32[8]{0:T(128)} %param.3) | copy-start | bytes 100
  1.9 4.7 %collective-permute-start = (bf16[256,4096]{1,0:T(8,128)(2,1)S(1)}, bf16[256,4096]{1,0:T(8,128)(2,1)}, u32[]{:S(2)}, u32[]{:S(2)}) collective-permute-start(bf16[256,4096]{1,0:T(8,128)(2,1)S(1)} %shard_map.28.refs_0_), channel_id=1, source_target_pairs={{0,1},{1,0},{2,3},{3,2},{4,5},{5,4},{6,7},{7,6},{8,9},{9,8},{10,11... | collective-permute-start | bytes 6291464 | tf_op jit(solution)/shard_map/ppermute | solution.py:19
  2.7 47.3 %collective-permute-start.1 = (bf16[256,4096]{1,0:T(8,128)(2,1)S(1)}, bf16[256,4096]{1,0:T(8,128)(2,1)}, u32[]{:S(2)}, u32[]{:S(2)}) collective-permute-start(bf16[256,4096]{1,0:T(8,128)(2,1)S(1)} %shard_map.28.refs_0_), channel_id=1, source_target_pairs={{0,2},{1,3},{2,0},{3,1},{4,6},{5,7},{6,4},{7,5},{8,10},{9,11},{10,... | collective-permute-start | bytes 6291464 | tf_op jit(solution)/shard_map/ppermute | solution.py:19
  3.9 46.9 %collective-permute-start.2 = (bf16[256,4096]{1,0:T(8,128)(2,1)S(1)}, bf16[256,4096]{1,0:T(8,128)(2,1)}, u32[]{:S(2)}, u32[]{:S(2)}) collective-permute-start(bf16[256,4096]{1,0:T(8,128)(2,1)S(1)} %shard_map.28.refs_0_), channel_id=1, source_target_pairs={{0,4},{2,6},{4,8},{6,10},{8,12},{9,1},{10,14},{11,3},{12,16},{13,5... | collective-permute-start | bytes 6291464 | tf_op jit(solution)/shard_map/ppermute | solution.py:24
  9.8 45.0 %collective-permute-start.3 = (bf16[256,4096]{1,0:T(8,128)(2,1)S(1)}, bf16[256,4096]{1,0:T(8,128)(2,1)S(1)}, u32[]{:S(2)}, u32[]{:S(2)}) collective-permute-start(bf16[256,4096]{1,0:T(8,128)(2,1)S(1)} %shard_map.28.refs_0_), channel_id=1, source_target_pairs={{1,5},{3,7},{5,9},{7,11},{8,0},{9,13},{10,2},{11,15},{12,4},{13,17... | collective-permute-start | bytes 6291464 | tf_op jit(solution)/shard_map/ppermute | solution.py:24
  50.0 7.8 %collective-permute-start.4 = (bf16[256,4096]{1,0:T(8,128)(2,1)}, bf16[256,4096]{1,0:T(8,128)(2,1)S(1)}, u32[]{:S(2)}, u32[]{:S(2)}) collective-permute-start(bf16[256,4096]{1,0:T(8,128)(2,1)} %collective-permute-done.1.refs_2_), channel_id=1, source_target_pairs={{0,1},{1,0},{2,3},{3,2},{4,5},{5,4},{6,7},{7,6},{8,9},{9,8},{10,11... | collective-permute-start | bytes 6291464 | tf_op jit(solution)/shard_map/ppermute | solution.py:19
  60.3 1.2 %collective-permute-start.5 = (f32[3,256]{1,0:T(4,128)S(1)}, f32[3,256]{1,0:T(4,128)S(1)}, u32[]{:S(2)}, u32[]{:S(2)}) collective-permute-start(f32[3,256]{1,0:T(4,128)S(1)} %pad_maximum_fusion), channel_id=1, source_target_pairs={{0,1},{1,0},{2,3},{3,2},{4,5},{5,4},{6,7},{7,6},{8,9},{9,8},{10,11... | collective-permute-start | bytes 9224 | tf_op jit(solution)/shard_map/ppermute | solution.py:19
  61.5 4.3 %collective-permute-start.7 = (f32[2,256]{1,0:T(2,128)S(1)}, f32[2,256]{1,0:T(2,128)S(1)}, u32[]{:S(2)}, u32[]{:S(2)}) collective-permute-start(f32[2,256]{1,0:T(2,128)S(1)} %pad_maximum_fusion.1), channel_id=1, source_target_pairs={{1,9},{3,11},{4,0},{5,13},{6,2},{7,15},{8,4},{9,17},{10,6},{11,19}... | collective-permute-start | bytes 6152 | tf_op jit(solution)/shard_map/ppermute | solution.py:24
  63.5 3.8 %collective-permute-start.6 = (f32[1,256]{1,0:T(1,128)S(1)}, f32[1,256]{1,0:T(1,128)S(1)}, u32[]{:S(2)}, u32[]{:S(2)}) collective-permute-start(f32[1,256]{1,0:T(1,128)S(1)} %slice.34), channel_id=1, source_target_pairs={{0,2},{1,3},{2,0},{3,1},{4,6},{5,7},{6,4},{7,5},{8,10},{9,11},{10,... | collective-permute-start | bytes 3080 | tf_op jit(solution)/shard_map/ppermute | solution.py:19
  65.8 2.2 %collective-permute-start.8 = (f32[1,256]{1,0:T(1,128)S(1)}, f32[1,256]{1,0:T(1,128)S(1)}, u32[]{:S(2)}, u32[]{:S(2)}) collective-permute-start(f32[1,256]{1,0:T(1,128)S(1)} %slice.37), channel_id=1, source_target_pairs={{0,1},{1,0},{2,3},{3,2},{4,5},{5,4},{6,7},{7,6},{8,9},{9,8},{10,11... | collective-permute-start | bytes 3080 | tf_op jit(solution)/shard_map/ppermute | solution.py:19

commit v10 on v9

--- a/solution.py
+++ b/solution.py
@@ -87,8 +87,15 @@
     if not starts:
         entering, refs = refs[:3], refs[3:]
     (quad_out, first_out, second_out), kept, refs = refs[:3], refs[3:3 + len(keep)], refs[3 + len(keep):]
+    length = sources[0].shape[0]
+    sources, copies = dict(zip(names, sources)), {}
+    if keep:
+        *refs, sems = refs
+        for i, (name, ref) in enumerate(zip(keep, kept)):
+            copies[name] = pltpu.make_async_copy(sources[name], ref, sems.at[i])
+            copies[name].start()
+            sources[name] = ref
     widest = dict(zip(("first", "second"), refs if ends else (first_out, second_out)))
-    length = sources[0].shape[0]
     for i, ref in enumerate((quad_out, widest["first"], widest["second"])):
         ref[...] = jnp.full_like(ref, FILLER) if starts else entering[i][...]
     place = place_ref[0]
@@ -98,10 +105,12 @@
     blocks["first"], blocks["second"] = jnp.where(even, below, above), jnp.where(even, above, below)
     spans = {name: spans_of(bounds_ref, blocks[name], length) for name in {pair[1]: 0 for pair in pairs}}
     for left, right in pairs:
+        for name in (left, right):
+            if name in copies:
+                copies.pop(name).wait()
 
         def multiply(left=left, right=right):
-            pair = sources[names.index(left)], sources[names.index(right)]
-            scores = masked_scores(*pair, blocks[left], spans[right])
+            scores = masked_scores(sources[left], sources[right], blocks[left], spans[right])
             if left == right:
                 rows = lax.broadcasted_iota(jnp.int32, scores.shape, 0)
                 columns = lax.broadcasted_iota(jnp.int32, scores.shape, 1)
@@ -110,19 +119,24 @@
             quad_out[b:b + 1, :] = jnp.maximum(quad_out[b:b + 1, :], over_rows(scores))
             if left in widest:
                 widest[left][...] = jnp.maximum(widest[left][...], folded(scores))
+            if left == "across":
+                b = IN_QUAD.index(left)
+                quad_out[b:b + 1, :] = jnp.maximum(quad_out[b:b + 1, :], over_rows(folded(scores).T))
 
         if left == right:
             multiply()
-        else:
-            pl.when(touch(bounds_ref, blocks[left], blocks[right], length))(multiply)
-    for name, ref in zip(keep, kept):
-        ref[...] = sources[names.index(name)][...]
+            continue
+        wanted = touch(bounds_ref, blocks[left], blocks[right], length)
+        if left == "across":
+            wanted &= place // 2 % 2 == ("own", "near").index(right)
+        pl.when(wanted)(multiply)
     if ends:
         first_out[...] = over_rows(widest["first"][...].T)
         second_out[...] = over_rows(widest["second"][...].T)
 
 
 HBM = pl.BlockSpec(memory_space=pltpu.HBM)
+ANY = pl.BlockSpec(memory_space=pl.ANY)
 VMEM = pl.BlockSpec(memory_space=pltpu.VMEM)
 SMEM = pl.BlockSpec(memory_space=pltpu.SMEM)
 
@@ -137,9 +151,10 @@
     results = pl.pallas_call(
         functools.partial(products_kernel, names, pairs, keep, state is None, ends),
         out_shape=(jax.ShapeDtypeStruct((QUAD, length), jnp.float32),) + ((line, line) if ends else (folds, folds)) + (block,) * len(keep),
-        in_specs=[SMEM, SMEM] + [VMEM] * (len(names) + len(entering)),
+        in_specs=[SMEM, SMEM] + [ANY if name in keep else VMEM for name in names] + [VMEM] * len(entering),
         out_specs=(VMEM,) * (3 + len(keep)),
-        scratch_shapes=[pltpu.VMEM((length, 128), jnp.float32)] * (2 if ends else 0),
+        scratch_shapes=[pltpu.VMEM((length, 128), jnp.float32)] * (2 if ends else 0)
+        + ([pltpu.SemaphoreType.DMA((len(keep),))] if keep else []),
         compiler_params=pltpu.CompilerParams(vmem_limit_bytes=24 << 20),
         cost_estimate=pl.CostEstimate(
             flops=0,
@@ -178,7 +193,7 @@
     across, *state = lax.optimization_barrier((across, *state))
     across_near = swapped(across, devices, 1)
     held["across"], held["first"] = across, first
-    pairs = (("across", "own"), ("first", "own"), ("first", "near"), ("first", "across"))
+    pairs = (("across", "own"), ("across", "near"), ("first", "own"), ("first", "near"), ("first", "across"))
     state, held = products(bounds, where, held, pairs, state, keep=("across", "first"))
 
     held["second"] = second
@@ -186,8 +201,8 @@
     state, held = products(bounds, where, held, pairs, state)
 
     held["across_near"] = across_near
-    del held["near"], held["across"]
-    pairs = (("across_near", "own"), ("first", "across_near"), ("second", "across_near"))
+    held = {name: held[name] for name in ("first", "second", "across_near")}
+    pairs = (("first", "across_near"), ("second", "across_near"))
     (quad, first_best, second_best), unused = products(bounds, where, held, pairs, state, ends=True)
 
     received = swapped(jnp.concatenate([quad[1::2], second_best]), devices, 1)

time: 68.9 us -> 67.9 us (0.985)
  the two profiles are of different devices: /device:TPU:17 before, /device:TPU:0 now
where the time goes in v10:
time: 67.9 us; the launch traced here: 67.2 us
  waiting for transfers between devices  43.5 us (64%)
  starting transfers between devices  13.4 us (20%)
  Pallas kernels  9.32 us (14%)
  other arithmetic  0.78 us (1%)
    ppermute x6, waiting for transfers between devices, swapped(): return lax.ppermute(x, AXES, [(i, i ^ bit) for i in range(devices)])  39.5 us
    pallas_call x4, Pallas kernels, products(): pl.pallas_call(functools.partial(products_kernel, names, pairs, keep, sta...  7.39 us
    ppermute x3, starting transfers between devices, shifted(): return lax.ppermute(x, AXES, [(i, j) for i, j in moves if 0 <= j < devices])  7.3 us
    ppermute x6, starting transfers between devices, swapped(): return lax.ppermute(x, AXES, [(i, i ^ bit) for i in range(devices)])  6.12 us
    ppermute x3, waiting for transfers between devices, shifted(): return lax.ppermute(x, AXES, [(i, j) for i, j in moves if 0 <= j < devices])  4.03 us
    pallas_call x1, Pallas kernels, local(): pl.pallas_call(normalize_kernel, out_shape=jax.ShapeDtypeStruct((length,...  1.93 us
  transfers between devices with their start and end apart: 9, of which 6 were waited for; matrix products, arithmetic and copies ran while one was open for 0% of the time, Pallas kernels for 10%

profile of v10, /device:TPU:0, one launch (start us, length us, event | category | flops | bytes accessed | tf_op | source)
XLA Modules:
  0.0 67.2 jit_solution(5148198756349216077)
XLA Ops:
  0.0 0.0 copy-start
  0.0 1.9 %shard_map.28.refs_0_ = bf16[256,4096]{1,0:T(8,128)(2,1)S(1)} custom-call(bf16[256,4096]{1,0:T(8,128)(2,1)} %raw_hbm.1), custom_call_target="tpu_custom_call" | custom-call | bytes 4194304 | tf_op jit(solution)/shard_map/pallas_call | solution.py:174
  1.9 0.5 collective-permute-start
  2.5 2.6 %collective-permute-start.1 = (bf16[256,4096]{1,0:T(8,128)(2,1)S(1)}, bf16[256,4096]{1,0:T(8,128)(2,1)}, u32[]{:S(2)}, u32[]{:S(2)}) collective-permute-start(bf16[256,4096]{1,0:T(8,128)(2,1)S(1)} %shard_map.28.refs_0_), channel_id=1, source_target_pairs={{0,2},{1,3},{2,0},{3,1},{4,6},{5,7},{6,4},{7,5},{8,10},{9,11},{10,... | collective-permute-start | bytes 6291464 | tf_op jit(solution)/shard_map/ppermute | solution.py:19
  5.1 4.7 %collective-permute-start.2 = (bf16[256,4096]{1,0:T(8,128)(2,1)S(1)}, bf16[256,4096]{1,0:T(8,128)(2,1)}, u32[]{:S(2)}, u32[]{:S(2)}) collective-permute-start(bf16[256,4096]{1,0:T(8,128)(2,1)S(1)} %shard_map.28.refs_0_), channel_id=1, source_target_pairs={{0,4},{2,6},{4,8},{6,10},{8,12},{9,1},{10,14},{11,3},{12,16},{13,5... | collective-permute-start | bytes 6291464 | tf_op jit(solution)/shard_map/ppermute | solution.py:24
  9.8 0.0 copy-done
  9.8 0.2 reduce-window.9
  10.0 0.0 collective-permute-done.refs_1_
  10.0 2.9 %shard_map.29 = (f32[4,256]{1,0:T(4,128)S(1)}, f32[256,128]{1,0:T(8,128)S(1)}, f32[256,128]{1,0:T(8,128)S(1)}, bf16[256,4096]{1,0:T(8,128)(2,1)S(1)}) custom-call(s32[8]{0:T(128)S(1)} %bitcast.4, s32[1]{0:T(128)} %bitcast.2.place_ref, bf16[256,4096]{1,0:T(8,128)(2,1)S(1)} %shard_map.28.refs_0_, bf16[256,4096]{1,0:T(8,128)(2,1)} %collective-permute-done.refs_1_), custom_call_target="tpu_custom_call" | custom-call | tf_op jit(solution)/shard_map/pallas_call | solution.py:151
  12.9 1.3 %collective-permute-start.3 = (bf16[256,4096]{1,0:T(8,128)(2,1)S(1)}, bf16[256,4096]{1,0:T(8,128)(2,1)S(1)}, u32[]{:S(2)}, u32[]{:S(2)}) collective-permute-start(bf16[256,4096]{1,0:T(8,128)(2,1)S(1)} %shard_map.28.refs_0_), channel_id=1, source_target_pairs={{1,5},{3,7},{5,9},{7,11},{8,0},{9,13},{10,2},{11,15},{12,4},{13,17... | collective-permute-start | bytes 6291464 | tf_op jit(solution)/shard_map/ppermute | solution.py:24
  14.2 37.2 %collective-permute-done.1.refs_2_ = bf16[256,4096]{1,0:T(8,128)(2,1)} collective-permute-done((bf16[256,4096]{1,0:T(8,128)(2,1)S(1)}, bf16[256,4096]{1,0:T(8,128)(2,1)}, u32[]{:S(2)}, u32[]{:S(2)}) %collective-permute-start.1) | collective-permute-done | bytes 2097184 | tf_op jit(solution)/shard_map/ppermute | solution.py:19
  51.4 0.0 collective-permute-start.4
  51.4 0.0 collective-permute-done.2.refs_3_
  51.4 3.1 %shard_map.30 = (f32[4,256]{1,0:T(4,128)S(1)}, f32[256,128]{1,0:T(8,128)S(1)}, f32[256,128]{1,0:T(8,128)S(1)}, bf16[256,4096]{1,0:T(8,128)(2,1)S(1)}, bf16[256,4096]{1,0:T(8,128)(2,1)S(1)}) custom-call(s32[8]{0:T(128)S(1)} %bitcast.5, s32[1]{0:T(128)} %bitcast.2.place_ref, bf16[256,4096]{1,0:T(8,128)(2,1)S(1)} %shard_map.28.refs_0_, ...), custom_call_target="tpu_custom_call" | custom-call | tf_op jit(solution)/shard_map/pallas_call | solution.py:151
  54.5 0.2 collective-permute-done.3.refs_4_.refs_1_
  54.6 0.7 shard_map.31
  55.3 0.5 collective-permute-done.4.refs_2_
  55.8 0.8 %shard_map.32 = (f32[4,256]{1,0:T(4,128)S(1)}, f32[1,256]{1,0:T(1,128)S(1)}, f32[1,256]{1,0:T(1,128)S(1)}) custom-call(s32[8]{0:T(128)S(1)} %bitcast.7, s32[1]{0:T(128)} %bitcast.2.place_ref, bf16[256,4096]{1,0:T(8,128)(2,1)S(1)} %get-tuple-element.39.refs_3_.refs_0_, bf16[256,4096]{1,0:T(8,128)(2,1)S(1)} %collective-permute-done.3.refs_4_.refs_1_, ...), custom_call_target="tpu_custom_call" | custom-call | tf_op jit(solution)/shard_map/pallas_call | solution.py:151
  56.5 0.2 collective-permute-start.5
  56.8 1.0 %collective-permute-done.5 = f32[3,256]{1,0:T(4,128)S(1)} collective-permute-done((f32[3,256]{1,0:T(4,128)S(1)}, f32[3,256]{1,0:T(4,128)S(1)}, u32[]{:S(2)}, u32[]{:S(2)}) %collective-permute-start.5) | collective-permute-done | bytes 3104 | tf_op jit(solution)/shard_map/ppermute | solution.py:19
  57.8 1.3 %collective-permute-start.7 = (f32[2,256]{1,0:T(2,128)S(1)}, f32[2,256]{1,0:T(2,128)S(1)}, u32[]{:S(2)}, u32[]{:S(2)}) collective-permute-start(f32[2,256]{1,0:T(2,128)S(1)} %pad_maximum_fusion.1), channel_id=1, source_target_pairs={{1,9},{3,11},{4,0},{5,13},{6,2},{7,15},{8,4},{9,17},{10,6},{11,19}... | collective-permute-start | bytes 6152 | tf_op jit(solution)/shard_map/ppermute | solution.py:24
  59.1 1.8 %collective-permute-start.6 = (f32[1,256]{1,0:T(1,128)S(1)}, f32[1,256]{1,0:T(1,128)S(1)}, u32[]{:S(2)}, u32[]{:S(2)}) collective-permute-start(f32[1,256]{1,0:T(1,128)S(1)} %slice.34), channel_id=1, source_target_pairs={{0,2},{1,3},{2,0},{3,1},{4,6},{5,7},{6,4},{7,5},{8,10},{9,11},{10,... | collective-permute-start | bytes 3080 | tf_op jit(solution)/shard_map/ppermute | solution.py:19
  60.9 3.9 %collective-permute-done.7 = f32[2,256]{1,0:T(2,128)S(1)} collective-permute-done((f32[2,256]{1,0:T(2,128)S(1)}, f32[2,256]{1,0:T(2,128)S(1)}, u32[]{:S(2)}, u32[]{:S(2)}) %collective-permute-start.7) | collective-permute-done | bytes 2080 | tf_op jit(solution)/shard_map/ppermute | solution.py:24
  64.8 1.0 %collective-permute-start.8 = (f32[1,256]{1,0:T(1,128)S(1)}, f32[1,256]{1,0:T(1,128)S(1)}, u32[]{:S(2)}, u32[]{:S(2)}) collective-permute-start(f32[1,256]{1,0:T(1,128)S(1)} %slice.37), channel_id=1, source_target_pairs={{0,1},{1,0},{2,3},{3,2},{4,5},{5,4},{6,7},{7,6},{8,9},{9,8},{10,11... | collective-permute-start | bytes 3080 | tf_op jit(solution)/shard_map/ppermute | solution.py:19
  65.8 0.0 collective-permute-done.6
  65.8 0.8 %collective-permute-done.8 = f32[1,256]{1,0:T(1,128)S(1)} collective-permute-done((f32[1,256]{1,0:T(1,128)S(1)}, f32[1,256]{1,0:T(1,128)S(1)}, u32[]{:S(2)}, u32[]{:S(2)}) %collective-permute-start.8) | collective-permute-done | bytes 1056 | tf_op jit(solution)/shard_map/ppermute | solution.py:19
  66.6 0.6 fusion
  (9 shorter events, 0.1 us)
Async XLA Ops:
  0.0 9.8 %copy-start = (s32[8]{0:T(128)S(1)}, s32[8]{0:T(128)}, u32[]{:S(2)}) copy-start(s32[8]{0:T(128)} %param.3) | copy-start | bytes 100
  1.9 8.0 %collective-permute-start = (bf16[256,4096]{1,0:T(8,128)(2,1)S(1)}, bf16[256,4096]{1,0:T(8,128)(2,1)}, u32[]{:S(2)}, u32[]{:S(2)}) collective-permute-start(bf16[256,4096]{1,0:T(8,128)(2,1)S(1)} %shard_map.28.refs_0_), channel_id=1, source_target_pairs={{0,1},{1,0},{2,3},{3,2},{4,5},{5,4},{6,7},{7,6},{8,9},{9,8},{10,11... | collective-permute-start | bytes 6291464 | tf_op jit(solution)/shard_map/ppermute | solution.py:19
  2.5 48.9 %collective-permute-start.1 = (bf16[256,4096]{1,0:T(8,128)(2,1)S(1)}, bf16[256,4096]{1,0:T(8,128)(2,1)}, u32[]{:S(2)}, u32[]{:S(2)}) collective-permute-start(bf16[256,4096]{1,0:T(8,128)(2,1)S(1)} %shard_map.28.refs_0_), channel_id=1, source_target_pairs={{0,2},{1,3},{2,0},{3,1},{4,6},{5,7},{6,4},{7,5},{8,10},{9,11},{10,... | collective-permute-start | bytes 6291464 | tf_op jit(solution)/shard_map/ppermute | solution.py:19
  5.1 46.3 %collective-permute-start.2 = (bf16[256,4096]{1,0:T(8,128)(2,1)S(1)}, bf16[256,4096]{1,0:T(8,128)(2,1)}, u32[]{:S(2)}, u32[]{:S(2)}) collective-permute-start(bf16[256,4096]{1,0:T(8,128)(2,1)S(1)} %shard_map.28.refs_0_), channel_id=1, source_target_pairs={{0,4},{2,6},{4,8},{6,10},{8,12},{9,1},{10,14},{11,3},{12,16},{13,5... | collective-permute-start | bytes 6291464 | tf_op jit(solution)/shard_map/ppermute | solution.py:24
  12.9 41.8 %collective-permute-start.3 = (bf16[256,4096]{1,0:T(8,128)(2,1)S(1)}, bf16[256,4096]{1,0:T(8,128)(2,1)S(1)}, u32[]{:S(2)}, u32[]{:S(2)}) collective-permute-start(bf16[256,4096]{1,0:T(8,128)(2,1)S(1)} %shard_map.28.refs_0_), channel_id=1, source_target_pairs={{1,5},{3,7},{5,9},{7,11},{8,0},{9,13},{10,2},{11,15},{12,4},{13,17... | collective-permute-start | bytes 6291464 | tf_op jit(solution)/shard_map/ppermute | solution.py:24
  51.4 4.4 %collective-permute-start.4 = (bf16[256,4096]{1,0:T(8,128)(2,1)}, bf16[256,4096]{1,0:T(8,128)(2,1)S(1)}, u32[]{:S(2)}, u32[]{:S(2)}) collective-permute-start(bf16[256,4096]{1,0:T(8,128)(2,1)} %collective-permute-done.1.refs_2_), channel_id=1, source_target_pairs={{0,1},{1,0},{2,3},{3,2},{4,5},{5,4},{6,7},{7,6},{8,9},{9,8},{10,11... | collective-permute-start | bytes 6291464 | tf_op jit(solution)/shard_map/ppermute | solution.py:19
  56.5 1.2 %collective-permute-start.5 = (f32[3,256]{1,0:T(4,128)S(1)}, f32[3,256]{1,0:T(4,128)S(1)}, u32[]{:S(2)}, u32[]{:S(2)}) collective-permute-start(f32[3,256]{1,0:T(4,128)S(1)} %pad_maximum_fusion), channel_id=1, source_target_pairs={{0,1},{1,0},{2,3},{3,2},{4,5},{5,4},{6,7},{7,6},{8,9},{9,8},{10,11... | collective-permute-start | bytes 9224 | tf_op jit(solution)/shard_map/ppermute | solution.py:19
  57.8 7.0 %collective-permute-start.7 = (f32[2,256]{1,0:T(2,128)S(1)}, f32[2,256]{1,0:T(2,128)S(1)}, u32[]{:S(2)}, u32[]{:S(2)}) collective-permute-start(f32[2,256]{1,0:T(2,128)S(1)} %pad_maximum_fusion.1), channel_id=1, source_target_pairs={{1,9},{3,11},{4,0},{5,13},{6,2},{7,15},{8,4},{9,17},{10,6},{11,19}... | collective-permute-start | bytes 6152 | tf_op jit(solution)/shard_map/ppermute | solution.py:24
  59.1 6.7 %collective-permute-start.6 = (f32[1,256]{1,0:T(1,128)S(1)}, f32[1,256]{1,0:T(1,128)S(1)}, u32[]{:S(2)}, u32[]{:S(2)}) collective-permute-start(f32[1,256]{1,0:T(1,128)S(1)} %slice.34), channel_id=1, source_target_pairs={{0,2},{1,3},{2,0},{3,1},{4,6},{5,7},{6,4},{7,5},{8,10},{9,11},{10,... | collective-permute-start | bytes 3080 | tf_op jit(solution)/shard_map/ppermute | solution.py:19
  64.8 1.8 %collective-permute-start.8 = (f32[1,256]{1,0:T(1,128)S(1)}, f32[1,256]{1,0:T(1,128)S(1)}, u32[]{:S(2)}, u32[]{:S(2)}) collective-permute-start(f32[1,256]{1,0:T(1,128)S(1)} %slice.37), channel_id=1, source_target_pairs={{0,1},{1,0},{2,3},{3,2},{4,5},{5,4},{6,7},{7,6},{8,9},{9,8},{10,11... | collective-permute-start | bytes 3080 | tf_op jit(solution)/shard_map/ppermute | solution.py:19
